TPU v7x, 128 devices: a whole 4x4x4 slice. The times are simulated.
128 devices in a mesh: node: 16 (over y, x), local: 8 (over z, core).
Axes of the slice: x: 4, y: 4, z: 4, core: 2. Of those that a mesh axis runs over, the one named last changes fastest.
Arguments:
- tokens: bfloat16 [2048, 7168], P('node', 'local'), may hold values from -6 to 6
- out_grad: bfloat16 [2048, 7168], P('node', 'local'), may hold values from -6 to 6
- expert_ids: int32 [2048, 8], P('node'), may hold values from 0 to 31, as said below
- gates: float32 [2048, 8], P('node'), may hold values from 0.05 to 1
- gate_weight: bfloat16 [32, 7168, 1024], P('node', 'local'), may hold values from -0.0625 to 0.0625
- up_weight: bfloat16 [32, 7168, 1024], P('node', 'local'), may hold values from -0.0625 to 0.0625
- down_weight: bfloat16 [32, 1024, 7168], P('node', None, 'local'), may hold values from -0.1875 to 0.1875
Outputs:
- grad_tokens: bfloat16 [2048, 7168], P('node', 'local')
- gate_grad: bfloat16 [32, 7168, 1024], P('node', 'local')
- up_grad: bfloat16 [32, 7168, 1024], P('node', 'local')
- down_grad: bfloat16 [32, 1024, 7168], P('node', None, 'local')
Inputs may be any that keep to these rules, and one draw needn't show every extreme that they name: `expert_ids`: each row names 8 different experts, all within at most 4 routing groups, group g being experts g * 4 to g * 4 + 3.
All inputs are finite; a program needn't handle non-finite values.
Results may differ from a plain program's by a relative error of at most 0.029.
Values may be sent and summed in bfloat16 or wider, within the bound.
No kernel may reach another device: no remote copies, remote signals or barrier semaphores. Data moves between devices by JAX's collectives and lax.ppermute only.
A program may use at most 128 MiB of HBM per device.

v0:
```python
import jax
import jax.numpy as jnp
from jax import lax
from jax.sharding import PartitionSpec as P


def swiglu_backward(gate_pre, up_pre, grad_hidden):
    sigmoid_g = jax.nn.sigmoid(gate_pre)
    activated = gate_pre * sigmoid_g
    hidden_act = (activated * up_pre).astype(jnp.bfloat16)
    grad_gate = (grad_hidden * up_pre * sigmoid_g * (1.0 + gate_pre * (1.0 - sigmoid_g))).astype(
        jnp.bfloat16
    )
    grad_up = (grad_hidden * activated).astype(jnp.bfloat16)
    return (hidden_act, grad_gate, grad_up)


def on_device(tokens, out_grad, expert_ids, gates, gate_weight, up_weight, down_weight):
    tok_rows, slice_width = tokens.shape
    top_count = expert_ids.shape[1]
    node_count = lax.axis_size("node")
    exp_local = gate_weight.shape[0]
    hidden = gate_weight.shape[2]
    experts = exp_local * node_count
    capacity = tok_rows * top_count * 5 // (experts * 4)
    row_count = node_count * capacity
    flat_ids = expert_ids.reshape(-1)
    onehot = (flat_ids[:, None] == jnp.arange(experts, dtype=jnp.int32)[None, :]).astype(jnp.int32)
    earlier = jnp.cumsum(onehot, axis=0) - onehot
    slot_pos = jnp.sum(earlier * onehot, axis=1)
    kept_mask = slot_pos < capacity
    owner_node = flat_ids // exp_local
    within = flat_ids % exp_local
    dest_row = jnp.where(
        kept_mask, (within * node_count + owner_node) * capacity + slot_pos, experts * capacity
    )
    x_rep = jnp.repeat(tokens, top_count, axis=0)
    dy_rep = (
        gates.reshape(-1, 1) * jnp.repeat(out_grad, top_count, axis=0).astype(jnp.float32)
    ).astype(jnp.bfloat16)
    blank = jnp.zeros((experts * capacity, slice_width), jnp.bfloat16)
    x_send = (
        blank.at[dest_row]
        .set(x_rep, mode="drop")
        .reshape(exp_local, node_count, capacity, slice_width)
    )
    dy_send = (
        blank.at[dest_row]
        .set(dy_rep, mode="drop")
        .reshape(exp_local, node_count, capacity, slice_width)
    )
    x_recv, dy_recv = (
        lax.all_to_all(x_send, "node", split_axis=1, concat_axis=1, tiled=True),
        lax.all_to_all(dy_send, "node", split_axis=1, concat_axis=1, tiled=True),
    )
    gate_pre = jnp.einsum("enrd,edf->enrf", x_recv, gate_weight, preferred_element_type=jnp.float32)
    up_pre = jnp.einsum("enrd,edf->enrf", x_recv, up_weight, preferred_element_type=jnp.float32)
    grad_hidden = jnp.einsum(
        "enrd,efd->enrf", dy_recv, down_weight, preferred_element_type=jnp.float32
    )
    stacked = jnp.stack((gate_pre, up_pre, grad_hidden), axis=3)
    x_flat = x_recv.reshape(exp_local, row_count, slice_width)
    dy_flat = dy_recv.reshape(exp_local, row_count, slice_width)
    stacked = stacked.reshape(exp_local, row_count, 3, hidden)
    totals = lax.psum(stacked.astype(jnp.bfloat16), "local").astype(jnp.float32)
    hidden_act, grad_gate, grad_up = swiglu_backward(
        totals[:, :, 0], totals[:, :, 1], totals[:, :, 2]
    )
    down_grad = jnp.einsum(
        "erf,erd->efd", hidden_act, dy_flat, preferred_element_type=jnp.float32
    ).astype(jnp.bfloat16)
    gate_grad = jnp.einsum(
        "erd,erf->edf", x_flat, grad_gate, preferred_element_type=jnp.float32
    ).astype(jnp.bfloat16)
    up_grad = jnp.einsum(
        "erd,erf->edf", x_flat, grad_up, preferred_element_type=jnp.float32
    ).astype(jnp.bfloat16)
    grad_rows = (
        jnp.einsum("erf,edf->erd", grad_gate, gate_weight, preferred_element_type=jnp.float32)
        + jnp.einsum("erf,edf->erd", grad_up, up_weight, preferred_element_type=jnp.float32)
    ).astype(jnp.bfloat16)
    returned = lax.all_to_all(
        grad_rows.reshape(exp_local, node_count, capacity, slice_width),
        "node",
        split_axis=1,
        concat_axis=1,
        tiled=True,
    )
    back_rows = returned.reshape(experts * capacity, slice_width)
    safe_row = jnp.minimum(dest_row, experts * capacity - 1)
    picked = jnp.where(
        kept_mask[:, None], back_rows[safe_row].astype(jnp.float32), jnp.float32(0.0)
    )
    grad_tokens = picked.reshape(tok_rows, top_count, slice_width).sum(axis=1).astype(jnp.bfloat16)
    return (grad_tokens, gate_grad, up_grad, down_grad)


def solution(mesh):
    return jax.shard_map(
        on_device,
        mesh=mesh,
        in_specs=(
            P("node", "local"),
            P("node", "local"),
            P("node", None),
            P("node", None),
            P("node", "local", None),
            P("node", "local", None),
            P("node", None, "local"),
        ),
        out_specs=(
            P("node", "local"),
            P("node", "local", None),
            P("node", "local", None),
            P("node", None, "local"),
        ),
        check_vma=False,
    )
```

profile of v0, /device:TPU:0, one launch (start us, length us, event | category | flops | bytes accessed | tf_op | source)
XLA Modules:
  0.0 316.8 jit_solution(6499910987329357838)
XLA Ops:
  9.2 9.0 %reduce-window.6 = s32[32,8,128]{2,1,0:T(8,128)S(1)} reduce-window(s32[32,8,128]{2,1,0:T(8,128)S(1)} %fusion.33, s32[]{:T(128)} %constant.36.clone.1), window={size=1x1x128 pad=0_0x0_0x127_0}, to_apply=%region_0.0 | reduce-window | flops 4161536 | bytes 262148 | tf_op jit(solution)/shard_map/reduce-window
  19.8 6.4 %scatter_custom_fusion.1 = bf16[1280,896]{1,0:T(8,128)(2,1)S(1)} fusion(s32[1024]{0:T(1024)S(1)} %bitcast.113, f32[128,896]{1,0:T(8,128)S(1)} %convert_element_type.54, f32[1024]{0:T(1024)S(1)} %mul.69, bf16[]{:T(256)} %constant.38.clone.1), kind=kCustom, calls=%fused_computation.30 | custom fusion | flops 1835008 | bytes 2756610 | tf_op jit(solution)/shard_map/scatter | solution.py:49
  26.1 1.6 copy.64
  27.7 7.1 %all-to-all-start.1 = ((bf16[2,16,40,896]{3,2,0,1:T(8,128)(2,1)}), bf16[2,16,40,896]{3,2,0,1:T(8,128)(2,1)S(1)}, u32[]{:S(2)}, u32[]{:S(2)}) async-start(bf16[2,16,40,896]{3,2,0,1:T(8,128)(2,1)} %copy.64), calls=%async_computation.1 | async-start | bytes 4587520 | tf_op jit(solution)/shard_map/all_to_all | solution.py:54
  34.8 6.9 %scatter_custom_fusion = bf16[1280,896]{1,0:T(8,128)(2,1)} fusion(s32[1024]{0:T(1024)S(1)} %bitcast.114, bf16[]{:T(256)} %constant.38.clone.1, bf16[128,896]{1,0:T(8,128)(2,1)S(1)} %copy-done), kind=kCustom, calls=%fused_computation.31 | custom fusion | bytes 2523138 | tf_op jit(solution)/shard_map/scatter | solution.py:44
  41.7 3.2 %copy.60 = bf16[2,16,40,896]{3,2,0,1:T(8,128)(2,1)} copy(bf16[2,16,40,896]{3,2,1,0:T(8,128)(2,1)} %bitcast.101) | data formatting | bytes 4587520 | tf_op jit(solution)/shard_map/reshape | solution.py:45
  44.9 24.4 %all-to-all-done.1 = bf16[2,16,40,896]{3,2,0,1:T(8,128)(2,1)S(1)} async-done(((bf16[2,16,40,896]{3,2,0,1:T(8,128)(2,1)}), bf16[2,16,40,896]{3,2,0,1:T(8,128)(2,1)S(1)}, u32[]{:S(2)}, u32[]{:S(2)}) %all-to-all-start.1) | async-done | bytes 2293792 | tf_op jit(solution)/shard_map/all_to_all | solution.py:54
  69.4 4.4 %all-to-all-start = ((bf16[2,16,40,896]{3,2,0,1:T(8,128)(2,1)}), bf16[2,16,40,896]{3,2,0,1:T(8,128)(2,1)}, u32[]{:S(2)}, u32[]{:S(2)}) async-start(bf16[2,16,40,896]{3,2,0,1:T(8,128)(2,1)} %copy.60), calls=%async_computation | async-start | bytes 4587520 | tf_op jit(solution)/shard_map/all_to_all | solution.py:53
  74.0 6.2 %fusion.17 = bf16[2,16,40,1024]{3,2,1,0:T(8,128)(2,1)} fusion(bf16[2,1024,896]{2,1,0:T(8,128)(2,1)} %param.13, bf16[2,16,40,896]{3,2,0,1:T(8,128)(2,1)S(1)} %all-to-all-done.1), kind=kOutput, calls=%fused_computation.29 | convolution fusion | flops 2350120960 | bytes 8585216 | tf_op jit(solution)/shard_map/enrd,efd->enrf/dot_general | solution.py:58
  80.3 3.1 copy.68
  83.4 22.7 %all-to-all-done = bf16[2,16,40,896]{3,2,0,1:T(8,128)(2,1)} async-done(((bf16[2,16,40,896]{3,2,0,1:T(8,128)(2,1)}), bf16[2,16,40,896]{3,2,0,1:T(8,128)(2,1)}, u32[]{:S(2)}, u32[]{:S(2)}) %all-to-all-start) | async-done | bytes 2293792 | tf_op jit(solution)/shard_map/all_to_all | solution.py:53
  106.1 7.1 %fusion.11 = bf16[2,16,40,1024]{3,2,1,0:T(8,128)(2,1)} fusion(bf16[2,896,1024]{2,1,0:T(8,128)(2,1)} %param.11, bf16[2,16,40,896]{3,2,0,1:T(8,128)(2,1)} %all-to-all-done), kind=kOutput, calls=%fused_computation.27 | convolution fusion | flops 2350120960 | bytes 8585216 | tf_op jit(solution)/shard_map/enrd,edf->enrf/dot_general | solution.py:56
  113.2 4.4 %copy.66 = bf16[2,640,1,1024]{1,3,0,2:T(8,128)(2,1)} copy(bf16[2,640,1,1024]{3,1,0,2:T(8,128)(2,1)} %bitcast.103) | data formatting | bytes 5242880 | tf_op jit(solution)/shard_map/stack | solution.py:61
  117.6 7.1 %fusion.14 = bf16[2,16,40,1024]{3,2,1,0:T(8,128)(2,1)} fusion(bf16[2,896,1024]{2,1,0:T(8,128)(2,1)} %param.12, bf16[2,16,40,896]{3,2,0,1:T(8,128)(2,1)} %all-to-all-done), kind=kOutput, calls=%fused_computation.28 | convolution fusion | flops 2350120960 | bytes 8585216 | tf_op jit(solution)/shard_map/enrd,edf->enrf/dot_general | solution.py:57
  124.7 4.4 %copy.67 = bf16[2,640,1,1024]{1,3,0,2:T(8,128)(2,1)} copy(bf16[2,640,1,1024]{3,1,0,2:T(8,128)(2,1)} %bitcast.104) | data formatting | bytes 5242880 | tf_op jit(solution)/shard_map/stack | solution.py:61
  129.1 6.3 %pad_maximum_fusion = bf16[2,640,3,1024]{1,3,0,2:T(8,128)(2,1)} fusion(bf16[2,640,1,1024]{1,3,0,2:T(8,128)(2,1)S(1)} %copy.68, bf16[2,640,1,1024]{1,3,0,2:T(8,128)(2,1)} %copy.67, bf16[2,640,1,1024]{1,3,0,2:T(8,128)(2,1)} %copy.66), kind=kLoop, calls=%fused_computation.3 | loop fusion | flops 7864320 | bytes 15728640 | tf_op jit(solution)/shard_map/stack | solution.py:61
  135.5 3.3 %copy.61 = bf16[2,16,40,896]{3,2,1,0:T(8,128)(2,1)} copy(bf16[2,16,40,896]{3,2,0,1:T(8,128)(2,1)} %all-to-all-done) | data formatting | bytes 4587520 | tf_op jit(solution)/shard_map/all_to_all | solution.py:53
  138.9 1.6 copy.65
  140.5 92.8 %all-reduce.2.cloned.1.call-done = bf16[2,640,3,1024]{1,3,0,2:T(8,128)(2,1)} async-done(((bf16[2,640,3,1024]{1,3,0,2:T(8,128)(2,1)}), bf16[2,640,3,1024]{1,3,0,2:T(8,128)(2,1)}) %all-reduce.2.cloned.1.call-update) | async-done | bytes 7864336 | tf_op jit(solution)/shard_map/psum | solution.py:65
  233.3 9.8 %convert_element_type.57 = f32[2,640,3,1024]{1,3,0,2:T(8,128)} convert(bf16[2,640,3,1024]{1,3,0,2:T(8,128)(2,1)} %all-reduce.2.cloned.1.call-done) | non-fusion elementwise | flops 3932160 | bytes 23592960 | tf_op jit(solution)/shard_map/convert_element_type | solution.py:65
  243.1 7.1 %multiply_convert_fusion.1 = (bf16[2,640,1024]{1,2,0:T(8,128)(2,1)S(1)}, bf16[2,640,1024]{1,2,0:T(8,128)(2,1)S(1)}) fusion(f32[2,640,3,1024]{1,3,0,2:T(8,128)} %convert_element_type.57), kind=kLoop, calls=%fused_computation.8 | loop fusion | flops 17039360 | bytes 20971520 | tf_op jit(solution)/shard_map/convert_element_type | solution.py:14
  250.3 3.4 %fusion.40 = f32[2,640,896]{2,1,0:T(8,128)S(1)} fusion(bf16[2,640,1024]{1,2,0:T(8,128)(2,1)S(1)} %get-tuple-element.7, bf16[2,896,1024]{2,1,0:T(8,128)(2,1)S(1)} %copy-done.7), kind=kOutput, calls=%fused_computation.62 | convolution fusion | flops 2348810240 | bytes 10878976 | tf_op jit(solution)/shard_map/erf,edf->erd/dot_general | solution.py:79
  253.7 4.1 %add_convert_fusion = bf16[2,640,896]{2,1,0:T(8,128)(2,1)S(1)} fusion(f32[2,640,896]{2,1,0:T(8,128)S(1)} %fusion.40, bf16[2,640,1024]{1,2,0:T(8,128)(2,1)S(1)} %get-tuple-element.6, bf16[2,896,1024]{2,1,0:T(8,128)(2,1)S(1)} %copy-done.8), kind=kOutput, calls=%fused_computation.12 | convolution fusion | flops 2351104000 | bytes 13172736 | tf_op jit(solution)/shard_map/erf,edf->erd/dot_general | solution.py:80
  257.9 1.6 copy.71
  259.4 6.9 %all-to-all-start.2 = ((bf16[2,16,40,896]{3,2,0,1:T(8,128)(2,1)}), bf16[2,16,40,896]{3,2,0,1:T(8,128)(2,1)}, u32[]{:S(2)}, u32[]{:S(2)}) async-start(bf16[2,16,40,896]{3,2,0,1:T(8,128)(2,1)} %copy.71), calls=%async_computation.2 | async-start | bytes 4587520 | tf_op jit(solution)/shard_map/all_to_all | solution.py:82
  266.3 7.8 %convolution_convert_fusion = bf16[2,896,1024]{2,1,0:T(8,128)(2,1)} fusion(bf16[2,640,896]{2,1,0:T(8,128)(2,1)} %bitcast.106, bf16[2,640,1024]{1,2,0:T(8,128)(2,1)} %copy-done.4), kind=kOutput, calls=%fused_computation.25 | convolution fusion | flops 2350645248 | bytes 8585216 | tf_op jit(solution)/shard_map/erd,erf->edf/dot_general | solution.py:75
  274.1 5.2 %convolution_convert_fusion.1 = bf16[2,896,1024]{2,1,0:T(8,128)(2,1)} fusion(bf16[2,640,896]{2,1,0:T(8,128)(2,1)S(1)} %bitcast.107, bf16[2,640,1024]{1,2,0:T(8,128)(2,1)S(1)} %get-tuple-element.7), kind=kOutput, calls=%fused_computation.26 | convolution fusion | flops 2350645248 | bytes 8585216 | tf_op jit(solution)/shard_map/erd,erf->edf/dot_general | solution.py:72
  279.3 9.2 %fusion.10 = bf16[2,1024,896]{2,1,0:T(8,128)(2,1)} fusion(bf16[2,640,896]{2,1,0:T(8,128)(2,1)S(1)} %bitcast.105, f32[2,640,3,1024]{1,3,0,2:T(8,128)} %convert_element_type.57), kind=kOutput, calls=%fused_computation.24 | convolution fusion | flops 2358509568 | bytes 16449536 | tf_op jit(solution)/shard_map/erf,erd->efd/dot_general | solution.py:69
  288.5 10.9 %all-to-all-done.2 = bf16[2,16,40,896]{3,2,0,1:T(8,128)(2,1)} async-done(((bf16[2,16,40,896]{3,2,0,1:T(8,128)(2,1)}), bf16[2,16,40,896]{3,2,0,1:T(8,128)(2,1)}, u32[]{:S(2)}, u32[]{:S(2)}) %all-to-all-start.2) | async-done | bytes 2293792 | tf_op jit(solution)/shard_map/all_to_all | solution.py:82
  299.4 1.8 copy.72
  301.3 5.2 %gather_fusion = bf16[1024,896]{1,0:T(8,128)(2,1)} fusion(bf16[1280,896]{1,0:T(8,128)(2,1)S(1)} %bitcast.99, s32[1024]{0:T(1024)S(1)} %broadcast_clamp_fusion), kind=kCustom, calls=%fused_computation | custom fusion | bytes 3674112 | tf_op jit(solution)/shard_map/gather | solution.py:92
  306.5 3.4 %fusion.1 = bf16[128,896]{1,0:T(8,128)(2,1)} fusion(bf16[1024,896]{1,0:T(8,128)(2,1)} %gather_fusion, pred[128,8]{1,0:T(8,128)(4,1)S(1)} %lt.50), kind=kLoop, calls=%fused_computation.14 | loop fusion | flops 2637824 | bytes 2065408 | tf_op jit(solution)/shard_map/reduce_sum | solution.py:94
  (40 shorter events, 3.9 us)
Async XLA Ops:
  7.2 27.7 %copy-start = (bf16[128,896]{1,0:T(8,128)(2,1)S(1)}, bf16[128,896]{1,0:T(8,128)(2,1)}, u32[]{:S(2)}) copy-start(bf16[128,896]{1,0:T(8,128)(2,1)} %param.7) | copy-start | bytes 688132
  27.7 41.7 %all-to-all-start.1 = ((bf16[2,16,40,896]{3,2,0,1:T(8,128)(2,1)}), bf16[2,16,40,896]{3,2,0,1:T(8,128)(2,1)S(1)}, u32[]{:S(2)}, u32[]{:S(2)}) async-start(bf16[2,16,40,896]{3,2,0,1:T(8,128)(2,1)} %copy.64), calls=%async_computation.1 | async-start | bytes 4587520 | tf_op jit(solution)/shard_map/all_to_all | solution.py:54
  69.4 10.9 %copy-start.2 = (bf16[2,16,40,896]{3,2,0,1:T(8,128)(2,1)}, bf16[2,16,40,896]{3,2,0,1:T(8,128)(2,1)S(1)}, u32[]{:S(2)}) copy-start(bf16[2,16,40,896]{3,2,0,1:T(8,128)(2,1)S(1)} %all-to-all-done.1) | copy-start | bytes 6881284
  69.4 36.8 %all-to-all-start = ((bf16[2,16,40,896]{3,2,0,1:T(8,128)(2,1)}), bf16[2,16,40,896]{3,2,0,1:T(8,128)(2,1)}, u32[]{:S(2)}, u32[]{:S(2)}) async-start(bf16[2,16,40,896]{3,2,0,1:T(8,128)(2,1)} %copy.60), calls=%async_computation | async-start | bytes 4587520 | tf_op jit(solution)/shard_map/all_to_all | solution.py:53
  73.8 159.5 %all-reduce.2.cloned.1.call-start = ((), (), s32[]{:S(2)}) async-start(), calls=%async_computation.3 | async-start | bytes 15728640 | tf_op jit(solution)/shard_map/psum | solution.py:65
  135.4 3.5 %copy-start.3 = (bf16[2,16,40,896]{3,2,0,1:T(8,128)(2,1)S(1)}, bf16[2,16,40,896]{3,2,0,1:T(8,128)(2,1)}, u32[]{:S(2)}) copy-start(bf16[2,16,40,896]{3,2,0,1:T(8,128)(2,1)} %copy-done.2) | copy-start | bytes 6881284
  243.1 7.2 %copy-start.7 = (bf16[2,896,1024]{2,1,0:T(8,128)(2,1)S(1)}, bf16[2,896,1024]{2,1,0:T(8,128)(2,1)}, u32[]{:S(2)}) copy-start(bf16[2,896,1024]{2,1,0:T(8,128)(2,1)} %param.11) | copy-start | bytes 11010052
  250.3 3.5 %copy-start.4 = (bf16[2,640,1024]{1,2,0:T(8,128)(2,1)}, bf16[2,640,1024]{1,2,0:T(8,128)(2,1)S(1)}, u32[]{:S(2)}) copy-start(bf16[2,640,1024]{1,2,0:T(8,128)(2,1)S(1)} %get-tuple-element.6) | copy-start | bytes 7864324
  250.3 3.4 %copy-start.8 = (bf16[2,896,1024]{2,1,0:T(8,128)(2,1)S(1)}, bf16[2,896,1024]{2,1,0:T(8,128)(2,1)}, u32[]{:S(2)}) copy-start(bf16[2,896,1024]{2,1,0:T(8,128)(2,1)} %param.12) | copy-start | bytes 11010052
  259.4 40.0 %all-to-all-start.2 = ((bf16[2,16,40,896]{3,2,0,1:T(8,128)(2,1)}), bf16[2,16,40,896]{3,2,0,1:T(8,128)(2,1)}, u32[]{:S(2)}, u32[]{:S(2)}) async-start(bf16[2,16,40,896]{3,2,0,1:T(8,128)(2,1)} %copy.71), calls=%async_computation.2 | async-start | bytes 4587520 | tf_op jit(solution)/shard_map/all_to_all | solution.py:82
  266.3 7.8 %copy-start.6 = (bf16[2,16,40,896]{3,2,1,0:T(8,128)(2,1)S(1)}, bf16[2,16,40,896]{3,2,1,0:T(8,128)(2,1)}, u32[]{:S(2)}) copy-start(bf16[2,16,40,896]{3,2,1,0:T(8,128)(2,1)} %copy.61) | copy-start | bytes 6881284
  274.1 5.2 %copy-start.5 = (bf16[2,16,40,896]{3,2,1,0:T(8,128)(2,1)S(1)}, bf16[2,16,40,896]{3,2,1,0:T(8,128)(2,1)}, u32[]{:S(2)}) copy-start(bf16[2,16,40,896]{3,2,1,0:T(8,128)(2,1)} %copy.65) | copy-start | bytes 6881284
  301.3 8.7 %copy-start.1 = (bf16[128,896]{1,0:T(8,128)(2,1)S(1)}, bf16[128,896]{1,0:T(8,128)(2,1)}, u32[]{:S(2)}) copy-start(bf16[128,896]{1,0:T(8,128)(2,1)} %param.7) | copy-start | bytes 688132
Sparse Core Ops, SparseCore 0:
  135.5 97.7 all-reduce.1
where the time goes:
time: 320 us; the launch traced here: 317 us
  waiting for transfers between devices  151 us (47%)
  matrix products  50.2 us (16%)
  other arithmetic  43.2 us (14%)
  local copies, waits for them, and re-layouts  39.6 us (12%)
  starting transfers between devices  18.6 us (6%)
  between operations  14.3 us (4%)
    psum x1, waiting for transfers between devices, on_device(): totals = lax.psum(stacked.astype(jnp.bfloat16), 'local').astype(jnp.float32)  92.8 us
    all_to_all x1, waiting for transfers between devices, on_device(): lax.all_to_all(dy_send, 'node', split_axis=1, concat_axis=1, tiled=True)  24.4 us
    all_to_all x1, waiting for transfers between devices, on_device(): lax.all_to_all(x_send, 'node', split_axis=1, concat_axis=1, tiled=True)  22.7 us
    another operation x3, local copies, waits for them, and re-layouts, on_device(): stacked = jnp.stack((gate_pre, up_pre, grad_hidden), axis=3)  11.9 us
    all_to_all x1, waiting for transfers between devices, on_device(): lax.all_to_all(grad_rows.reshape(exp_local, node_count, capacity, slice_w...  10.9 us
    convert_element_type x1, other arithmetic, on_device(): totals = lax.psum(stacked.astype(jnp.bfloat16), 'local').astype(jnp.float32)  9.81 us
    dot_general x1, matrix products, on_device(): jnp.einsum('erf,erd->efd', hidden_act, dy_flat, preferred_element_type=jn...  9.23 us
    another operation x3, other arithmetic  9.15 us
  transfers between devices with their start and end apart: 4, of which 4 were waited for; matrix products, arithmetic and copies ran while one was open for 15% of the time, Pallas kernels for 0%

commit v1 on v0

v1 whole, which is shorter than its diff:
```python
import functools
import jax
import jax.numpy as jnp
from jax import lax
from jax.experimental import pallas as pl
from jax.experimental.pallas import tpu as pltpu
from jax.sharding import PartitionSpec as P

BF = jnp.bfloat16
F32 = jnp.float32
MIB = 1024 * 1024
NN = (((1,), (0,)), ((), ()))
NT = (((1,), (1,)), ((), ()))
TN = (((0,), (0,)), ((), ()))


def dot(a, b, dims):
    return lax.dot_general(a, b, dims, preferred_element_type=F32)


def params(mib):
    return pltpu.CompilerParams(vmem_limit_bytes=mib * MIB)


def cost(flops, moved):
    return pl.CostEstimate(flops=flops, bytes_accessed=moved, transcendentals=0)


def whole(shape):
    return pl.BlockSpec(shape, lambda *_: (0,) * len(shape))


def slot_map(ids, gates):
    tok, top = ids.shape
    lane = lax.broadcasted_iota(jnp.int32, (tok, tok), 1)
    row = lax.broadcasted_iota(jnp.int32, (tok, tok), 0)
    named = jnp.zeros((tok, tok), F32)
    weight = jnp.zeros((tok, tok), F32)
    for k in range(top):
        hit = ids[:, k : k + 1] == lane
        named = jnp.where(hit, 1.0, named)
        weight = jnp.where(hit, gates[:, k : k + 1], weight)
    named_t = named.T
    before = (row < lane).astype(BF)
    pos = dot(named_t.astype(BF), before, NN)
    return jnp.where(named_t > 0.0, pos, -1.0), weight.T


def one_hot(pos, e, cap, exp_local, nodes):
    slot = lax.broadcasted_iota(jnp.int32, (cap, pos.shape[1]), 0).astype(F32)
    return jnp.concatenate(
        [
            (pos[n * exp_local + e : n * exp_local + e + 1, :] == slot).astype(F32)
            for n in range(nodes)
        ],
        axis=0,
    )


def pack_kernel(e, cap, exp_local, nodes, ids_ref, gates_ref, tok_ref, grad_ref, out_ref, pos_ref):
    pos, weight = slot_map(ids_ref[...], gates_ref[...])
    pos_ref[...] = pos
    width = tok_ref.shape[1]
    sel = one_hot(pos, e, cap, exp_local, nodes)
    scale = jnp.concatenate(
        [
            jnp.sum(
                sel[n * cap : (n + 1) * cap]
                * weight[n * exp_local + e : n * exp_local + e + 1, :],
                axis=1,
                keepdims=True,
            )
            for n in range(nodes)
        ],
        axis=0,
    )
    sel = sel.astype(BF)
    out_ref[:, :width] = dot(sel, tok_ref[...], NN).astype(BF)
    out_ref[:, width:] = (scale * dot(sel, grad_ref[...], NN)).astype(BF)


def pack(e, cap, exp_local, nodes, ids, gates, tokens, out_grad):
    tok, width = tokens.shape
    rows = nodes * cap
    return pl.pallas_call(
        functools.partial(pack_kernel, e, cap, exp_local, nodes),
        out_shape=(
            jax.ShapeDtypeStruct((rows, 2 * width), BF),
            jax.ShapeDtypeStruct((tok, tok), F32),
        ),
        compiler_params=params(24),
        cost_estimate=cost(4 * rows * tok * width, 4 * rows * width + 4 * tok * width),
        name="pack",
    )(ids, gates, tokens, out_grad)


def ring_slot(half, j):
    if half == 0:
        return jnp.where(j == 0, 6, jnp.where(j == 1, 4, jnp.where(j == 2, 0, 3)))
    return jnp.where(j == 0, 7, jnp.where(j == 1, 1, jnp.where(j == 2, 2, 5)))


def products_kernel(blk, place, rows_ref, wg_ref, wu_ref, wd_ref, own_ref, other_ref):
    half = pl.program_id(0)
    z, core = place[0], place[1]
    rows, width2 = rows_ref.shape
    width = width2 // 2
    x = rows_ref[:, :width]
    dy = rows_ref[:, width:]
    vals = (
        dot(x, wg_ref[0], NN).astype(BF),
        dot(x, wu_ref[0], NN).astype(BF),
        dot(dy, wd_ref[0], NT).astype(BF),
    )
    for q in range(rows // blk):
        j = lax.rem(q // 2 - z + 4, 4)
        slot = jnp.where(half == 0, ring_slot(0, j), ring_slot(1, j))

        def put(ref, q=q, slot=slot):
            for k in range(3):
                ref[slot, k] = vals[k][q * blk : (q + 1) * blk]

        pl.when(core == q % 2)(functools.partial(put, own_ref))
        pl.when(core != q % 2)(functools.partial(put, other_ref))


def products(e, blk, place, rows_x_dy, wg, wu, wd):
    rows, width2 = rows_x_dy.shape
    width = width2 // 2
    hidden = wg.shape[2]
    hh = hidden // 2
    out = jax.ShapeDtypeStruct((8, 3, blk, hh), BF)
    return pl.pallas_call(
        functools.partial(products_kernel, blk),
        out_shape=(out, out),
        grid_spec=pltpu.PrefetchScalarGridSpec(
            num_scalar_prefetch=1,
            grid=(2,),
            in_specs=[
                whole((rows, width2)),
                pl.BlockSpec((1, width, hh), lambda h, _: (e, 0, h)),
                pl.BlockSpec((1, width, hh), lambda h, _: (e, 0, h)),
                pl.BlockSpec((1, hh, width), lambda h, _: (e, h, 0)),
            ],
            out_specs=[whole(out.shape), whole(out.shape)],
        ),
        compiler_params=params(40),
        cost_estimate=cost(6 * rows * width * hidden, 6 * width * hidden + 10 * rows * width),
        name="products",
    )(place, rows_x_dy, wg, wu, wd)


def swiglu_kernel(kept_ref, rm_ref, rp_ref, sp_ref, sm_ref, out_ref):
    for half, (direct, ringed) in enumerate(((rm_ref, sp_ref), (rp_ref, sm_ref))):
        tot = [
            kept_ref[2 + half, k].astype(F32)
            + direct[1, k].astype(F32)
            + ringed[k].astype(F32)
            for k in range(3)
        ]
        gate, up, gh = tot
        sig = jax.nn.sigmoid(gate)
        act = gate * sig
        out_ref[half, 0] = (act * up).astype(BF)
        out_ref[half, 1] = (gh * up * sig * (1.0 + gate * (1.0 - sig))).astype(BF)
        out_ref[half, 2] = (gh * act).astype(BF)


def swiglu(kept, rm, rp, sp, sm):
    shape = (2,) + kept.shape[1:]
    return pl.pallas_call(
        swiglu_kernel,
        out_shape=jax.ShapeDtypeStruct(shape, BF),
        compiler_params=params(24),
        cost_estimate=cost(0, 8 * kept.size),
        name="swiglu",
    )(kept, rm, rp, sp, sm)


def move(x, dz, dcore=0):
    return lax.ppermute(
        x, "local", [(i, ((i // 2 + dz) % 4) * 2 + (i + dcore) % 2) for i in range(8)]
    )


def sum_over_width(own, other):
    got = move(other, 0, 1)
    to_next = own[0:2] + got[0:2]
    to_prev = own[2:4] + got[2:4]
    kept = own[4:8] + got[4:8]
    rp = move(to_next, 1)
    rm = move(to_prev, -1)
    sp = move(kept[0] + rp[0], 1)
    sm = move(kept[1] + rm[0], -1)
    return swiglu(kept, rm, rp, sp, sm)


def gather_rows(mine):
    prev = move(mine, 1)
    nxt = move(mine, -1)
    far0 = move(prev[0], 1)
    far1 = move(nxt[1], -1)
    parts = (mine, prev, nxt, far0, far1)
    return parts + tuple(move(p, 0, 1) for p in parts)


def grad_rows_kernel(blk, place, *refs):
    parts, (wg_ref, wu_ref), (out_ref, h_ref, acc_ref) = refs[:10], refs[10:12], refs[12:]
    f = pl.program_id(0)
    hh = h_ref.shape[2] // 2
    z, core = place[0], place[1]

    @pl.when(f == 0)
    def _():
        for c in range(2):
            mine, prev, nxt, far0, far1 = parts[5 * c : 5 * c + 5]
            for j in range(4):
                q = lax.rem(z + j, 4) * 2 + lax.rem(core + c, 2)
                at = pl.ds(pl.multiple_of(q * blk, 16), blk)
                for half in range(2):
                    for k in range(3):
                        if j == 2:
                            val = (far0, far1)[half][k]
                        else:
                            val = (mine, nxt, None, prev)[j][half, k]
                        h_ref[k, at, half * hh : (half + 1) * hh] = val

    def part(half):
        cols = slice(half * hh, (half + 1) * hh)
        return dot(h_ref[1, :, cols], wg_ref[0], NT) + dot(h_ref[2, :, cols], wu_ref[0], NT)

    @pl.when(f == 0)
    def _():
        acc_ref[...] = part(0)

    @pl.when(f == 1)
    def _():
        out_ref[...] = (acc_ref[...] + part(1)).astype(BF)


def grad_rows(e, blk, rows, place, parts, wg, wu):
    width, hidden = wg.shape[1:]
    hh = hidden // 2
    return pl.pallas_call(
        functools.partial(grad_rows_kernel, blk),
        out_shape=(
            jax.ShapeDtypeStruct((rows, width), BF),
            jax.ShapeDtypeStruct((3, rows, hidden), BF),
        ),
        grid_spec=pltpu.PrefetchScalarGridSpec(
            num_scalar_prefetch=1,
            grid=(2,),
            in_specs=[whole(p.shape) for p in parts]
            + [pl.BlockSpec((1, width, hh), lambda f, _: (e, 0, f))] * 2,
            out_specs=[whole((rows, width)), whole((3, rows, hidden))],
            scratch_shapes=[pltpu.VMEM((rows, width), F32)],
        ),
        compiler_params=params(40),
        cost_estimate=cost(4 * rows * width * hidden, 4 * width * hidden + 14 * rows * hidden),
        name="grad_rows",
    )(place, *parts, wg, wu)


def weight_grads_kernel(h_ref, rows_ref, *refs):
    dg_ref, du_ref, dd_ref = refs[-3:]
    width = rows_ref.shape[1] // 2
    x = rows_ref[:, :width]
    dg_ref[0] = dot(x, h_ref[1], TN).astype(BF)
    du_ref[0] = dot(x, h_ref[2], TN).astype(BF)
    dd_ref[0] = dot(h_ref[0], rows_ref[:, width:], TN).astype(BF)


def weight_grads(e, exp_local, h, rows_x_dy, into):
    rows, width2 = rows_x_dy.shape
    width, hidden = width2 // 2, h.shape[2]
    hh = hidden // 2
    up = jax.ShapeDtypeStruct((exp_local, width, hidden), BF)
    down = jax.ShapeDtypeStruct((exp_local, hidden, width), BF)
    return pl.pallas_call(
        weight_grads_kernel,
        out_shape=(up, up, down),
        grid=(2,),
        in_specs=[
            pl.BlockSpec((3, rows, hh), lambda f: (0, 0, f)),
            whole((rows, width2)),
        ]
        + [pl.BlockSpec(memory_space=pl.ANY)] * len(into),
        out_specs=[
            pl.BlockSpec((1, width, hh), lambda f: (e, 0, f)),
            pl.BlockSpec((1, width, hh), lambda f: (e, 0, f)),
            pl.BlockSpec((1, hh, width), lambda f: (e, f, 0)),
        ],
        input_output_aliases={2 + i: i for i in range(len(into))},
        compiler_params=params(40),
        cost_estimate=cost(6 * rows * width * hidden, 6 * width * hidden + 10 * rows * hidden),
        name="weight_grads",
    )(h, rows_x_dy, *into)


def combine_kernel(cap, exp_local, nodes, pos_ref, *refs):
    backs, out_ref = refs[:-1], refs[-1]
    pos = pos_ref[...]
    sel = [one_hot(pos, e, cap, exp_local, nodes).astype(BF) for e in range(exp_local)]
    tot = dot(sel[0], backs[0][...], TN)
    for e in range(1, exp_local):
        tot = tot + dot(sel[e], backs[e][...], TN)
    out_ref[...] = tot.astype(BF)


def combine(cap, exp_local, nodes, pos, backs):
    tok = pos.shape[0]
    rows, width = backs[0].shape
    return pl.pallas_call(
        functools.partial(combine_kernel, cap, exp_local, nodes),
        out_shape=jax.ShapeDtypeStruct((tok, width), BF),
        compiler_params=params(24),
        cost_estimate=cost(4 * rows * tok * width, 4 * rows * width),
        name="combine",
    )(pos, *backs)


def on_device(tokens, out_grad, expert_ids, gates, gate_weight, up_weight, down_weight):
    tok, width = tokens.shape
    top = expert_ids.shape[1]
    nodes = lax.axis_size("node")
    exp_local = gate_weight.shape[0]
    cap = tok * top * 5 // (exp_local * nodes * 4)
    rows = nodes * cap
    blk = rows // 8
    local = lax.axis_index("local")
    place = jnp.stack([local // 2, local % 2]).astype(jnp.int32)

    got, pos = [], None
    for e in range(exp_local):
        sent, pos_e = pack(e, cap, exp_local, nodes, expert_ids, gates, tokens, out_grad)
        pos = pos_e if pos is None else pos
        got.append(lax.all_to_all(sent, "node", split_axis=0, concat_axis=0, tiled=True))

    grads, backs = (), []
    for e in range(exp_local):
        own, other = products(e, blk, place, got[e], gate_weight, up_weight, down_weight)
        mine = sum_over_width(own, other)
        parts = gather_rows(mine)
        out_rows, h = grad_rows(e, blk, rows, place, parts, gate_weight, up_weight)
        backs.append(lax.all_to_all(out_rows, "node", split_axis=0, concat_axis=0, tiled=True))
        grads = weight_grads(e, exp_local, h, got[e], grads)
    grad_tokens = combine(cap, exp_local, nodes, pos, backs)
    return (grad_tokens,) + tuple(grads)


def solution(mesh):
    return jax.shard_map(
        on_device,
        mesh=mesh,
        in_specs=(
            P("node", "local"),
            P("node", "local"),
            P("node", None),
            P("node", None),
            P("node", "local", None),
            P("node", "local", None),
            P("node", None, "local"),
        ),
        out_specs=(
            P("node", "local"),
            P("node", "local", None),
            P("node", "local", None),
            P("node", None, "local"),
        ),
        check_vma=False,
    )
```

time: 320 us -> 228 us (0.71)
  waiting for transfers between devices: 151 us -> 99.4 us
  matrix products: 50.2 us -> 0 us
  Pallas kernels: 0 us -> 49.3 us
  other arithmetic: 43.2 us -> 3.05 us
  starting transfers between devices: 18.6 us -> 48.9 us
  local copies, waits for them, and re-layouts: 39.6 us -> 25.9 us
  between operations: 14.3 us -> 0.93 us
    psum x1 -> x0, waiting for transfers between devices: 92.8 us -> none  [on_device(): totals = lax.psum(stacked.astype(jnp.bfloat16), 'local').astype(jnp.float32)]
    dot_general x8 -> x0, matrix products: 50.2 us -> none  [the longest x1 9.23 us: on_device(): jnp.einsum('erf,erd->efd', hidden_act, dy_flat, preferred_element_type=jn...]
    pallas_call x0 -> x11, Pallas kernels: none -> 49.3 us  [the longest x2 15.5 us: products(): pl.pallas_call(functools.partial(products_kernel, blk), out_shape=(out, o...]
    ppermute x0 -> x28, waiting for transfers between devices: none -> 45.3 us  [move(): lax.ppermute(x, 'local', [(i, (i // 2 + dz) % 4 * 2 + (i + dcore) % 2) fo...]
    ppermute x0 -> x28, starting transfers between devices: none -> 26.6 us  [move(): lax.ppermute(x, 'local', [(i, (i // 2 + dz) % 4 * 2 + (i + dcore) % 2) fo...]
    unnamed x20 -> x42, local copies, waits for them, and re-layouts: 1.67 us -> 23.9 us
    convert_element_type x4 -> x0, other arithmetic: 17.9 us -> none  [the longest x1 9.81 us: on_device(): totals = lax.psum(stacked.astype(jnp.bfloat16), 'local').astype(jnp.float32)]
    another operation x4 -> x1, other arithmetic: 15.4 us -> 0.08 us  [on_device(): place = jnp.stack([local // 2, local % 2]).astype(jnp.int32)]
  transfers between devices with their start and end apart: 4 -> 32, of which waited for: 4 -> 15; matrix products, arithmetic and copies ran while one was open for 15% -> 2% of each run, Pallas kernels for 0% -> 20%
where the time goes in v1:
time: 228 us; the launch traced here: 227 us
  waiting for transfers between devices  99.4 us (44%)
  Pallas kernels  49.3 us (22%)
  starting transfers between devices  48.9 us (21%)
  local copies, waits for them, and re-layouts  25.9 us (11%)
  other arithmetic  3.05 us (1%)
    all_to_all x2, waiting for transfers between devices, on_device(): lax.all_to_all(sent, 'node', split_axis=0, concat_axis=0, tiled=True)  50.8 us
    ppermute x28, waiting for transfers between devices, move(): lax.ppermute(x, 'local', [(i, (i // 2 + dz) % 4 * 2 + (i + dcore) % 2) fo...  45.3 us
    ppermute x28, starting transfers between devices, move(): lax.ppermute(x, 'local', [(i, (i // 2 + dz) % 4 * 2 + (i + dcore) % 2) fo...  26.6 us
    unnamed x42, local copies, waits for them, and re-layouts  23.9 us
    pallas_call x2, Pallas kernels, products(): pl.pallas_call(functools.partial(products_kernel, blk), out_shape=(out, o...  15.5 us
    pallas_call x2, Pallas kernels, weight_grads(): pl.pallas_call(weight_grads_kernel, out_shape=(up, up, down), grid=(2,),...  13.8 us
    pallas_call x2, Pallas kernels, grad_rows(): pl.pallas_call(functools.partial(grad_rows_kernel, blk), out_shape=(jax.S...  13.6 us
    all_to_all x2, starting transfers between devices, on_device(): lax.all_to_all(sent, 'node', split_axis=0, concat_axis=0, tiled=True)  11.7 us
  transfers between devices with their start and end apart: 32, of which 15 were waited for; matrix products, arithmetic and copies ran while one was open for 2% of the time, Pallas kernels for 20%

profile of v1, /device:TPU:0, one launch (start us, length us, event | category | flops | bytes accessed | tf_op | source)
XLA Modules:
  0.0 227.4 jit_solution(5582345997501043837)
XLA Ops:
  6.7 7.2 %all-to-all-start.2 = ((bf16[16,40,1792]{2,1,0:T(8,128)(2,1)}), bf16[16,40,1792]{2,1,0:T(8,128)(2,1)S(1)}, u32[]{:S(2)}, u32[]{:S(2)}) async-start(bf16[16,40,1792]{2,1,0:T(8,128)(2,1)} %bitcast.30), calls=%async_computation.2 | async-start | bytes 4587520 | tf_op jit(solution)/shard_map/all_to_all | solution.py:337
  16.6 31.9 %all-to-all-done.2 = bf16[16,40,1792]{2,1,0:T(8,128)(2,1)S(1)} async-done(((bf16[16,40,1792]{2,1,0:T(8,128)(2,1)}), bf16[16,40,1792]{2,1,0:T(8,128)(2,1)S(1)}, u32[]{:S(2)}, u32[]{:S(2)}) %all-to-all-start.2) | async-done | bytes 2293792 | tf_op jit(solution)/shard_map/all_to_all | solution.py:337
  48.5 4.5 %all-to-all-start = ((bf16[16,40,1792]{2,1,0:T(8,128)(2,1)}), bf16[16,40,1792]{2,1,0:T(8,128)(2,1)}, u32[]{:S(2)}, u32[]{:S(2)}) async-start(bf16[16,40,1792]{2,1,0:T(8,128)(2,1)} %bitcast.29), calls=%async_computation | async-start | bytes 4587520 | tf_op jit(solution)/shard_map/all_to_all | solution.py:337
  53.1 2.0 copy-done
  57.2 8.0 %products.3 = (bf16[8,3,80,512]{3,2,1,0:T(8,128)(2,1)S(1)}, bf16[8,3,80,512]{3,2,1,0:T(8,128)(2,1)}) custom-call(s32[2]{0:T(128)S(1)} %pad_add_fusion.place, bf16[640,1792]{1,0:T(8,128)(2,1)S(1)} %bitcast.26, bf16[2,896,1024]{2,1,0:T(8,128)(2,1)S(1)} %copy-done, bf16[2,896,1024]{2,1,0:T(8,128)(2,1)S(1)} %copy-done.4, bf16[2,1024,896]{2,1,0:T(8,128)(2,1)} %wd_ref.3), custom_call_target="tpu_custom_call" | custom-call | flops 3523215360 | bytes 11239424 | tf_op jit(solution)/shard_map/products/pallas_call | solution.py:133
  66.4 18.9 %all-to-all-done = bf16[16,40,1792]{2,1,0:T(8,128)(2,1)} async-done(((bf16[16,40,1792]{2,1,0:T(8,128)(2,1)}), bf16[16,40,1792]{2,1,0:T(8,128)(2,1)}, u32[]{:S(2)}, u32[]{:S(2)}) %all-to-all-start) | async-done | bytes 2293792 | tf_op jit(solution)/shard_map/all_to_all | solution.py:337
  85.3 2.0 copy-done.1
  89.4 7.5 %products.2 = (bf16[8,3,80,512]{3,2,1,0:T(8,128)(2,1)S(1)}, bf16[8,3,80,512]{3,2,1,0:T(8,128)(2,1)S(1)}) custom-call(s32[2]{0:T(128)S(1)} %pad_add_fusion.place, bf16[640,1792]{1,0:T(8,128)(2,1)} %bitcast.3.rows_ref, bf16[2,896,1024]{2,1,0:T(8,128)(2,1)S(1)} %copy-done.1, bf16[2,896,1024]{2,1,0:T(8,128)(2,1)S(1)} %copy-done.5, bf16[2,1024,896]{2,1,0:T(8,128)(2,1)} %wd_ref.3), custom_call_target="tpu_custom_call" | custom-call | flops 3523215360 | bytes 11239424 | tf_op jit(solution)/shard_map/products/pallas_call | solution.py:133
  100.3 2.2 collective-permute-start.15
  103.8 10.5 %collective-permute-done.16.rp_ref = bf16[2,3,80,512]{3,2,1,0:T(8,128)(2,1)S(1)} collective-permute-done((bf16[2,3,80,512]{3,2,1,0:T(8,128)(2,1)S(1)}, bf16[2,3,80,512]{3,2,1,0:T(8,128)(2,1)S(1)}, u32[]{:S(2)}, u32[]{:S(2)}) %collective-permute-start.16) | collective-permute-done | bytes 491552 | tf_op jit(solution)/shard_map/ppermute | solution.py:181
  114.3 3.1 %collective-permute-start.18 = (bf16[3,80,512]{2,1,0:T(8,128)(2,1)S(1)}, bf16[3,80,512]{2,1,0:T(8,128)(2,1)S(1)}, u32[]{:S(2)}, u32[]{:S(2)}) collective-permute-start(bf16[3,80,512]{2,1,0:T(8,128)(2,1)S(1)} %get-tuple-element.42), channel_id=1, source_target_pairs={{0,6},{1,7},{2,0},{3,1},{4,2},{5,3},{6,4},{7,5},{8,14},{9,15},{10,... | collective-permute-start | bytes 737288 | tf_op jit(solution)/shard_map/ppermute | solution.py:181
  117.9 3.1 %collective-permute-start.1 = (bf16[2,3,80,512]{3,2,1,0:T(8,128)(2,1)S(1)}, bf16[2,3,80,512]{3,2,1,0:T(8,128)(2,1)S(1)}, u32[]{:S(2)}, u32[]{:S(2)}) collective-permute-start(bf16[2,3,80,512]{3,2,1,0:T(8,128)(2,1)S(1)} %get-tuple-element.41), channel_id=1, source_target_pairs={{0,6},{1,7},{2,0},{3,1},{4,2},{5,3},{6,4},{7,5},{8,14},{9,15},{10,... | collective-permute-start | bytes 1474568 | tf_op jit(solution)/shard_map/ppermute | solution.py:181
  120.9 2.8 %collective-permute-done.18.sm_ref = bf16[3,80,512]{2,1,0:T(8,128)(2,1)S(1)} collective-permute-done((bf16[3,80,512]{2,1,0:T(8,128)(2,1)S(1)}, bf16[3,80,512]{2,1,0:T(8,128)(2,1)S(1)}, u32[]{:S(2)}, u32[]{:S(2)}) %collective-permute-start.18) | collective-permute-done | bytes 245792 | tf_op jit(solution)/shard_map/ppermute | solution.py:181
  123.8 3.7 %collective-permute-done.17.sp_ref = bf16[3,80,512]{2,1,0:T(8,128)(2,1)S(1)} collective-permute-done((bf16[3,80,512]{2,1,0:T(8,128)(2,1)S(1)}, bf16[3,80,512]{2,1,0:T(8,128)(2,1)S(1)}, u32[]{:S(2)}, u32[]{:S(2)}) %collective-permute-start.17) | collective-permute-done | bytes 245792 | tf_op jit(solution)/shard_map/ppermute | solution.py:181
  128.1 2.1 collective-permute-start.19
  130.1 7.9 %collective-permute-done.2.rp_ref = bf16[2,3,80,512]{3,2,1,0:T(8,128)(2,1)S(1)} collective-permute-done((bf16[2,3,80,512]{3,2,1,0:T(8,128)(2,1)S(1)}, bf16[2,3,80,512]{3,2,1,0:T(8,128)(2,1)S(1)}, u32[]{:S(2)}, u32[]{:S(2)}) %collective-permute-start.2) | collective-permute-done | bytes 491552 | tf_op jit(solution)/shard_map/ppermute | solution.py:181
  140.2 4.7 %collective-permute-done.20.refs_2_ = bf16[2,3,80,512]{3,2,1,0:T(8,128)(2,1)S(1)} collective-permute-done((bf16[2,3,80,512]{3,2,1,0:T(8,128)(2,1)S(1)}, bf16[2,3,80,512]{3,2,1,0:T(8,128)(2,1)S(1)}, u32[]{:S(2)}, u32[]{:S(2)}) %collective-permute-start.20) | collective-permute-done | bytes 491552 | tf_op jit(solution)/shard_map/ppermute | solution.py:181
  144.9 3.8 %collective-permute-start.22 = (bf16[3,80,512]{2,1,0:T(8,128)(2,1)S(1)}, bf16[3,80,512]{2,1,0:T(8,128)(2,1)S(1)}, u32[]{:S(2)}, u32[]{:S(2)}) collective-permute-start(bf16[3,80,512]{2,1,0:T(8,128)(2,1)S(1)} %slice_bitcast_fusion), channel_id=1, source_target_pairs={{0,6},{1,7},{2,0},{3,1},{4,2},{5,3},{6,4},{7,5},{8,14},{9,15},{10,... | collective-permute-start | bytes 737288 | tf_op jit(solution)/shard_map/ppermute | solution.py:181
  155.2 3.7 %collective-permute-start.6 = (bf16[2,3,80,512]{3,2,1,0:T(8,128)(2,1)}, bf16[2,3,80,512]{3,2,1,0:T(8,128)(2,1)}, u32[]{:S(2)}, u32[]{:S(2)}) collective-permute-start(bf16[2,3,80,512]{3,2,1,0:T(8,128)(2,1)} %swiglu.2.refs_0_), channel_id=1, source_target_pairs={{0,6},{1,7},{2,0},{3,1},{4,2},{5,3},{6,4},{7,5},{8,14},{9,15},{10,... | collective-permute-start | bytes 1474568 | tf_op jit(solution)/shard_map/ppermute | solution.py:181
  160.4 6.1 %grad_rows.3 = (bf16[640,896]{1,0:T(8,128)(2,1)S(1)}, bf16[3,640,1024]{2,1,0:T(8,128)(2,1)}) custom-call(s32[2]{0:T(128)S(1)} %pad_add_fusion.place, bf16[2,3,80,512]{3,2,1,0:T(8,128)(2,1)S(1)} %swiglu.3.refs_0_, bf16[2,3,80,512]{3,2,1,0:T(8,128)(2,1)S(1)} %collective-permute-done.19.refs_1_, bf16[2,3,80,512]{3,2,1,0:T(8,128)(2,1)S(1)} %collective-permute-done.20.refs_2_, ...), custom_call_target="tpu_custom_call" | custom-call | flops 2348810240 | bytes 12845056 | tf_op jit(solution)/shard_map/grad_rows/pallas_call | solution.py:244
  167.5 3.7 %all-to-all-start.3 = ((bf16[16,40,896]{2,1,0:T(8,128)(2,1)}), bf16[16,40,896]{2,1,0:T(8,128)(2,1)S(1)}, u32[]{:S(2)}, u32[]{:S(2)}) async-start(bf16[16,40,896]{2,1,0:T(8,128)(2,1)} %bitcast.31), calls=%async_computation.3 | async-start | bytes 2293760 | tf_op jit(solution)/shard_map/all_to_all | solution.py:345
  172.2 2.9 %collective-permute-start.8 = (bf16[3,80,512]{2,1,0:T(8,128)(2,1)S(1)}, bf16[3,80,512]{2,1,0:T(8,128)(2,1)S(1)}, u32[]{:S(2)}, u32[]{:S(2)}) collective-permute-start(bf16[3,80,512]{2,1,0:T(8,128)(2,1)S(1)} %slice_bitcast_fusion.2), channel_id=1, source_target_pairs={{0,6},{1,7},{2,0},{3,1},{4,2},{5,3},{6,4},{7,5},{8,14},{9,15},{10,... | collective-permute-start | bytes 737288 | tf_op jit(solution)/shard_map/ppermute | solution.py:181
  176.7 3.6 %collective-permute-done.8.refs_4_ = bf16[3,80,512]{2,1,0:T(8,128)(2,1)S(1)} collective-permute-done((bf16[3,80,512]{2,1,0:T(8,128)(2,1)S(1)}, bf16[3,80,512]{2,1,0:T(8,128)(2,1)S(1)}, u32[]{:S(2)}, u32[]{:S(2)}) %collective-permute-start.8) | collective-permute-done | bytes 245792 | tf_op jit(solution)/shard_map/ppermute | solution.py:181
  180.3 4.3 %collective-permute-done.7.refs_3_ = bf16[3,80,512]{2,1,0:T(8,128)(2,1)S(1)} collective-permute-done((bf16[3,80,512]{2,1,0:T(8,128)(2,1)S(1)}, bf16[3,80,512]{2,1,0:T(8,128)(2,1)S(1)}, u32[]{:S(2)}, u32[]{:S(2)}) %collective-permute-start.7) | collective-permute-done | bytes 245792 | tf_op jit(solution)/shard_map/ppermute | solution.py:181
  186.1 2.0 copy-done.3
  190.2 7.5 %grad_rows.2 = (bf16[640,896]{1,0:T(8,128)(2,1)S(1)}, bf16[3,640,1024]{2,1,0:T(8,128)(2,1)}) custom-call(s32[2]{0:T(128)S(1)} %pad_add_fusion.place, bf16[2,3,80,512]{3,2,1,0:T(8,128)(2,1)} %swiglu.2.refs_0_, bf16[2,3,80,512]{3,2,1,0:T(8,128)(2,1)} %collective-permute-done.5.refs_1_, bf16[2,3,80,512]{3,2,1,0:T(8,128)(2,1)} %collective-permute-done.6.refs_2_, ...), custom_call_target="tpu_custom_call" | custom-call | flops 2348810240 | bytes 12845056 | tf_op jit(solution)/shard_map/grad_rows/pallas_call | solution.py:244
  198.8 6.9 %all-to-all-start.1 = ((bf16[16,40,896]{2,1,0:T(8,128)(2,1)}), bf16[16,40,896]{2,1,0:T(8,128)(2,1)}, u32[]{:S(2)}, u32[]{:S(2)}) async-start(bf16[16,40,896]{2,1,0:T(8,128)(2,1)} %bitcast.32), calls=%async_computation.1 | async-start | bytes 2293760 | tf_op jit(solution)/shard_map/all_to_all | solution.py:345
  205.7 2.1 copy-done.15
  207.8 7.7 %weight_grads.2 = (bf16[2,896,1024]{2,1,0:T(8,128)(2,1)}, bf16[2,896,1024]{2,1,0:T(8,128)(2,1)}, bf16[2,1024,896]{2,1,0:T(8,128)(2,1)}) custom-call(bf16[3,640,1024]{2,1,0:T(8,128)(2,1)S(1)} %copy-done.15, bf16[640,1792]{1,0:T(8,128)(2,1)} %bitcast.3.rows_ref), custom_call_target="tpu_custom_call" | custom-call | flops 3523215360 | bytes 12058624 | tf_op jit(solution)/shard_map/weight_grads/pallas_call | solution.py:279
  215.5 6.1 %weight_grads.3 = (bf16[2,896,1024]{2,1,0:T(8,128)(2,1)}, bf16[2,896,1024]{2,1,0:T(8,128)(2,1)}, bf16[2,1024,896]{2,1,0:T(8,128)(2,1)}) custom-call(bf16[3,640,1024]{2,1,0:T(8,128)(2,1)S(1)} %copy-done.8, bf16[640,1792]{1,0:T(8,128)(2,1)S(1)} %bitcast.27, ...), custom_call_target="tpu_custom_call", output_to_operand_aliasing={{0}: (2, {}), {1}: (3, {}), {2}: (4, {})} | custom-call | flops 3523215360 | bytes 12058624 | tf_op jit(solution)/shard_map/weight_grads/pallas_call | solution.py:279
  221.5 3.3 %all-to-all-done.1 = bf16[16,40,896]{2,1,0:T(8,128)(2,1)} async-done(((bf16[16,40,896]{2,1,0:T(8,128)(2,1)}), bf16[16,40,896]{2,1,0:T(8,128)(2,1)}, u32[]{:S(2)}, u32[]{:S(2)}) %all-to-all-start.1) | async-done | bytes 1146912 | tf_op jit(solution)/shard_map/all_to_all | solution.py:345
  224.9 2.5 %combine.1 = bf16[128,896]{1,0:T(8,128)(2,1)} custom-call(f32[128,128]{1,0:T(8,128)S(1)} %get-tuple-element.21.pos_ref, bf16[640,896]{1,0:T(8,128)(2,1)} %bitcast.9.refs_0_, bf16[640,896]{1,0:T(8,128)(2,1)S(1)} %bitcast.28), custom_call_target="tpu_custom_call" | custom-call | flops 293601280 | bytes 2293760 | tf_op jit(solution)/shard_map/combine/pallas_call | solution.py:313
  (96 shorter events, 38.2 us)
Async XLA Ops:
  6.7 41.8 %all-to-all-start.2 = ((bf16[16,40,1792]{2,1,0:T(8,128)(2,1)}), bf16[16,40,1792]{2,1,0:T(8,128)(2,1)S(1)}, u32[]{:S(2)}, u32[]{:S(2)}) async-start(bf16[16,40,1792]{2,1,0:T(8,128)(2,1)} %bitcast.30), calls=%async_computation.2 | async-start | bytes 4587520 | tf_op jit(solution)/shard_map/all_to_all | solution.py:337
  48.5 36.8 %all-to-all-start = ((bf16[16,40,1792]{2,1,0:T(8,128)(2,1)}), bf16[16,40,1792]{2,1,0:T(8,128)(2,1)}, u32[]{:S(2)}, u32[]{:S(2)}) async-start(bf16[16,40,1792]{2,1,0:T(8,128)(2,1)} %bitcast.29), calls=%async_computation | async-start | bytes 4587520 | tf_op jit(solution)/shard_map/all_to_all | solution.py:337
  66.4 30.6 %collective-permute-start.14 = (bf16[8,3,80,512]{3,2,1,0:T(8,128)(2,1)}, bf16[8,3,80,512]{3,2,1,0:T(8,128)(2,1)}, u32[]{:S(2)}, u32[]{:S(2)}) collective-permute-start(bf16[8,3,80,512]{3,2,1,0:T(8,128)(2,1)} %get-tuple-element.28), channel_id=1, source_target_pairs={{0,1},{1,0},{2,3},{3,2},{4,5},{5,4},{6,7},{7,6},{8,9},{9,8},{10,11... | collective-permute-start | bytes 5898248 | tf_op jit(solution)/shard_map/ppermute | solution.py:181
  96.9 20.5 %collective-permute-start = (bf16[8,3,80,512]{3,2,1,0:T(8,128)(2,1)S(1)}, bf16[8,3,80,512]{3,2,1,0:T(8,128)(2,1)S(1)}, u32[]{:S(2)}, u32[]{:S(2)}) collective-permute-start(bf16[8,3,80,512]{3,2,1,0:T(8,128)(2,1)S(1)} %get-tuple-element.24), channel_id=1, source_target_pairs={{0,1},{1,0},{2,3},{3,2},{4,5},{5,4},{6,7},{7,6},{8,9},{9,8},{10,11... | collective-permute-start | bytes 5898248 | tf_op jit(solution)/shard_map/ppermute | solution.py:181
  98.3 15.9 %collective-permute-start.16 = (bf16[2,3,80,512]{3,2,1,0:T(8,128)(2,1)S(1)}, bf16[2,3,80,512]{3,2,1,0:T(8,128)(2,1)S(1)}, u32[]{:S(2)}, u32[]{:S(2)}) collective-permute-start(bf16[2,3,80,512]{3,2,1,0:T(8,128)(2,1)S(1)} %get-tuple-element.38), channel_id=1, source_target_pairs={{0,2},{1,3},{2,4},{3,5},{4,6},{5,7},{6,0},{7,1},{8,10},{9,11},{10,... | collective-permute-start | bytes 1474568 | tf_op jit(solution)/shard_map/ppermute | solution.py:181
  100.3 14.0 %collective-permute-start.15 = (bf16[2,3,80,512]{3,2,1,0:T(8,128)(2,1)S(1)}, bf16[2,3,80,512]{3,2,1,0:T(8,128)(2,1)S(1)}, u32[]{:S(2)}, u32[]{:S(2)}) collective-permute-start(bf16[2,3,80,512]{3,2,1,0:T(8,128)(2,1)S(1)} %get-tuple-element.39), channel_id=1, source_target_pairs={{0,6},{1,7},{2,0},{3,1},{4,2},{5,3},{6,4},{7,5},{8,14},{9,15},{10,... | collective-permute-start | bytes 1474568 | tf_op jit(solution)/shard_map/ppermute | solution.py:181
  114.3 9.5 %collective-permute-start.18 = (bf16[3,80,512]{2,1,0:T(8,128)(2,1)S(1)}, bf16[3,80,512]{2,1,0:T(8,128)(2,1)S(1)}, u32[]{:S(2)}, u32[]{:S(2)}) collective-permute-start(bf16[3,80,512]{2,1,0:T(8,128)(2,1)S(1)} %get-tuple-element.42), channel_id=1, source_target_pairs={{0,6},{1,7},{2,0},{3,1},{4,2},{5,3},{6,4},{7,5},{8,14},{9,15},{10,... | collective-permute-start | bytes 737288 | tf_op jit(solution)/shard_map/ppermute | solution.py:181
  117.4 10.1 %collective-permute-start.17 = (bf16[3,80,512]{2,1,0:T(8,128)(2,1)S(1)}, bf16[3,80,512]{2,1,0:T(8,128)(2,1)S(1)}, u32[]{:S(2)}, u32[]{:S(2)}) collective-permute-start(bf16[3,80,512]{2,1,0:T(8,128)(2,1)S(1)} %get-tuple-element.43), channel_id=1, source_target_pairs={{0,2},{1,3},{2,4},{3,5},{4,6},{5,7},{6,0},{7,1},{8,10},{9,11},{10,... | collective-permute-start | bytes 737288 | tf_op jit(solution)/shard_map/ppermute | solution.py:181
  117.6 20.5 %collective-permute-start.2 = (bf16[2,3,80,512]{3,2,1,0:T(8,128)(2,1)S(1)}, bf16[2,3,80,512]{3,2,1,0:T(8,128)(2,1)S(1)}, u32[]{:S(2)}, u32[]{:S(2)}) collective-permute-start(bf16[2,3,80,512]{3,2,1,0:T(8,128)(2,1)S(1)} %get-tuple-element.40), channel_id=1, source_target_pairs={{0,2},{1,3},{2,4},{3,5},{4,6},{5,7},{6,0},{7,1},{8,10},{9,11},{10,... | collective-permute-start | bytes 1474568 | tf_op jit(solution)/shard_map/ppermute | solution.py:181
  117.9 20.2 %collective-permute-start.1 = (bf16[2,3,80,512]{3,2,1,0:T(8,128)(2,1)S(1)}, bf16[2,3,80,512]{3,2,1,0:T(8,128)(2,1)S(1)}, u32[]{:S(2)}, u32[]{:S(2)}) collective-permute-start(bf16[2,3,80,512]{3,2,1,0:T(8,128)(2,1)S(1)} %get-tuple-element.41), channel_id=1, source_target_pairs={{0,6},{1,7},{2,0},{3,1},{4,2},{5,3},{6,4},{7,5},{8,14},{9,15},{10,... | collective-permute-start | bytes 1474568 | tf_op jit(solution)/shard_map/ppermute | solution.py:181
  127.8 17.0 %collective-permute-start.20 = (bf16[2,3,80,512]{3,2,1,0:T(8,128)(2,1)S(1)}, bf16[2,3,80,512]{3,2,1,0:T(8,128)(2,1)S(1)}, u32[]{:S(2)}, u32[]{:S(2)}) collective-permute-start(bf16[2,3,80,512]{3,2,1,0:T(8,128)(2,1)S(1)} %swiglu.3.refs_0_), channel_id=1, source_target_pairs={{0,6},{1,7},{2,0},{3,1},{4,2},{5,3},{6,4},{7,5},{8,14},{9,15},{10,... | collective-permute-start | bytes 1474568 | tf_op jit(solution)/shard_map/ppermute | solution.py:181
  128.1 20.6 %collective-permute-start.19 = (bf16[2,3,80,512]{3,2,1,0:T(8,128)(2,1)S(1)}, bf16[2,3,80,512]{3,2,1,0:T(8,128)(2,1)S(1)}, u32[]{:S(2)}, u32[]{:S(2)}) collective-permute-start(bf16[2,3,80,512]{3,2,1,0:T(8,128)(2,1)S(1)} %swiglu.3.refs_0_), channel_id=1, source_target_pairs={{0,2},{1,3},{2,4},{3,5},{4,6},{5,7},{6,0},{7,1},{8,10},{9,11},{10,... | collective-permute-start | bytes 1474568 | tf_op jit(solution)/shard_map/ppermute | solution.py:181
  138.1 12.0 %collective-permute-start.4 = (bf16[3,80,512]{2,1,0:T(8,128)(2,1)S(1)}, bf16[3,80,512]{2,1,0:T(8,128)(2,1)S(1)}, u32[]{:S(2)}, u32[]{:S(2)}) collective-permute-start(bf16[3,80,512]{2,1,0:T(8,128)(2,1)S(1)} %get-tuple-element.44), channel_id=1, source_target_pairs={{0,6},{1,7},{2,0},{3,1},{4,2},{5,3},{6,4},{7,5},{8,14},{9,15},{10,... | collective-permute-start | bytes 737288 | tf_op jit(solution)/shard_map/ppermute | solution.py:181
  138.2 14.0 %collective-permute-start.3 = (bf16[3,80,512]{2,1,0:T(8,128)(2,1)S(1)}, bf16[3,80,512]{2,1,0:T(8,128)(2,1)S(1)}, u32[]{:S(2)}, u32[]{:S(2)}) collective-permute-start(bf16[3,80,512]{2,1,0:T(8,128)(2,1)S(1)} %get-tuple-element.45), channel_id=1, source_target_pairs={{0,2},{1,3},{2,4},{3,5},{4,6},{5,7},{6,0},{7,1},{8,10},{9,11},{10,... | collective-permute-start | bytes 737288 | tf_op jit(solution)/shard_map/ppermute | solution.py:181
  140.2 15.0 %collective-permute-start.23 = (bf16[2,3,80,512]{3,2,1,0:T(8,128)(2,1)S(1)}, bf16[2,3,80,512]{3,2,1,0:T(8,128)(2,1)S(1)}, u32[]{:S(2)}, u32[]{:S(2)}) collective-permute-start(bf16[2,3,80,512]{3,2,1,0:T(8,128)(2,1)S(1)} %swiglu.3.refs_0_), channel_id=1, source_target_pairs={{0,1},{1,0},{2,3},{3,2},{4,5},{5,4},{6,7},{7,6},{8,9},{9,8},{10,11... | collective-permute-start | bytes 1474568 | tf_op jit(solution)/shard_map/ppermute | solution.py:181
  144.9 9.2 %collective-permute-start.22 = (bf16[3,80,512]{2,1,0:T(8,128)(2,1)S(1)}, bf16[3,80,512]{2,1,0:T(8,128)(2,1)S(1)}, u32[]{:S(2)}, u32[]{:S(2)}) collective-permute-start(bf16[3,80,512]{2,1,0:T(8,128)(2,1)S(1)} %slice_bitcast_fusion), channel_id=1, source_target_pairs={{0,6},{1,7},{2,0},{3,1},{4,2},{5,3},{6,4},{7,5},{8,14},{9,15},{10,... | collective-permute-start | bytes 737288 | tf_op jit(solution)/shard_map/ppermute | solution.py:181
  148.6 10.5 %collective-permute-start.25 = (bf16[2,3,80,512]{3,2,1,0:T(8,128)(2,1)S(1)}, bf16[2,3,80,512]{3,2,1,0:T(8,128)(2,1)S(1)}, u32[]{:S(2)}, u32[]{:S(2)}) collective-permute-start(bf16[2,3,80,512]{3,2,1,0:T(8,128)(2,1)S(1)} %collective-permute-done.20.refs_2_), channel_id=1, source_target_pairs={{0,1},{1,0},{2,3},{3,2},{4,5},{5,4},{6,7},{7,6},{8,9},{9,8},{10,11... | collective-permute-start | bytes 1474568 | tf_op jit(solution)/shard_map/ppermute | solution.py:181
  150.1 8.8 %collective-permute-start.21 = (bf16[3,80,512]{2,1,0:T(8,128)(2,1)S(1)}, bf16[3,80,512]{2,1,0:T(8,128)(2,1)S(1)}, u32[]{:S(2)}, u32[]{:S(2)}) collective-permute-start(bf16[3,80,512]{2,1,0:T(8,128)(2,1)S(1)} %slice_bitcast_fusion.1), channel_id=1, source_target_pairs={{0,2},{1,3},{2,4},{3,5},{4,6},{5,7},{6,0},{7,1},{8,10},{9,11},{10,... | collective-permute-start | bytes 737288 | tf_op jit(solution)/shard_map/ppermute | solution.py:181
  152.2 8.2 %collective-permute-start.24 = (bf16[2,3,80,512]{3,2,1,0:T(8,128)(2,1)S(1)}, bf16[2,3,80,512]{3,2,1,0:T(8,128)(2,1)S(1)}, u32[]{:S(2)}, u32[]{:S(2)}) collective-permute-start(bf16[2,3,80,512]{3,2,1,0:T(8,128)(2,1)S(1)} %collective-permute-done.19.refs_1_), channel_id=1, source_target_pairs={{0,1},{1,0},{2,3},{3,2},{4,5},{5,4},{6,7},{7,6},{8,9},{9,8},{10,11... | collective-permute-start | bytes 1474568 | tf_op jit(solution)/shard_map/ppermute | solution.py:181
  154.1 5.0 %collective-permute-start.27 = (bf16[3,80,512]{2,1,0:T(8,128)(2,1)S(1)}, bf16[3,80,512]{2,1,0:T(8,128)(2,1)S(1)}, u32[]{:S(2)}, u32[]{:S(2)}) collective-permute-start(bf16[3,80,512]{2,1,0:T(8,128)(2,1)S(1)} %collective-permute-done.22.refs_4_), channel_id=1, source_target_pairs={{0,1},{1,0},{2,3},{3,2},{4,5},{5,4},{6,7},{7,6},{8,9},{9,8},{10,11... | collective-permute-start | bytes 737288 | tf_op jit(solution)/shard_map/ppermute | solution.py:181
  155.2 16.0 %collective-permute-start.6 = (bf16[2,3,80,512]{3,2,1,0:T(8,128)(2,1)}, bf16[2,3,80,512]{3,2,1,0:T(8,128)(2,1)}, u32[]{:S(2)}, u32[]{:S(2)}) collective-permute-start(bf16[2,3,80,512]{3,2,1,0:T(8,128)(2,1)} %swiglu.2.refs_0_), channel_id=1, source_target_pairs={{0,6},{1,7},{2,0},{3,1},{4,2},{5,3},{6,4},{7,5},{8,14},{9,15},{10,... | collective-permute-start | bytes 1474568 | tf_op jit(solution)/shard_map/ppermute | solution.py:181
  158.9 1.5 collective-permute-start.26
  159.1 16.0 %collective-permute-start.5 = (bf16[2,3,80,512]{3,2,1,0:T(8,128)(2,1)}, bf16[2,3,80,512]{3,2,1,0:T(8,128)(2,1)}, u32[]{:S(2)}, u32[]{:S(2)}) collective-permute-start(bf16[2,3,80,512]{3,2,1,0:T(8,128)(2,1)} %swiglu.2.refs_0_), channel_id=1, source_target_pairs={{0,2},{1,3},{2,4},{3,5},{4,6},{5,7},{6,0},{7,1},{8,10},{9,11},{10,... | collective-permute-start | bytes 1474568 | tf_op jit(solution)/shard_map/ppermute | solution.py:181
  159.1 25.5 %collective-permute-start.9 = (bf16[2,3,80,512]{3,2,1,0:T(8,128)(2,1)}, bf16[2,3,80,512]{3,2,1,0:T(8,128)(2,1)}, u32[]{:S(2)}, u32[]{:S(2)}) collective-permute-start(bf16[2,3,80,512]{3,2,1,0:T(8,128)(2,1)} %swiglu.2.refs_0_), channel_id=1, source_target_pairs={{0,1},{1,0},{2,3},{3,2},{4,5},{5,4},{6,7},{7,6},{8,9},{9,8},{10,11... | collective-permute-start | bytes 1474568 | tf_op jit(solution)/shard_map/ppermute | solution.py:181
  167.5 31.3 %all-to-all-start.3 = ((bf16[16,40,896]{2,1,0:T(8,128)(2,1)}), bf16[16,40,896]{2,1,0:T(8,128)(2,1)S(1)}, u32[]{:S(2)}, u32[]{:S(2)}) async-start(bf16[16,40,896]{2,1,0:T(8,128)(2,1)} %bitcast.31), calls=%async_computation.3 | async-start | bytes 2293760 | tf_op jit(solution)/shard_map/all_to_all | solution.py:345
  172.2 8.2 %collective-permute-start.8 = (bf16[3,80,512]{2,1,0:T(8,128)(2,1)S(1)}, bf16[3,80,512]{2,1,0:T(8,128)(2,1)S(1)}, u32[]{:S(2)}, u32[]{:S(2)}) collective-permute-start(bf16[3,80,512]{2,1,0:T(8,128)(2,1)S(1)} %slice_bitcast_fusion.2), channel_id=1, source_target_pairs={{0,6},{1,7},{2,0},{3,1},{4,2},{5,3},{6,4},{7,5},{8,14},{9,15},{10,... | collective-permute-start | bytes 737288 | tf_op jit(solution)/shard_map/ppermute | solution.py:181
  176.0 8.6 %collective-permute-start.7 = (bf16[3,80,512]{2,1,0:T(8,128)(2,1)S(1)}, bf16[3,80,512]{2,1,0:T(8,128)(2,1)S(1)}, u32[]{:S(2)}, u32[]{:S(2)}) collective-permute-start(bf16[3,80,512]{2,1,0:T(8,128)(2,1)S(1)} %slice_bitcast_fusion.3), channel_id=1, source_target_pairs={{0,2},{1,3},{2,4},{3,5},{4,6},{5,7},{6,0},{7,1},{8,10},{9,11},{10,... | collective-permute-start | bytes 737288 | tf_op jit(solution)/shard_map/ppermute | solution.py:181
  176.1 8.5 %collective-permute-start.11 = (bf16[2,3,80,512]{3,2,1,0:T(8,128)(2,1)}, bf16[2,3,80,512]{3,2,1,0:T(8,128)(2,1)S(1)}, u32[]{:S(2)}, u32[]{:S(2)}) collective-permute-start(bf16[2,3,80,512]{3,2,1,0:T(8,128)(2,1)} %collective-permute-done.6.refs_2_), channel_id=1, source_target_pairs={{0,1},{1,0},{2,3},{3,2},{4,5},{5,4},{6,7},{7,6},{8,9},{9,8},{10,11... | collective-permute-start | bytes 1474568 | tf_op jit(solution)/shard_map/ppermute | solution.py:181
  176.2 9.9 %collective-permute-start.10 = (bf16[2,3,80,512]{3,2,1,0:T(8,128)(2,1)}, bf16[2,3,80,512]{3,2,1,0:T(8,128)(2,1)S(1)}, u32[]{:S(2)}, u32[]{:S(2)}) collective-permute-start(bf16[2,3,80,512]{3,2,1,0:T(8,128)(2,1)} %collective-permute-done.5.refs_1_), channel_id=1, source_target_pairs={{0,1},{1,0},{2,3},{3,2},{4,5},{5,4},{6,7},{7,6},{8,9},{9,8},{10,11... | collective-permute-start | bytes 1474568 | tf_op jit(solution)/shard_map/ppermute | solution.py:181
  180.3 4.3 %collective-permute-start.13 = (bf16[3,80,512]{2,1,0:T(8,128)(2,1)S(1)}, bf16[3,80,512]{2,1,0:T(8,128)(2,1)S(1)}, u32[]{:S(2)}, u32[]{:S(2)}) collective-permute-start(bf16[3,80,512]{2,1,0:T(8,128)(2,1)S(1)} %collective-permute-done.8.refs_4_), channel_id=1, source_target_pairs={{0,1},{1,0},{2,3},{3,2},{4,5},{5,4},{6,7},{7,6},{8,9},{9,8},{10,11... | collective-permute-start | bytes 737288 | tf_op jit(solution)/shard_map/ppermute | solution.py:181
  184.6 1.5 collective-permute-start.12
  198.8 26.1 %all-to-all-start.1 = ((bf16[16,40,896]{2,1,0:T(8,128)(2,1)}), bf16[16,40,896]{2,1,0:T(8,128)(2,1)}, u32[]{:S(2)}, u32[]{:S(2)}) async-start(bf16[16,40,896]{2,1,0:T(8,128)(2,1)} %bitcast.32), calls=%async_computation.1 | async-start | bytes 2293760 | tf_op jit(solution)/shard_map/all_to_all | solution.py:345
  (20 other events, 106.9 us)

commit v2 on v1

v2 whole, which is shorter than its diff:
```python
import functools
import jax
import jax.numpy as jnp
from jax import lax
from jax.experimental import pallas as pl
from jax.experimental.pallas import tpu as pltpu
from jax.sharding import PartitionSpec as P

BF = jnp.bfloat16
F32 = jnp.float32
MIB = 1024 * 1024
BIG = 20
NN = (((1,), (0,)), ((), ()))
NT = (((1,), (1,)), ((), ()))
TN = (((0,), (0,)), ((), ()))


def dot(a, b, dims):
    return lax.dot_general(a, b, dims, preferred_element_type=F32)


def params(mib):
    return pltpu.CompilerParams(vmem_limit_bytes=mib * MIB)


def cost(flops, moved):
    return pl.CostEstimate(flops=flops, bytes_accessed=moved, transcendentals=0)


def whole(shape):
    return pl.BlockSpec(shape, lambda *_: (0,) * len(shape))


ANY = pl.BlockSpec(memory_space=pl.ANY)
VM = pl.BlockSpec(memory_space=pltpu.VMEM)
SM = pl.BlockSpec(memory_space=pltpu.SMEM)


def copy(src, dst, sems, i):
    c = pltpu.make_async_copy(src, dst, sems.at[i])
    c.start()
    return c


def in_hbm(x):
    return pltpu.with_memory_space_constraint(x, pltpu.HBM)


def slot_map(ids, gates, experts):
    top, tok = ids.shape
    row = lax.broadcasted_iota(jnp.int32, (experts, tok), 0)
    named = jnp.zeros((experts, tok), F32)
    weight = jnp.zeros((experts, tok), F32)
    for k in range(top):
        hit = ids[k : k + 1, :] == row
        named = jnp.where(hit, 1.0, named)
        weight = jnp.where(hit, gates[k : k + 1, :], weight)
    at = lax.broadcasted_iota(jnp.int32, (tok, tok), 0)
    before = (at < lax.broadcasted_iota(jnp.int32, (tok, tok), 1)).astype(BF)
    pos = dot(named.astype(BF), before, NN)
    return jnp.where(named > 0.0, pos, -1.0), weight


def one_hot(pos, e, cap, exp_local, nodes):
    slot = lax.broadcasted_iota(jnp.int32, (cap, pos.shape[1]), 0).astype(F32)
    return jnp.concatenate(
        [
            (pos[n * exp_local + e : n * exp_local + e + 1, :] == slot).astype(F32)
            for n in range(nodes)
        ],
        axis=0,
    )


def pack_kernel(cols, cap, exp_local, nodes, ids_ref, gates_ref, tok_ref, grad_ref, *refs):
    out_ref, pos_ref, out_val, sems = refs[-4:]
    outs = []
    pos, weight = slot_map(ids_ref[...], gates_ref[...], exp_local * nodes)
    pos_ref[...] = pos
    width = tok_ref.shape[1]
    for e in range(exp_local):
        if all(col[0] != e for col in cols):
            continue
        sel = one_hot(pos, e, cap, exp_local, nodes)
        sel_bf = sel.astype(BF)
        for i, (col_e, kind) in enumerate(cols):
            at = slice(i * width, (i + 1) * width)
            if col_e == e and kind == 0:
                out_val[:, at] = dot(sel_bf, tok_ref[...], NN).astype(BF)
                outs.append(copy(out_val.at[:, at], out_ref.at[:, at], sems, i))
            elif col_e == e:
                scale = jnp.concatenate(
                    [
                        jnp.sum(
                            sel[n * cap : (n + 1) * cap]
                            * weight[n * exp_local + e : n * exp_local + e + 1, :],
                            axis=1,
                            keepdims=True,
                        )
                        for n in range(nodes)
                    ],
                    axis=0,
                )
                out_val[:, at] = (scale * dot(sel_bf, grad_ref[...], NN)).astype(BF)
                outs.append(copy(out_val.at[:, at], out_ref.at[:, at], sems, i))
    for c in outs:
        c.wait()


def pack(cols, cap, exp_local, nodes, ids, gates, tokens, out_grad, after):
    tok, width = tokens.shape
    rows = nodes * cap
    return pl.pallas_call(
        functools.partial(pack_kernel, cols, cap, exp_local, nodes),
        out_shape=(
            pltpu.HBM((rows, len(cols) * width), BF),
            jax.ShapeDtypeStruct((exp_local * nodes, tok), F32),
        ),
        in_specs=[VM] * 4 + [ANY] * len(after),
        out_specs=(pl.BlockSpec(memory_space=pltpu.HBM), VM),
        scratch_shapes=[
            pltpu.VMEM((rows, len(cols) * width), BF),
            pltpu.SemaphoreType.DMA((len(cols),)),
        ],
        compiler_params=params(24),
        cost_estimate=cost(1, 1),
        name="pack",
    )(ids.T, gates.T, in_hbm(tokens), in_hbm(out_grad), *after)


def ring_slot(half, j):
    if half == 0:
        return jnp.where(j == 0, 6, jnp.where(j == 1, 4, jnp.where(j == 2, 0, 3)))
    return jnp.where(j == 0, 7, jnp.where(j == 1, 1, jnp.where(j == 2, 2, 5)))


def products_kernel(e, blk, ks, x_at, dy_at, n_after, place, x_ref, dy_ref, *refs):
    w_refs = refs[:3]
    own_ref, *other_refs, x, w, wd, stage, sems, out_sems = refs[3 + n_after :]
    z, core = place[0], place[1]
    rows, width = x.shape[1:]
    hh = wd.shape[1]
    cols = [slice(0, hh), slice(hh, 2 * hh)]

    def rows_copy(kind):
        ref, at = ((x_ref, x_at), (dy_ref, dy_at))[kind]
        return copy(ref.at[:, at * width : (at + 1) * width], x.at[kind], sems, kind)

    def weight_copies(k):
        if k == 2:
            return [copy(w_refs[2].at[e, cols[h]], wd.at[h], sems, 6 + h) for h in range(2)]
        return [copy(w_refs[k].at[e, :, cols[h]], w.at[k, h], sems, 2 + 2 * k + h) for h in range(2)]

    x_in = {ks[0] // 2: rows_copy(ks[0] // 2)}
    w_in = {ks[0]: weight_copies(ks[0])}
    outs = []
    for k in ks:
        for h in range(2):
            if h == 0 and k in (ks[0], 2):
                x_in[k // 2].wait()
            w_in[k][h].wait()
            if k == ks[0] and h == 0:
                for later in ks[1:]:
                    if later == 2:
                        x_in[1] = rows_copy(1)
                    w_in[later] = weight_copies(later)
            val = dot(x[k // 2], wd[h] if k == 2 else w[k, h], NT if k == 2 else NN).astype(BF)
            for q in range(rows // blk):
                slot = ring_slot(h, lax.rem(q // 2 - z + 4, 4))
                stage[lax.rem(q + core, 2), slot, k] = val[q * blk : (q + 1) * blk]
        outs.append(copy(
            stage.at[1, :, k],
            other_refs[0].at[:, k] if len(other_refs) == 1 else other_refs[k].at[:, 0],
            out_sems,
            2 * k + 1,
        ))
        outs.append(copy(stage.at[0, :, k], own_ref.at[:, k], out_sems, 2 * k))
    for c in outs:
        c.wait()


def products(e, blk, ks, place, x_rows, dy_rows, weights, after, pieces):
    (x_arr, x_at), (dy_arr, dy_at) = x_rows, dy_rows
    rows = x_arr.shape[0]
    width, hidden = weights[0].shape[1:]
    hh = hidden // 2
    out = jax.ShapeDtypeStruct((8, 3, blk, hh), BF)
    return pl.pallas_call(
        functools.partial(products_kernel, e, blk, ks, x_at, dy_at, len(after)),
        out_shape=(out,)
        + tuple(jax.ShapeDtypeStruct((8, 3 // pieces, blk, hh), BF) for _ in range(pieces)),
        in_specs=[SM] + [ANY] * (5 + len(after)),
        out_specs=[ANY] * (1 + pieces),
        scratch_shapes=[
            pltpu.VMEM((2, rows, width), BF),
            pltpu.VMEM((2, 2, width, hh), BF),
            pltpu.VMEM((2, hh, width), BF),
            pltpu.VMEM((2, 8, 3, blk, hh), BF),
            pltpu.SemaphoreType.DMA((8,)),
            pltpu.SemaphoreType.DMA((6,)),
        ],
        compiler_params=params(BIG),
        cost_estimate=cost(1, 1),
        name="products",
    )(place, in_hbm(x_arr), in_hbm(dy_arr), *[in_hbm(w) for w in weights], *after)


def swiglu_kernel(kept_ref, rm_ref, rp_ref, sp_ref, sm_ref, *refs):
    out_ref = refs[-1]
    for half, (direct, ringed) in enumerate(((rm_ref, sp_ref), (rp_ref, sm_ref))):
        gate, up, gh = [
            kept_ref[2 + half, k].astype(F32)
            + direct[1, k].astype(F32)
            + ringed[k].astype(F32)
            for k in range(3)
        ]
        sig = jax.nn.sigmoid(gate)
        act = gate * sig
        out_ref[half, 0] = (act * up).astype(BF)
        out_ref[half, 1] = (gh * up * sig * (1.0 + gate * (1.0 - sig))).astype(BF)
        out_ref[half, 2] = (gh * act).astype(BF)


def swiglu(kept, rm, rp, sp, sm, after):
    return pl.pallas_call(
        swiglu_kernel,
        out_shape=jax.ShapeDtypeStruct(rm.shape, BF),
        in_specs=[VM] * 5 + [ANY] * len(after),
        out_specs=VM,
        compiler_params=params(24),
        cost_estimate=cost(1, 1),
        name="swiglu",
    )(kept, rm, rp, sp, sm, *after)


def move(x, dz, dcore=0):
    return lax.ppermute(
        x, "local", [(i, ((i // 2 + dz) % 4) * 2 + (i + dcore) % 2) for i in range(8)]
    )


def fold_kernel(kept_ref, rp_ref, rm_ref, *refs):
    next_ref, prev_ref = refs[-2:]
    next_ref[...] = (kept_ref[0].astype(F32) + rp_ref[0].astype(F32)).astype(BF)
    prev_ref[...] = (kept_ref[1].astype(F32) + rm_ref[0].astype(F32)).astype(BF)


def fold(kept, rp, rm, after):
    out = jax.ShapeDtypeStruct(rp.shape[1:], BF)
    return pl.pallas_call(
        fold_kernel,
        out_shape=(out, out),
        in_specs=[VM] * 3 + [ANY] * len(after),
        out_specs=(VM, VM),
        compiler_params=params(24),
        cost_estimate=cost(1, 1),
        name="fold",
    )(kept, rp, rm, *after)


def add_kernel(pieces, own_ref, *refs):
    got_refs = refs[:pieces]
    outs = refs[pieces:]
    for out_ref, at in zip(outs, (0, 2, 4)):
        n = out_ref.shape[0]
        if pieces == 1:
            got = got_refs[0][at : at + n].astype(F32)
            out_ref[...] = (own_ref[at : at + n].astype(F32) + got).astype(BF)
        else:
            for k in range(3):
                got = got_refs[k][at : at + n, 0].astype(F32)
                out_ref[:, k] = (own_ref[at : at + n, k].astype(F32) + got).astype(BF)


def add(own, got):
    tail = own.shape[1:]
    return pl.pallas_call(
        functools.partial(add_kernel, len(got)),
        out_shape=tuple(jax.ShapeDtypeStruct((n,) + tail, BF) for n in (2, 2, 4)),
        compiler_params=params(24),
        cost_estimate=cost(1, 1),
        name="add",
    )(own, *got)


def sum_over_width(own, other, swap_after, last_after, pieces):
    if pieces == 1:
        other = (tie(other, *swap_after),) if swap_after else (other,)
    got = [move(piece, 0, 1) for piece in other]
    to_next, to_prev, kept = add(own, got)
    rp = move(to_next, 1)
    rm = move(to_prev, -1)
    add_next, add_prev = fold(kept, rp, rm, ())
    sp = move(add_next, 1)
    sm = move(add_prev, -1)
    return swiglu(kept, rm, rp, sp, sm, last_after), (sp, sm)


def tie_kernel(*refs):
    del refs


def tie(x, *others):
    return pl.pallas_call(
        tie_kernel,
        out_shape=jax.ShapeDtypeStruct(x.shape, x.dtype),
        in_specs=[ANY] * (1 + len(others)),
        out_specs=ANY,
        input_output_aliases={0: 0},
        compiler_params=params(BIG),
        cost_estimate=cost(1, 1),
        name="tie",
    )(x, *others)


def gather_rows(mine):
    prev = move(mine, 1)
    nxt = move(mine, -1)
    far0 = move(prev[0], 1)
    far1 = move(nxt[1], -1)
    parts = (mine, prev, nxt, far0, far1)
    return parts + tuple(move(p, 0, 1) for p in parts)


def place_rows(blk, z, core, parts, k, dst):
    for c in range(2):
        for i, j in enumerate((0, 3, 1, 2, 2)):
            q = lax.rem(z + j, 4) * 2 + lax.rem(core + c, 2)
            at = pl.ds(pl.multiple_of(q * blk, 16), blk)
            part = parts[5 * c + i]
            for half in range(2):
                for n in range(dst.shape[0]):
                    cols = slice(half * part.shape[-1], (half + 1) * part.shape[-1])
                    if i < 3:
                        dst[n, at, cols] = part[half, k + n]
                    elif half == i - 3:
                        dst[n, at, cols] = part[k + n]


def grad_rows_kernel(e, blk, place, *refs):
    parts = refs[:10]
    wg_ref, wu_ref, out_ref, h_ref, h_val, w, out_val, sems, out_sems = refs[10:]
    w_in = [copy(w_ref.at[e], w.at[n], sems, n) for n, w_ref in enumerate((wg_ref, wu_ref))]
    place_rows(blk, place[0], place[1], parts, 0, h_val)
    w_in[0].wait()
    tot = dot(h_val[1], w[0], NT)
    w_in[1].wait()
    outs = [copy(h_val, h_ref, out_sems, 0)]
    part = out_val.shape[0] // 2
    for m in range(2):
        at = slice(m * part, (m + 1) * part)
        out_val[at] = (tot[at] + dot(h_val[2, at], w[1], NT)).astype(BF)
        outs.append(copy(out_val.at[at], out_ref.at[at], out_sems, 1 + m))
    for c in outs:
        c.wait()


def grad_rows(e, blk, rows, place, parts, weights):
    width, hidden = weights[0].shape[1:]
    return pl.pallas_call(
        functools.partial(grad_rows_kernel, e, blk),
        out_shape=(
            pltpu.HBM((rows, width), BF),
            pltpu.HBM((3, rows, hidden), BF),
        ),
        in_specs=[SM] + [VM] * 10 + [ANY] * 2,
        out_specs=(pl.BlockSpec(memory_space=pltpu.HBM),) * 2,
        scratch_shapes=[
            pltpu.VMEM((3, rows, hidden), BF),
            pltpu.VMEM((2, width, hidden), BF),
            pltpu.VMEM((rows, width), BF),
            pltpu.SemaphoreType.DMA((2,)),
            pltpu.SemaphoreType.DMA((3,)),
        ],
        compiler_params=params(BIG),
        cost_estimate=cost(1, 1),
        name="grad_rows",
    )(place, *parts, *[in_hbm(w) for w in weights[:2]])


def weight_grads_kernel(e, x_at, dy_at, x_ref, dy_ref, h_ref, *refs):
    out_refs = refs[-9:-6]
    x, h_val, dgu, dd, sems, out_sems = refs[-6:]
    width = x.shape[2]
    hh = h_val.shape[2] // 2
    cols = [slice(0, hh), slice(hh, 2 * hh)]
    x_in = [copy(x_ref.at[:, x_at * width : (x_at + 1) * width], x.at[0], sems, 0)]
    h_in = {k: copy(h_ref.at[k], h_val.at[k], sems, 2 + k) for k in (1, 2, 0)}
    x_in.append(copy(dy_ref.at[:, dy_at * width : (dy_at + 1) * width], x.at[1], sems, 1))
    outs = []
    for k in (1, 2, 0):
        h_in[k].wait()
        if k != 2:
            x_in[0 if k == 1 else 1].wait()
        for h in range(2):
            if k == 0:
                dd[h] = dot(h_val[k, :, cols[h]], x[1], TN).astype(BF)
                outs.append(copy(dd.at[h], out_refs[2].at[e, cols[h]], out_sems, 4 + h))
            else:
                dgu[k - 1, h] = dot(x[0], h_val[k, :, cols[h]], TN).astype(BF)
                outs.append(
                    copy(dgu.at[k - 1, h], out_refs[k - 1].at[e, :, cols[h]], out_sems, 2 * k - 2 + h)
                )
    for c in outs:
        c.wait()


def weight_grads(e, exp_local, width, x_rows, dy_rows, hidden_vals, into):
    (x_arr, x_at), (dy_arr, dy_at) = x_rows, dy_rows
    rows, hidden = hidden_vals.shape[1:]
    hh = hidden // 2
    up = jax.ShapeDtypeStruct((exp_local, width, hidden), BF)
    down = jax.ShapeDtypeStruct((exp_local, hidden, width), BF)
    return pl.pallas_call(
        functools.partial(weight_grads_kernel, e, x_at, dy_at),
        out_shape=(up, up, down),
        in_specs=[ANY] * (3 + len(into)),
        out_specs=[ANY] * 3,
        scratch_shapes=[
            pltpu.VMEM((2, rows, width), BF),
            pltpu.VMEM((3, rows, hidden), BF),
            pltpu.VMEM((2, 2, width, hh), BF),
            pltpu.VMEM((2, hh, width), BF),
            pltpu.SemaphoreType.DMA((5,)),
            pltpu.SemaphoreType.DMA((6,)),
        ],
        input_output_aliases={3 + i: i for i in range(len(into))},
        compiler_params=params(BIG),
        cost_estimate=cost(1, 1),
        name="weight_grads",
    )(in_hbm(x_arr), in_hbm(dy_arr), in_hbm(hidden_vals), *into)


def combine_kernel(cap, exp_local, nodes, pos_ref, *refs):
    backs, out_ref = refs[:-1], refs[-1]
    pos = pos_ref[...]
    sel = [one_hot(pos, e, cap, exp_local, nodes).astype(BF) for e in range(exp_local)]
    tot = dot(sel[0], backs[0][...], TN)
    for e in range(1, exp_local):
        tot = tot + dot(sel[e], backs[e][...], TN)
    out_ref[...] = tot.astype(BF)


def combine(cap, exp_local, nodes, pos, backs):
    tok = pos.shape[1]
    rows, width = backs[0].shape
    return pl.pallas_call(
        functools.partial(combine_kernel, cap, exp_local, nodes),
        out_shape=jax.ShapeDtypeStruct((tok, width), BF),
        compiler_params=params(24),
        cost_estimate=cost(1, 1),
        name="combine",
    )(pos, *backs)


def on_device(tokens, out_grad, expert_ids, gates, gate_weight, up_weight, down_weight):
    tok, width = tokens.shape
    top = expert_ids.shape[1]
    nodes = lax.axis_size("node")
    exp_local = gate_weight.shape[0]
    cap = tok * top * 5 // (exp_local * nodes * 4)
    rows = nodes * cap
    blk = rows // 8
    local = lax.axis_index("local")
    place = jnp.stack([local // 2, local % 2]).astype(jnp.int32)

    weights = (gate_weight, up_weight, down_weight)
    def exchange(x):
        return lax.all_to_all(x, "node", split_axis=0, concat_axis=0, tiled=True)

    pack_args = (cap, exp_local, nodes, expert_ids, gates, tokens, out_grad)
    first, pos = pack(((0, 0), (0, 1)), *pack_args, (place,))
    second, packed = pack(((1, 0), (1, 1)), *pack_args, ())
    got = (exchange(first), exchange(second))
    x_rows = tuple((g, 0) for g in got)
    dy_rows = tuple((g, 1) for g in got)

    all_ks = (0, 1, 2)
    own0, *other0 = products(0, blk, all_ks, place, x_rows[0], dy_rows[0], weights, (packed,), 3)
    mine0, step2 = sum_over_width(own0, other0, (), (), 3)
    out0, hidden0 = grad_rows(0, blk, rows, place, gather_rows(mine0), weights)
    own1, other1 = products(1, blk, all_ks, place, x_rows[1], dy_rows[1], weights, (), 1)
    mine1, _ = sum_over_width(own1, other1, step2, (), 1)
    out1, hidden1 = grad_rows(1, blk, rows, place, gather_rows(mine1), weights)
    backs = [exchange(out0), exchange(out1)]
    grads = ()
    for e, hidden_vals in enumerate((hidden0, hidden1)):
        grads = weight_grads(e, exp_local, width, x_rows[e], dy_rows[e], hidden_vals, grads)
    grad_tokens = combine(cap, exp_local, nodes, pos, backs)
    return (grad_tokens,) + tuple(grads)


def solution(mesh):
    return jax.shard_map(
        on_device,
        mesh=mesh,
        in_specs=(
            P("node", "local"),
            P("node", "local"),
            P("node", None),
            P("node", None),
            P("node", "local", None),
            P("node", "local", None),
            P("node", None, "local"),
        ),
        out_specs=(
            P("node", "local"),
            P("node", "local", None),
            P("node", "local", None),
            P("node", None, "local"),
        ),
        check_vma=False,
    )
```

time: 228 us -> 197 us (0.86)
  local copies, waits for them, and re-layouts: 25.9 us -> 2.92 us
  waiting for transfers between devices: 99.4 us -> 92.2 us
  other arithmetic: 3.05 us -> 0.08 us
  Pallas kernels: 49.3 us -> 51.8 us
    unnamed x42 -> x10, local copies, waits for them, and re-layouts: 23.9 us -> 2.85 us
    all_to_all x4, waiting for transfers between devices: 54.1 us -> 35.2 us  [exchange(): return lax.all_to_all(x, 'node', split_axis=0, concat_axis=0, tiled=True)]
    ppermute x28 -> x30, waiting for transfers between devices: 45.3 us -> 57 us  [move(): lax.ppermute(x, 'local', [(i, (i // 2 + dz) % 4 * 2 + (i + dcore) % 2) fo...]
    pallas_call x10 -> x15, Pallas kernels: 46.8 us -> 50.5 us  [the longest x2 15.4 us: weight_grads(): pl.pallas_call(functools.partial(weight_grads_kernel, e, x_at, dy_at), ou...]
    add x6 -> x0, other arithmetic: 2.98 us -> none  [the longest x2 1.44 us: sum_over_width(): kept = own[4:8] + got[4:8]]
    ppermute x28 -> x30, starting transfers between devices: 26.6 us -> 24.6 us  [move(): lax.ppermute(x, 'local', [(i, (i // 2 + dz) % 4 * 2 + (i + dcore) % 2) fo...]
  transfers between devices with their start and end apart: 32 -> 34, of which waited for: 15 -> 18; matrix products, arithmetic and copies ran while one was open for 2% -> 0% of each run, Pallas kernels for 20% -> 24%
where the time goes in v2:
time: 197 us; the launch traced here: 196 us
  waiting for transfers between devices  92.2 us (47%)
  Pallas kernels  51.8 us (26%)
  starting transfers between devices  48.1 us (24%)
  local copies, waits for them, and re-layouts  2.92 us (1%)
    ppermute x30, waiting for transfers between devices, move(): lax.ppermute(x, 'local', [(i, (i // 2 + dz) % 4 * 2 + (i + dcore) % 2) fo...  57 us
    all_to_all x4, waiting for transfers between devices, exchange(): return lax.all_to_all(x, 'node', split_axis=0, concat_axis=0, tiled=True)  35.2 us
    ppermute x30, starting transfers between devices, move(): lax.ppermute(x, 'local', [(i, (i // 2 + dz) % 4 * 2 + (i + dcore) % 2) fo...  24.6 us
    all_to_all x4, starting transfers between devices, exchange(): return lax.all_to_all(x, 'node', split_axis=0, concat_axis=0, tiled=True)  23.5 us
    pallas_call x2, Pallas kernels, weight_grads(): pl.pallas_call(functools.partial(weight_grads_kernel, e, x_at, dy_at), ou...  15.4 us
    pallas_call x2, Pallas kernels, products(): pl.pallas_call(functools.partial(products_kernel, e, blk, ks, x_at, dy_at...  15.4 us
    pallas_call x2, Pallas kernels, grad_rows(): pl.pallas_call(functools.partial(grad_rows_kernel, e, blk), out_shape=(pl...  11.9 us
    pallas_call x2, Pallas kernels, pack(): pl.pallas_call(functools.partial(pack_kernel, cols, cap, exp_local, nodes...  6.14 us
  transfers between devices with their start and end apart: 34, of which 18 were waited for; matrix products, arithmetic and copies ran while one was open for 0% of the time, Pallas kernels for 24%

profile of v2, /device:TPU:0, one launch (start us, length us, event | category | flops | bytes accessed | tf_op | source)
XLA Modules:
  0.0 196.1 jit_solution(3224296449376185682)
XLA Ops:
  2.1 3.1 %pack.2 = (bf16[640,1792]{1,0:T(8,128)(2,1)}, f32[32,128]{1,0:T(8,128)S(1)}) custom-call(s32[8,128]{1,0:T(8,128)S(1)} %bitcast.22, f32[8,128]{1,0:T(8,128)S(1)} %bitcast.24, bf16[128,896]{1,0:T(8,128)(2,1)} %tok_ref.3, bf16[128,896]{1,0:T(8,128)(2,1)} %grad_ref.3, s32[2]{0:T(128)S(1)} %pad_add_fusion.refs_0_.place), custom_call_target="tpu_custom_call" | custom-call | flops 1 | bytes 1 | tf_op jit(solution)/shard_map/pack/pallas_call | solution.py:113
  5.2 7.1 %all-to-all-start = ((bf16[16,40,1792]{2,1,0:T(8,128)(2,1)}), bf16[16,40,1792]{2,1,0:T(8,128)(2,1)S(1)}, u32[]{:S(2)}, u32[]{:S(2)}) async-start(bf16[16,40,1792]{2,1,0:T(8,128)(2,1)} %bitcast.31), calls=%async_computation | async-start | bytes 4587520 | tf_op jit(solution)/shard_map/all_to_all | solution.py:469
  12.4 3.1 %pack.3 = (bf16[640,1792]{1,0:T(8,128)(2,1)}, f32[32,128]{1,0:T(8,128)S(1)}) custom-call(s32[8,128]{1,0:T(8,128)S(1)} %bitcast.23, f32[8,128]{1,0:T(8,128)S(1)} %bitcast.25, bf16[128,896]{1,0:T(8,128)(2,1)} %tok_ref.3, bf16[128,896]{1,0:T(8,128)(2,1)} %grad_ref.3), custom_call_target="tpu_custom_call" | custom-call | flops 1 | bytes 1 | tf_op jit(solution)/shard_map/pack/pallas_call | solution.py:113
  15.4 31.4 %all-to-all-done = bf16[16,40,1792]{2,1,0:T(8,128)(2,1)S(1)} async-done(((bf16[16,40,1792]{2,1,0:T(8,128)(2,1)}), bf16[16,40,1792]{2,1,0:T(8,128)(2,1)S(1)}, u32[]{:S(2)}, u32[]{:S(2)}) %all-to-all-start) | async-done | bytes 2293792 | tf_op jit(solution)/shard_map/all_to_all | solution.py:469
  48.3 4.4 %all-to-all-start.2 = ((bf16[16,40,1792]{2,1,0:T(8,128)(2,1)}), bf16[16,40,1792]{2,1,0:T(8,128)(2,1)}, u32[]{:S(2)}, u32[]{:S(2)}) async-start(bf16[16,40,1792]{2,1,0:T(8,128)(2,1)} %bitcast.30), calls=%async_computation.2 | async-start | bytes 4587520 | tf_op jit(solution)/shard_map/all_to_all | solution.py:469
  52.8 7.7 %products.2 = (bf16[8,3,80,512]{3,2,1,0:T(8,128)(2,1)S(1)}, bf16[8,1,80,512]{3,2,1,0:T(8,128)(2,1)S(1)}, bf16[8,1,80,512]{3,2,1,0:T(8,128)(2,1)S(1)}, bf16[8,1,80,512]{3,2,1,0:T(8,128)(2,1)S(1)}) custom-call(s32[2]{0:T(128)S(1)} %pad_add_fusion.refs_0_.place, bf16[640,1792]{1,0:T(8,128)(2,1)} %bitcast.26, bf16[640,1792]{1,0:T(8,128)(2,1)} %bitcast.27, ...), custom_call_target="tpu_custom_call" | custom-call | flops 1 | bytes 1 | tf_op jit(solution)/shard_map/products/pallas_call | solution.py:188
  61.2 1.5 collective-permute-done.refs_0_
  65.0 4.1 %collective-permute-start.3 = (bf16[2,3,80,512]{3,2,1,0:T(8,128)(2,1)S(1)}, bf16[2,3,80,512]{3,2,1,0:T(8,128)(2,1)S(1)}, u32[]{:S(2)}, u32[]{:S(2)}) collective-permute-start(bf16[2,3,80,512]{3,2,1,0:T(8,128)(2,1)S(1)} %get-tuple-element.42), channel_id=1, source_target_pairs={{0,6},{1,7},{2,0},{3,1},{4,2},{5,3},{6,4},{7,5},{8,14},{9,15},{10,... | collective-permute-start | bytes 1474568 | tf_op jit(solution)/shard_map/ppermute | solution.py:237
  69.1 10.8 %collective-permute-done.3.rm_ref = bf16[2,3,80,512]{3,2,1,0:T(8,128)(2,1)S(1)} collective-permute-done((bf16[2,3,80,512]{3,2,1,0:T(8,128)(2,1)S(1)}, bf16[2,3,80,512]{3,2,1,0:T(8,128)(2,1)S(1)}, u32[]{:S(2)}, u32[]{:S(2)}) %collective-permute-start.3) | collective-permute-done | bytes 491552 | tf_op jit(solution)/shard_map/ppermute | solution.py:237
  79.9 3.4 %collective-permute-done.4.rp_ref = bf16[2,3,80,512]{3,2,1,0:T(8,128)(2,1)S(1)} collective-permute-done((bf16[2,3,80,512]{3,2,1,0:T(8,128)(2,1)S(1)}, bf16[2,3,80,512]{3,2,1,0:T(8,128)(2,1)S(1)}, u32[]{:S(2)}, u32[]{:S(2)}) %collective-permute-start.4) | collective-permute-done | bytes 491552 | tf_op jit(solution)/shard_map/ppermute | solution.py:237
  83.5 3.2 %collective-permute-start.6 = (bf16[3,80,512]{2,1,0:T(8,128)(2,1)S(1)}, bf16[3,80,512]{2,1,0:T(8,128)(2,1)S(1)}, u32[]{:S(2)}, u32[]{:S(2)}) collective-permute-start(bf16[3,80,512]{2,1,0:T(8,128)(2,1)S(1)} %get-tuple-element.45), channel_id=1, source_target_pairs={{0,6},{1,7},{2,0},{3,1},{4,2},{5,3},{6,4},{7,5},{8,14},{9,15},{10,... | collective-permute-start | bytes 737288 | tf_op jit(solution)/shard_map/ppermute | solution.py:237
  86.7 7.7 %products.3 = (bf16[8,3,80,512]{3,2,1,0:T(8,128)(2,1)S(1)}, bf16[8,3,80,512]{3,2,1,0:T(8,128)(2,1)S(1)}) custom-call(s32[2]{0:T(128)S(1)} %pad_add_fusion.refs_0_.place, bf16[640,1792]{1,0:T(8,128)(2,1)} %bitcast.11.x_ref.dy_ref, bf16[640,1792]{1,0:T(8,128)(2,1)} %bitcast.11.x_ref.dy_ref, bf16[2,896,1024]{2,1,0:T(8,128)(2,1)} %refs_10_.3, ...), custom_call_target="tpu_custom_call" | custom-call | flops 1 | bytes 1 | tf_op jit(solution)/shard_map/products/pallas_call | solution.py:188
  94.8 2.7 %collective-permute-start.8 = (bf16[2,3,80,512]{3,2,1,0:T(8,128)(2,1)S(1)}, bf16[2,3,80,512]{3,2,1,0:T(8,128)(2,1)S(1)}, u32[]{:S(2)}, u32[]{:S(2)}) collective-permute-start(bf16[2,3,80,512]{3,2,1,0:T(8,128)(2,1)S(1)} %swiglu.2.refs_0_), channel_id=1, source_target_pairs={{0,6},{1,7},{2,0},{3,1},{4,2},{5,3},{6,4},{7,5},{8,14},{9,15},{10,... | collective-permute-start | bytes 1474568 | tf_op jit(solution)/shard_map/ppermute | solution.py:237
  98.9 2.5 %collective-permute-start.17 = (bf16[2,3,80,512]{3,2,1,0:T(8,128)(2,1)S(1)}, bf16[2,3,80,512]{3,2,1,0:T(8,128)(2,1)S(1)}, u32[]{:S(2)}, u32[]{:S(2)}) collective-permute-start(bf16[2,3,80,512]{3,2,1,0:T(8,128)(2,1)S(1)} %get-tuple-element.51), channel_id=1, source_target_pairs={{0,6},{1,7},{2,0},{3,1},{4,2},{5,3},{6,4},{7,5},{8,14},{9,15},{10,... | collective-permute-start | bytes 1474568 | tf_op jit(solution)/shard_map/ppermute | solution.py:237
  101.5 7.6 %collective-permute-done.8.refs_2_ = bf16[2,3,80,512]{3,2,1,0:T(8,128)(2,1)S(1)} collective-permute-done((bf16[2,3,80,512]{3,2,1,0:T(8,128)(2,1)S(1)}, bf16[2,3,80,512]{3,2,1,0:T(8,128)(2,1)S(1)}, u32[]{:S(2)}, u32[]{:S(2)}) %collective-permute-start.8) | collective-permute-done | bytes 491552 | tf_op jit(solution)/shard_map/ppermute | solution.py:237
  109.1 3.7 %collective-permute-start.10 = (bf16[3,80,512]{2,1,0:T(8,128)(2,1)S(1)}, bf16[3,80,512]{2,1,0:T(8,128)(2,1)S(1)}, u32[]{:S(2)}, u32[]{:S(2)}) collective-permute-start(bf16[3,80,512]{2,1,0:T(8,128)(2,1)S(1)} %slice_bitcast_fusion.2), channel_id=1, source_target_pairs={{0,6},{1,7},{2,0},{3,1},{4,2},{5,3},{6,4},{7,5},{8,14},{9,15},{10,... | collective-permute-start | bytes 737288 | tf_op jit(solution)/shard_map/ppermute | solution.py:237
  112.9 6.8 %collective-permute-done.17.rm_ref = bf16[2,3,80,512]{3,2,1,0:T(8,128)(2,1)S(1)} collective-permute-done((bf16[2,3,80,512]{3,2,1,0:T(8,128)(2,1)S(1)}, bf16[2,3,80,512]{3,2,1,0:T(8,128)(2,1)S(1)}, u32[]{:S(2)}, u32[]{:S(2)}) %collective-permute-start.17) | collective-permute-done | bytes 491552 | tf_op jit(solution)/shard_map/ppermute | solution.py:237
  120.2 3.4 %collective-permute-start.20 = (bf16[3,80,512]{2,1,0:T(8,128)(2,1)S(1)}, bf16[3,80,512]{2,1,0:T(8,128)(2,1)S(1)}, u32[]{:S(2)}, u32[]{:S(2)}) collective-permute-start(bf16[3,80,512]{2,1,0:T(8,128)(2,1)S(1)} %get-tuple-element.54), channel_id=1, source_target_pairs={{0,6},{1,7},{2,0},{3,1},{4,2},{5,3},{6,4},{7,5},{8,14},{9,15},{10,... | collective-permute-start | bytes 737288 | tf_op jit(solution)/shard_map/ppermute | solution.py:237
  123.6 3.7 %collective-permute-done.7.refs_1_ = bf16[2,3,80,512]{3,2,1,0:T(8,128)(2,1)S(1)} collective-permute-done((bf16[2,3,80,512]{3,2,1,0:T(8,128)(2,1)S(1)}, bf16[2,3,80,512]{3,2,1,0:T(8,128)(2,1)S(1)}, u32[]{:S(2)}, u32[]{:S(2)}) %collective-permute-start.7) | collective-permute-done | bytes 491552 | tf_op jit(solution)/shard_map/ppermute | solution.py:237
  127.5 5.1 %collective-permute-done.19.sp_ref = bf16[3,80,512]{2,1,0:T(8,128)(2,1)S(1)} collective-permute-done((bf16[3,80,512]{2,1,0:T(8,128)(2,1)S(1)}, bf16[3,80,512]{2,1,0:T(8,128)(2,1)S(1)}, u32[]{:S(2)}, u32[]{:S(2)}) %collective-permute-start.19) | collective-permute-done | bytes 245792 | tf_op jit(solution)/shard_map/ppermute | solution.py:237
  133.9 2.9 %collective-permute-done.9.refs_3_ = bf16[3,80,512]{2,1,0:T(8,128)(2,1)S(1)} collective-permute-done((bf16[3,80,512]{2,1,0:T(8,128)(2,1)S(1)}, bf16[3,80,512]{2,1,0:T(8,128)(2,1)S(1)}, u32[]{:S(2)}, u32[]{:S(2)}) %collective-permute-start.9) | collective-permute-done | bytes 245792 | tf_op jit(solution)/shard_map/ppermute | solution.py:237
  136.7 1.5 collective-permute-done.14.refs_8_
  138.2 5.9 %grad_rows.2 = (bf16[640,896]{1,0:T(8,128)(2,1)}, bf16[3,640,1024]{2,1,0:T(8,128)(2,1)}) custom-call(s32[2]{0:T(128)S(1)} %pad_add_fusion.refs_0_.place, bf16[2,3,80,512]{3,2,1,0:T(8,128)(2,1)S(1)} %swiglu.2.refs_0_, bf16[2,3,80,512]{3,2,1,0:T(8,128)(2,1)S(1)} %collective-permute-done.7.refs_1_, bf16[2,3,80,512]{3,2,1,0:T(8,128)(2,1)S(1)} %collective-permute-done.8.refs_2_, ...), custom_call_target="tpu_custom_call" | custom-call | flops 1 | bytes 1 | tf_op jit(solution)/shard_map/grad_rows/pallas_call | solution.py:360
  144.2 5.0 %all-to-all-start.1 = ((bf16[16,40,896]{2,1,0:T(8,128)(2,1)}), bf16[16,40,896]{2,1,0:T(8,128)(2,1)S(1)}, u32[]{:S(2)}, u32[]{:S(2)}) async-start(bf16[16,40,896]{2,1,0:T(8,128)(2,1)} %bitcast.32), calls=%async_computation.1 | async-start | bytes 2293760 | tf_op jit(solution)/shard_map/all_to_all | solution.py:469
  149.3 1.8 collective-permute-start.24
  152.0 5.7 %collective-permute-done.24.refs_4_ = bf16[3,80,512]{2,1,0:T(8,128)(2,1)S(1)} collective-permute-done((bf16[3,80,512]{2,1,0:T(8,128)(2,1)S(1)}, bf16[3,80,512]{2,1,0:T(8,128)(2,1)S(1)}, u32[]{:S(2)}, u32[]{:S(2)}) %collective-permute-start.24) | collective-permute-done | bytes 245792 | tf_op jit(solution)/shard_map/ppermute | solution.py:237
  157.7 3.5 %collective-permute-done.23.refs_3_ = bf16[3,80,512]{2,1,0:T(8,128)(2,1)S(1)} collective-permute-done((bf16[3,80,512]{2,1,0:T(8,128)(2,1)S(1)}, bf16[3,80,512]{2,1,0:T(8,128)(2,1)S(1)}, u32[]{:S(2)}, u32[]{:S(2)}) %collective-permute-start.23) | collective-permute-done | bytes 245792 | tf_op jit(solution)/shard_map/ppermute | solution.py:237
  162.8 5.9 %grad_rows.3 = (bf16[640,896]{1,0:T(8,128)(2,1)}, bf16[3,640,1024]{2,1,0:T(8,128)(2,1)}) custom-call(s32[2]{0:T(128)S(1)} %pad_add_fusion.refs_0_.place, bf16[2,3,80,512]{3,2,1,0:T(8,128)(2,1)S(1)} %swiglu.3.refs_0_, bf16[2,3,80,512]{3,2,1,0:T(8,128)(2,1)S(1)} %collective-permute-done.21.refs_1_, ...), custom_call_target="tpu_custom_call" | custom-call | flops 1 | bytes 1 | tf_op jit(solution)/shard_map/grad_rows/pallas_call | solution.py:360
  168.7 6.9 %all-to-all-start.3 = ((bf16[16,40,896]{2,1,0:T(8,128)(2,1)}), bf16[16,40,896]{2,1,0:T(8,128)(2,1)S(1)}, u32[]{:S(2)}, u32[]{:S(2)}) async-start(bf16[16,40,896]{2,1,0:T(8,128)(2,1)} %bitcast.33), calls=%async_computation.3 | async-start | bytes 2293760 | tf_op jit(solution)/shard_map/all_to_all | solution.py:469
  175.7 7.7 %weight_grads.2 = (bf16[2,896,1024]{2,1,0:T(8,128)(2,1)}, bf16[2,896,1024]{2,1,0:T(8,128)(2,1)}, bf16[2,1024,896]{2,1,0:T(8,128)(2,1)}) custom-call(bf16[640,1792]{1,0:T(8,128)(2,1)} %bitcast.28, bf16[640,1792]{1,0:T(8,128)(2,1)} %bitcast.29, bf16[3,640,1024]{2,1,0:T(8,128)(2,1)} %get-tuple-element.57.h_ref), custom_call_target="tpu_custom_call" | custom-call | flops 1 | bytes 1 | tf_op jit(solution)/shard_map/weight_grads/pallas_call | solution.py:414
  183.4 7.7 %weight_grads.3 = (bf16[2,896,1024]{2,1,0:T(8,128)(2,1)}, bf16[2,896,1024]{2,1,0:T(8,128)(2,1)}, bf16[2,1024,896]{2,1,0:T(8,128)(2,1)}) custom-call(bf16[640,1792]{1,0:T(8,128)(2,1)} %bitcast.11.x_ref.dy_ref, bf16[640,1792]{1,0:T(8,128)(2,1)} %bitcast.11.x_ref.dy_ref, ...), custom_call_target="tpu_custom_call", output_to_operand_aliasing={{0}: (3, {}), {1}: (4, {}), {2}: (5, {})} | custom-call | flops 1 | bytes 1 | tf_op jit(solution)/shard_map/weight_grads/pallas_call | solution.py:414
  191.1 3.7 %all-to-all-done.3 = bf16[16,40,896]{2,1,0:T(8,128)(2,1)S(1)} async-done(((bf16[16,40,896]{2,1,0:T(8,128)(2,1)}), bf16[16,40,896]{2,1,0:T(8,128)(2,1)S(1)}, u32[]{:S(2)}, u32[]{:S(2)}) %all-to-all-start.3) | async-done | bytes 1146912 | tf_op jit(solution)/shard_map/all_to_all | solution.py:469
  (67 shorter events, 13.7 us)
Async XLA Ops:
  5.2 41.7 %all-to-all-start = ((bf16[16,40,1792]{2,1,0:T(8,128)(2,1)}), bf16[16,40,1792]{2,1,0:T(8,128)(2,1)S(1)}, u32[]{:S(2)}, u32[]{:S(2)}) async-start(bf16[16,40,1792]{2,1,0:T(8,128)(2,1)} %bitcast.31), calls=%async_computation | async-start | bytes 4587520 | tf_op jit(solution)/shard_map/all_to_all | solution.py:469
  48.3 38.4 %all-to-all-start.2 = ((bf16[16,40,1792]{2,1,0:T(8,128)(2,1)}), bf16[16,40,1792]{2,1,0:T(8,128)(2,1)}, u32[]{:S(2)}, u32[]{:S(2)}) async-start(bf16[16,40,1792]{2,1,0:T(8,128)(2,1)} %bitcast.30), calls=%async_computation.2 | async-start | bytes 4587520 | tf_op jit(solution)/shard_map/all_to_all | solution.py:469
  60.5 2.2 %collective-permute-start = (bf16[8,1,80,512]{3,2,1,0:T(8,128)(2,1)S(1)}, bf16[8,1,80,512]{3,2,1,0:T(8,128)(2,1)S(1)}, u32[]{:S(2)}, u32[]{:S(2)}) collective-permute-start(bf16[8,1,80,512]{3,2,1,0:T(8,128)(2,1)S(1)} %get-tuple-element.38), channel_id=1, source_target_pairs={{0,1},{1,0},{2,3},{3,2},{4,5},{5,4},{6,7},{7,6},{8,9},{9,8},{10,11... | collective-permute-start | bytes 1966088 | tf_op jit(solution)/shard_map/ppermute | solution.py:237
  60.6 3.0 %collective-permute-start.1 = (bf16[8,1,80,512]{3,2,1,0:T(8,128)(2,1)S(1)}, bf16[8,1,80,512]{3,2,1,0:T(8,128)(2,1)S(1)}, u32[]{:S(2)}, u32[]{:S(2)}) collective-permute-start(bf16[8,1,80,512]{3,2,1,0:T(8,128)(2,1)S(1)} %get-tuple-element.39), channel_id=1, source_target_pairs={{0,1},{1,0},{2,3},{3,2},{4,5},{5,4},{6,7},{7,6},{8,9},{9,8},{10,11... | collective-permute-start | bytes 1966088 | tf_op jit(solution)/shard_map/ppermute | solution.py:237
  61.1 3.5 %collective-permute-start.2 = (bf16[8,1,80,512]{3,2,1,0:T(8,128)(2,1)S(1)}, bf16[8,1,80,512]{3,2,1,0:T(8,128)(2,1)S(1)}, u32[]{:S(2)}, u32[]{:S(2)}) collective-permute-start(bf16[8,1,80,512]{3,2,1,0:T(8,128)(2,1)S(1)} %get-tuple-element.40), channel_id=1, source_target_pairs={{0,1},{1,0},{2,3},{3,2},{4,5},{5,4},{6,7},{7,6},{8,9},{9,8},{10,11... | collective-permute-start | bytes 1966088 | tf_op jit(solution)/shard_map/ppermute | solution.py:237
  65.0 14.9 %collective-permute-start.3 = (bf16[2,3,80,512]{3,2,1,0:T(8,128)(2,1)S(1)}, bf16[2,3,80,512]{3,2,1,0:T(8,128)(2,1)S(1)}, u32[]{:S(2)}, u32[]{:S(2)}) collective-permute-start(bf16[2,3,80,512]{3,2,1,0:T(8,128)(2,1)S(1)} %get-tuple-element.42), channel_id=1, source_target_pairs={{0,6},{1,7},{2,0},{3,1},{4,2},{5,3},{6,4},{7,5},{8,14},{9,15},{10,... | collective-permute-start | bytes 1474568 | tf_op jit(solution)/shard_map/ppermute | solution.py:237
  69.1 14.2 %collective-permute-start.4 = (bf16[2,3,80,512]{3,2,1,0:T(8,128)(2,1)S(1)}, bf16[2,3,80,512]{3,2,1,0:T(8,128)(2,1)S(1)}, u32[]{:S(2)}, u32[]{:S(2)}) collective-permute-start(bf16[2,3,80,512]{3,2,1,0:T(8,128)(2,1)S(1)} %get-tuple-element.43), channel_id=1, source_target_pairs={{0,2},{1,3},{2,4},{3,5},{4,6},{5,7},{6,0},{7,1},{8,10},{9,11},{10,... | collective-permute-start | bytes 1474568 | tf_op jit(solution)/shard_map/ppermute | solution.py:237
  83.4 11.0 %collective-permute-start.5 = (bf16[3,80,512]{2,1,0:T(8,128)(2,1)S(1)}, bf16[3,80,512]{2,1,0:T(8,128)(2,1)S(1)}, u32[]{:S(2)}, u32[]{:S(2)}) collective-permute-start(bf16[3,80,512]{2,1,0:T(8,128)(2,1)S(1)} %get-tuple-element.44), channel_id=1, source_target_pairs={{0,2},{1,3},{2,4},{3,5},{4,6},{5,7},{6,0},{7,1},{8,10},{9,11},{10,... | collective-permute-start | bytes 737288 | tf_op jit(solution)/shard_map/ppermute | solution.py:237
  83.5 10.9 %collective-permute-start.6 = (bf16[3,80,512]{2,1,0:T(8,128)(2,1)S(1)}, bf16[3,80,512]{2,1,0:T(8,128)(2,1)S(1)}, u32[]{:S(2)}, u32[]{:S(2)}) collective-permute-start(bf16[3,80,512]{2,1,0:T(8,128)(2,1)S(1)} %get-tuple-element.45), channel_id=1, source_target_pairs={{0,6},{1,7},{2,0},{3,1},{4,2},{5,3},{6,4},{7,5},{8,14},{9,15},{10,... | collective-permute-start | bytes 737288 | tf_op jit(solution)/shard_map/ppermute | solution.py:237
  94.4 4.1 %collective-permute-start.16 = (bf16[8,3,80,512]{3,2,1,0:T(8,128)(2,1)S(1)}, bf16[8,3,80,512]{3,2,1,0:T(8,128)(2,1)S(1)}, u32[]{:S(2)}, u32[]{:S(2)}) collective-permute-start(bf16[8,3,80,512]{3,2,1,0:T(8,128)(2,1)S(1)} %tie.1), channel_id=1, source_target_pairs={{0,1},{1,0},{2,3},{3,2},{4,5},{5,4},{6,7},{7,6},{8,9},{9,8},{10,11... | collective-permute-start | bytes 5898248 | tf_op jit(solution)/shard_map/ppermute | solution.py:237
  94.8 14.3 %collective-permute-start.8 = (bf16[2,3,80,512]{3,2,1,0:T(8,128)(2,1)S(1)}, bf16[2,3,80,512]{3,2,1,0:T(8,128)(2,1)S(1)}, u32[]{:S(2)}, u32[]{:S(2)}) collective-permute-start(bf16[2,3,80,512]{3,2,1,0:T(8,128)(2,1)S(1)} %swiglu.2.refs_0_), channel_id=1, source_target_pairs={{0,6},{1,7},{2,0},{3,1},{4,2},{5,3},{6,4},{7,5},{8,14},{9,15},{10,... | collective-permute-start | bytes 1474568 | tf_op jit(solution)/shard_map/ppermute | solution.py:237
  98.9 20.7 %collective-permute-start.17 = (bf16[2,3,80,512]{3,2,1,0:T(8,128)(2,1)S(1)}, bf16[2,3,80,512]{3,2,1,0:T(8,128)(2,1)S(1)}, u32[]{:S(2)}, u32[]{:S(2)}) collective-permute-start(bf16[2,3,80,512]{3,2,1,0:T(8,128)(2,1)S(1)} %get-tuple-element.51), channel_id=1, source_target_pairs={{0,6},{1,7},{2,0},{3,1},{4,2},{5,3},{6,4},{7,5},{8,14},{9,15},{10,... | collective-permute-start | bytes 1474568 | tf_op jit(solution)/shard_map/ppermute | solution.py:237
  101.5 18.2 %collective-permute-start.18 = (bf16[2,3,80,512]{3,2,1,0:T(8,128)(2,1)S(1)}, bf16[2,3,80,512]{3,2,1,0:T(8,128)(2,1)S(1)}, u32[]{:S(2)}, u32[]{:S(2)}) collective-permute-start(bf16[2,3,80,512]{3,2,1,0:T(8,128)(2,1)S(1)} %get-tuple-element.52), channel_id=1, source_target_pairs={{0,2},{1,3},{2,4},{3,5},{4,6},{5,7},{6,0},{7,1},{8,10},{9,11},{10,... | collective-permute-start | bytes 1474568 | tf_op jit(solution)/shard_map/ppermute | solution.py:237
  101.5 25.8 %collective-permute-start.7 = (bf16[2,3,80,512]{3,2,1,0:T(8,128)(2,1)S(1)}, bf16[2,3,80,512]{3,2,1,0:T(8,128)(2,1)S(1)}, u32[]{:S(2)}, u32[]{:S(2)}) collective-permute-start(bf16[2,3,80,512]{3,2,1,0:T(8,128)(2,1)S(1)} %swiglu.2.refs_0_), channel_id=1, source_target_pairs={{0,2},{1,3},{2,4},{3,5},{4,6},{5,7},{6,0},{7,1},{8,10},{9,11},{10,... | collective-permute-start | bytes 1474568 | tf_op jit(solution)/shard_map/ppermute | solution.py:237
  101.5 32.0 %collective-permute-start.11 = (bf16[2,3,80,512]{3,2,1,0:T(8,128)(2,1)S(1)}, bf16[2,3,80,512]{3,2,1,0:T(8,128)(2,1)S(1)}, u32[]{:S(2)}, u32[]{:S(2)}) collective-permute-start(bf16[2,3,80,512]{3,2,1,0:T(8,128)(2,1)S(1)} %swiglu.2.refs_0_), channel_id=1, source_target_pairs={{0,1},{1,0},{2,3},{3,2},{4,5},{5,4},{6,7},{7,6},{8,9},{9,8},{10,11... | collective-permute-start | bytes 1474568 | tf_op jit(solution)/shard_map/ppermute | solution.py:237
  109.1 18.3 %collective-permute-start.10 = (bf16[3,80,512]{2,1,0:T(8,128)(2,1)S(1)}, bf16[3,80,512]{2,1,0:T(8,128)(2,1)S(1)}, u32[]{:S(2)}, u32[]{:S(2)}) collective-permute-start(bf16[3,80,512]{2,1,0:T(8,128)(2,1)S(1)} %slice_bitcast_fusion.2), channel_id=1, source_target_pairs={{0,6},{1,7},{2,0},{3,1},{4,2},{5,3},{6,4},{7,5},{8,14},{9,15},{10,... | collective-permute-start | bytes 737288 | tf_op jit(solution)/shard_map/ppermute | solution.py:237
  119.8 12.8 %collective-permute-start.19 = (bf16[3,80,512]{2,1,0:T(8,128)(2,1)S(1)}, bf16[3,80,512]{2,1,0:T(8,128)(2,1)S(1)}, u32[]{:S(2)}, u32[]{:S(2)}) collective-permute-start(bf16[3,80,512]{2,1,0:T(8,128)(2,1)S(1)} %get-tuple-element.53), channel_id=1, source_target_pairs={{0,2},{1,3},{2,4},{3,5},{4,6},{5,7},{6,0},{7,1},{8,10},{9,11},{10,... | collective-permute-start | bytes 737288 | tf_op jit(solution)/shard_map/ppermute | solution.py:237
  120.2 12.4 %collective-permute-start.20 = (bf16[3,80,512]{2,1,0:T(8,128)(2,1)S(1)}, bf16[3,80,512]{2,1,0:T(8,128)(2,1)S(1)}, u32[]{:S(2)}, u32[]{:S(2)}) collective-permute-start(bf16[3,80,512]{2,1,0:T(8,128)(2,1)S(1)} %get-tuple-element.54), channel_id=1, source_target_pairs={{0,6},{1,7},{2,0},{3,1},{4,2},{5,3},{6,4},{7,5},{8,14},{9,15},{10,... | collective-permute-start | bytes 737288 | tf_op jit(solution)/shard_map/ppermute | solution.py:237
  127.3 9.4 %collective-permute-start.9 = (bf16[3,80,512]{2,1,0:T(8,128)(2,1)S(1)}, bf16[3,80,512]{2,1,0:T(8,128)(2,1)S(1)}, u32[]{:S(2)}, u32[]{:S(2)}) collective-permute-start(bf16[3,80,512]{2,1,0:T(8,128)(2,1)S(1)} %slice_bitcast_fusion.3), channel_id=1, source_target_pairs={{0,2},{1,3},{2,4},{3,5},{4,6},{5,7},{6,0},{7,1},{8,10},{9,11},{10,... | collective-permute-start | bytes 737288 | tf_op jit(solution)/shard_map/ppermute | solution.py:237
  127.4 9.3 %collective-permute-start.13 = (bf16[2,3,80,512]{3,2,1,0:T(8,128)(2,1)S(1)}, bf16[2,3,80,512]{3,2,1,0:T(8,128)(2,1)S(1)}, u32[]{:S(2)}, u32[]{:S(2)}) collective-permute-start(bf16[2,3,80,512]{3,2,1,0:T(8,128)(2,1)S(1)} %collective-permute-done.8.refs_2_), channel_id=1, source_target_pairs={{0,1},{1,0},{2,3},{3,2},{4,5},{5,4},{6,7},{7,6},{8,9},{9,8},{10,11... | collective-permute-start | bytes 1474568 | tf_op jit(solution)/shard_map/ppermute | solution.py:237
  132.6 5.7 %collective-permute-start.12 = (bf16[2,3,80,512]{3,2,1,0:T(8,128)(2,1)S(1)}, bf16[2,3,80,512]{3,2,1,0:T(8,128)(2,1)S(1)}, u32[]{:S(2)}, u32[]{:S(2)}) collective-permute-start(bf16[2,3,80,512]{3,2,1,0:T(8,128)(2,1)S(1)} %collective-permute-done.7.refs_1_), channel_id=1, source_target_pairs={{0,1},{1,0},{2,3},{3,2},{4,5},{5,4},{6,7},{7,6},{8,9},{9,8},{10,11... | collective-permute-start | bytes 1474568 | tf_op jit(solution)/shard_map/ppermute | solution.py:237
  132.6 4.1 %collective-permute-start.15 = (bf16[3,80,512]{2,1,0:T(8,128)(2,1)S(1)}, bf16[3,80,512]{2,1,0:T(8,128)(2,1)S(1)}, u32[]{:S(2)}, u32[]{:S(2)}) collective-permute-start(bf16[3,80,512]{2,1,0:T(8,128)(2,1)S(1)} %collective-permute-done.10.refs_4_), channel_id=1, source_target_pairs={{0,1},{1,0},{2,3},{3,2},{4,5},{5,4},{6,7},{7,6},{8,9},{9,8},{10,11... | collective-permute-start | bytes 737288 | tf_op jit(solution)/shard_map/ppermute | solution.py:237
  133.4 15.9 %collective-permute-start.22 = (bf16[2,3,80,512]{3,2,1,0:T(8,128)(2,1)S(1)}, bf16[2,3,80,512]{3,2,1,0:T(8,128)(2,1)S(1)}, u32[]{:S(2)}, u32[]{:S(2)}) collective-permute-start(bf16[2,3,80,512]{3,2,1,0:T(8,128)(2,1)S(1)} %swiglu.3.refs_0_), channel_id=1, source_target_pairs={{0,6},{1,7},{2,0},{3,1},{4,2},{5,3},{6,4},{7,5},{8,14},{9,15},{10,... | collective-permute-start | bytes 1474568 | tf_op jit(solution)/shard_map/ppermute | solution.py:237
  136.7 14.8 %collective-permute-start.21 = (bf16[2,3,80,512]{3,2,1,0:T(8,128)(2,1)S(1)}, bf16[2,3,80,512]{3,2,1,0:T(8,128)(2,1)S(1)}, u32[]{:S(2)}, u32[]{:S(2)}) collective-permute-start(bf16[2,3,80,512]{3,2,1,0:T(8,128)(2,1)S(1)} %swiglu.3.refs_0_), channel_id=1, source_target_pairs={{0,2},{1,3},{2,4},{3,5},{4,6},{5,7},{6,0},{7,1},{8,10},{9,11},{10,... | collective-permute-start | bytes 1474568 | tf_op jit(solution)/shard_map/ppermute | solution.py:237
  144.2 24.6 %all-to-all-start.1 = ((bf16[16,40,896]{2,1,0:T(8,128)(2,1)}), bf16[16,40,896]{2,1,0:T(8,128)(2,1)S(1)}, u32[]{:S(2)}, u32[]{:S(2)}) async-start(bf16[16,40,896]{2,1,0:T(8,128)(2,1)} %bitcast.32), calls=%async_computation.1 | async-start | bytes 2293760 | tf_op jit(solution)/shard_map/all_to_all | solution.py:469
  149.2 12.1 %collective-permute-start.25 = (bf16[2,3,80,512]{3,2,1,0:T(8,128)(2,1)S(1)}, bf16[2,3,80,512]{3,2,1,0:T(8,128)(2,1)S(1)}, u32[]{:S(2)}, u32[]{:S(2)}) collective-permute-start(bf16[2,3,80,512]{3,2,1,0:T(8,128)(2,1)S(1)} %swiglu.3.refs_0_), channel_id=1, source_target_pairs={{0,1},{1,0},{2,3},{3,2},{4,5},{5,4},{6,7},{7,6},{8,9},{9,8},{10,11... | collective-permute-start | bytes 1474568 | tf_op jit(solution)/shard_map/ppermute | solution.py:237
  149.3 8.4 %collective-permute-start.24 = (bf16[3,80,512]{2,1,0:T(8,128)(2,1)S(1)}, bf16[3,80,512]{2,1,0:T(8,128)(2,1)S(1)}, u32[]{:S(2)}, u32[]{:S(2)}) collective-permute-start(bf16[3,80,512]{2,1,0:T(8,128)(2,1)S(1)} %slice_bitcast_fusion), channel_id=1, source_target_pairs={{0,6},{1,7},{2,0},{3,1},{4,2},{5,3},{6,4},{7,5},{8,14},{9,15},{10,... | collective-permute-start | bytes 737288 | tf_op jit(solution)/shard_map/ppermute | solution.py:237
  151.1 10.1 %collective-permute-start.27 = (bf16[2,3,80,512]{3,2,1,0:T(8,128)(2,1)S(1)}, bf16[2,3,80,512]{3,2,1,0:T(8,128)(2,1)S(1)}, u32[]{:S(2)}, u32[]{:S(2)}) collective-permute-start(bf16[2,3,80,512]{3,2,1,0:T(8,128)(2,1)S(1)} %collective-permute-done.22.refs_2_), channel_id=1, source_target_pairs={{0,1},{1,0},{2,3},{3,2},{4,5},{5,4},{6,7},{7,6},{8,9},{9,8},{10,11... | collective-permute-start | bytes 1474568 | tf_op jit(solution)/shard_map/ppermute | solution.py:237
  151.6 9.7 %collective-permute-start.26 = (bf16[2,3,80,512]{3,2,1,0:T(8,128)(2,1)S(1)}, bf16[2,3,80,512]{3,2,1,0:T(8,128)(2,1)S(1)}, u32[]{:S(2)}, u32[]{:S(2)}) collective-permute-start(bf16[2,3,80,512]{3,2,1,0:T(8,128)(2,1)S(1)} %collective-permute-done.21.refs_1_), channel_id=1, source_target_pairs={{0,1},{1,0},{2,3},{3,2},{4,5},{5,4},{6,7},{7,6},{8,9},{9,8},{10,11... | collective-permute-start | bytes 1474568 | tf_op jit(solution)/shard_map/ppermute | solution.py:237
  151.8 9.5 %collective-permute-start.23 = (bf16[3,80,512]{2,1,0:T(8,128)(2,1)S(1)}, bf16[3,80,512]{2,1,0:T(8,128)(2,1)S(1)}, u32[]{:S(2)}, u32[]{:S(2)}) collective-permute-start(bf16[3,80,512]{2,1,0:T(8,128)(2,1)S(1)} %slice_bitcast_fusion.1), channel_id=1, source_target_pairs={{0,2},{1,3},{2,4},{3,5},{4,6},{5,7},{6,0},{7,1},{8,10},{9,11},{10,... | collective-permute-start | bytes 737288 | tf_op jit(solution)/shard_map/ppermute | solution.py:237
  157.7 3.5 %collective-permute-start.29 = (bf16[3,80,512]{2,1,0:T(8,128)(2,1)S(1)}, bf16[3,80,512]{2,1,0:T(8,128)(2,1)S(1)}, u32[]{:S(2)}, u32[]{:S(2)}) collective-permute-start(bf16[3,80,512]{2,1,0:T(8,128)(2,1)S(1)} %collective-permute-done.24.refs_4_), channel_id=1, source_target_pairs={{0,1},{1,0},{2,3},{3,2},{4,5},{5,4},{6,7},{7,6},{8,9},{9,8},{10,11... | collective-permute-start | bytes 737288 | tf_op jit(solution)/shard_map/ppermute | solution.py:237
  168.7 26.1 %all-to-all-start.3 = ((bf16[16,40,896]{2,1,0:T(8,128)(2,1)}), bf16[16,40,896]{2,1,0:T(8,128)(2,1)S(1)}, u32[]{:S(2)}, u32[]{:S(2)}) async-start(bf16[16,40,896]{2,1,0:T(8,128)(2,1)} %bitcast.33), calls=%async_computation.3 | async-start | bytes 2293760 | tf_op jit(solution)/shard_map/all_to_all | solution.py:469
  (7 other events, 20.2 us)

commit v3 on v2

--- a/solution.py
+++ b/solution.py
@@ -40,6 +40,10 @@
     c = pltpu.make_async_copy(src, dst, sems.at[i])
     c.start()
     return c
+
+
+def in_vmem(x):
+    return pltpu.with_memory_space_constraint(x, pltpu.VMEM)
 
 
 def in_hbm(x):
@@ -72,60 +76,77 @@
     )
 
 
-def pack_kernel(cols, cap, exp_local, nodes, ids_ref, gates_ref, tok_ref, grad_ref, *refs):
-    out_ref, pos_ref, out_val, sems = refs[-4:]
+def pack_kernel(cap, exp_local, nodes, ids_ref, gates_ref, tok_ref, grad_ref, *refs):
+    out_refs, pos_ref, out_val, sems = refs[-exp_local - 3 : -3], refs[-3], refs[-2], refs[-1]
     outs = []
     pos, weight = slot_map(ids_ref[...], gates_ref[...], exp_local * nodes)
     pos_ref[...] = pos
     width = tok_ref.shape[1]
     for e in range(exp_local):
-        if all(col[0] != e for col in cols):
-            continue
         sel = one_hot(pos, e, cap, exp_local, nodes)
-        sel_bf = sel.astype(BF)
-        for i, (col_e, kind) in enumerate(cols):
-            at = slice(i * width, (i + 1) * width)
-            if col_e == e and kind == 0:
-                out_val[:, at] = dot(sel_bf, tok_ref[...], NN).astype(BF)
-                outs.append(copy(out_val.at[:, at], out_ref.at[:, at], sems, i))
-            elif col_e == e:
-                scale = jnp.concatenate(
-                    [
-                        jnp.sum(
-                            sel[n * cap : (n + 1) * cap]
-                            * weight[n * exp_local + e : n * exp_local + e + 1, :],
-                            axis=1,
-                            keepdims=True,
-                        )
-                        for n in range(nodes)
-                    ],
-                    axis=0,
+        scale = jnp.concatenate(
+            [
+                jnp.sum(
+                    sel[n * cap : (n + 1) * cap]
+                    * weight[n * exp_local + e : n * exp_local + e + 1, :],
+                    axis=1,
+                    keepdims=True,
                 )
-                out_val[:, at] = (scale * dot(sel_bf, grad_ref[...], NN)).astype(BF)
-                outs.append(copy(out_val.at[:, at], out_ref.at[:, at], sems, i))
+                for n in range(nodes)
+            ],
+            axis=0,
+        )
+        sel = sel.astype(BF)
+        out_val[e, :, :width] = dot(sel, tok_ref[...], NN).astype(BF)
+        out_val[e, :, width:] = (scale * dot(sel, grad_ref[...], NN)).astype(BF)
+        outs.append(copy(out_val.at[e], out_refs[e], sems, e))
     for c in outs:
         c.wait()
 
 
-def pack(cols, cap, exp_local, nodes, ids, gates, tokens, out_grad, after):
+def pack(cap, exp_local, nodes, ids, gates, tokens, out_grad, after):
     tok, width = tokens.shape
     rows = nodes * cap
     return pl.pallas_call(
-        functools.partial(pack_kernel, cols, cap, exp_local, nodes),
-        out_shape=(
-            pltpu.HBM((rows, len(cols) * width), BF),
-            jax.ShapeDtypeStruct((exp_local * nodes, tok), F32),
-        ),
+        functools.partial(pack_kernel, cap, exp_local, nodes),
+        out_shape=tuple(pltpu.HBM((rows, 2 * width), BF) for _ in range(exp_local))
+        + (jax.ShapeDtypeStruct((exp_local * nodes, tok), F32),),
         in_specs=[VM] * 4 + [ANY] * len(after),
-        out_specs=(pl.BlockSpec(memory_space=pltpu.HBM), VM),
+        out_specs=(pl.BlockSpec(memory_space=pltpu.HBM),) * exp_local + (VM,),
         scratch_shapes=[
-            pltpu.VMEM((rows, len(cols) * width), BF),
-            pltpu.SemaphoreType.DMA((len(cols),)),
+            pltpu.VMEM((exp_local, rows, 2 * width), BF),
+            pltpu.SemaphoreType.DMA((exp_local,)),
         ],
         compiler_params=params(24),
         cost_estimate=cost(1, 1),
         name="pack",
-    )(ids.T, gates.T, in_hbm(tokens), in_hbm(out_grad), *after)
+    )(in_hbm(ids.T), in_hbm(gates.T), in_hbm(tokens), in_hbm(out_grad), *after)
+
+
+def slot_map(ids, gates, experts):
+    top, tok = ids.shape
+    row = lax.broadcasted_iota(jnp.int32, (experts, tok), 0)
+    named = jnp.zeros((experts, tok), F32)
+    weight = jnp.zeros((experts, tok), F32)
+    for k in range(top):
+        hit = ids[k : k + 1, :] == row
+        named = jnp.where(hit, 1.0, named)
+        weight = jnp.where(hit, gates[k : k + 1, :], weight)
+    at = lax.broadcasted_iota(jnp.int32, (tok, tok), 0)
+    before = (at < lax.broadcasted_iota(jnp.int32, (tok, tok), 1)).astype(BF)
+    pos = dot(named.astype(BF), before, NN)
+    return jnp.where(named > 0.0, pos, -1.0), weight
+
+
+def one_hot(pos, e, cap, exp_local, nodes):
+    slot = lax.broadcasted_iota(jnp.int32, (cap, pos.shape[1]), 0).astype(F32)
+    return jnp.concatenate(
+        [
+            (pos[n * exp_local + e : n * exp_local + e + 1, :] == slot).astype(F32)
+            for n in range(nodes)
+        ],
+        axis=0,
+    )
 
 
 def ring_slot(half, j):
@@ -134,9 +155,11 @@
     return jnp.where(j == 0, 7, jnp.where(j == 1, 1, jnp.where(j == 2, 2, 5)))
 
 
-def products_kernel(e, blk, ks, x_at, dy_at, n_after, place, x_ref, dy_ref, *refs):
+def products_kernel(e, blk, ks, x_at, dy_at, n_after, keep, place, x_ref, dy_ref, *refs):
     w_refs = refs[:3]
     own_ref, *other_refs, x, w, wd, stage, sems, out_sems = refs[3 + n_after :]
+    if keep:
+        kept_ref = other_refs.pop()
     z, core = place[0], place[1]
     rows, width = x.shape[1:]
     hh = wd.shape[1]
@@ -158,6 +181,9 @@
         for h in range(2):
             if h == 0 and k in (ks[0], 2):
                 x_in[k // 2].wait()
+                if keep:
+                    kind = slice(k // 2 * width, (k // 2 + 1) * width)
+                    outs.append(copy(x.at[k // 2], kept_ref.at[:, kind], out_sems, 6 + k // 2))
             w_in[k][h].wait()
             if k == ks[0] and h == 0:
                 for later in ks[1:]:
@@ -179,30 +205,33 @@
         c.wait()
 
 
-def products(e, blk, ks, place, x_rows, dy_rows, weights, after, pieces):
+def products(e, blk, ks, place, x_rows, dy_rows, weights, after, pieces, keep):
     (x_arr, x_at), (dy_arr, dy_at) = x_rows, dy_rows
+    at_home = in_vmem if keep else in_hbm
     rows = x_arr.shape[0]
     width, hidden = weights[0].shape[1:]
     hh = hidden // 2
     out = jax.ShapeDtypeStruct((8, 3, blk, hh), BF)
     return pl.pallas_call(
-        functools.partial(products_kernel, e, blk, ks, x_at, dy_at, len(after)),
+        functools.partial(products_kernel, e, blk, ks, x_at, dy_at, len(after), keep),
         out_shape=(out,)
-        + tuple(jax.ShapeDtypeStruct((8, 3 // pieces, blk, hh), BF) for _ in range(pieces)),
+        + tuple(jax.ShapeDtypeStruct((8, 3 // pieces, blk, hh), BF) for _ in range(pieces))
+        + ((pltpu.HBM((rows, 2 * width), BF),) if keep else ()),
         in_specs=[SM] + [ANY] * (5 + len(after)),
-        out_specs=[ANY] * (1 + pieces),
+        out_specs=[ANY] * (1 + pieces)
+        + ([pl.BlockSpec(memory_space=pltpu.HBM)] if keep else []),
         scratch_shapes=[
             pltpu.VMEM((2, rows, width), BF),
             pltpu.VMEM((2, 2, width, hh), BF),
             pltpu.VMEM((2, hh, width), BF),
             pltpu.VMEM((2, 8, 3, blk, hh), BF),
             pltpu.SemaphoreType.DMA((8,)),
-            pltpu.SemaphoreType.DMA((6,)),
+            pltpu.SemaphoreType.DMA((8,)),
         ],
         compiler_params=params(BIG),
         cost_estimate=cost(1, 1),
         name="products",
-    )(place, in_hbm(x_arr), in_hbm(dy_arr), *[in_hbm(w) for w in weights], *after)
+    )(place, at_home(x_arr), at_home(dy_arr), *[in_hbm(w) for w in weights], *after)
 
 
 def swiglu_kernel(kept_ref, rm_ref, rp_ref, sp_ref, sm_ref, *refs):
@@ -283,13 +312,15 @@
     )(own, *got)
 
 
-def sum_over_width(own, other, swap_after, last_after, pieces):
+def sum_on_ring(own, other, swap_after, pieces):
     if pieces == 1:
         other = (tie(other, *swap_after),) if swap_after else (other,)
     got = [move(piece, 0, 1) for piece in other]
     to_next, to_prev, kept = add(own, got)
-    rp = move(to_next, 1)
-    rm = move(to_prev, -1)
+    return kept, move(to_next, 1), move(to_prev, -1)
+
+
+def finish_sum(kept, rp, rm, last_after):
     add_next, add_prev = fold(kept, rp, rm, ())
     sp = move(add_next, 1)
     sm = move(add_prev, -1)
@@ -313,13 +344,15 @@
     )(x, *others)
 
 
-def gather_rows(mine):
+def forward_rows(mine):
     prev = move(mine, 1)
     nxt = move(mine, -1)
-    far0 = move(prev[0], 1)
-    far1 = move(nxt[1], -1)
-    parts = (mine, prev, nxt, far0, far1)
-    return parts + tuple(move(p, 0, 1) for p in parts)
+    return mine, prev, nxt, move(prev[0], 1), move(nxt[1], -1)
+
+
+def swap_rows(parts, far_after):
+    late = tuple(tie(p, *far_after) for p in parts[3:]) if far_after else parts[3:]
+    return parts + tuple(move(p, 0, 1) for p in parts[:3] + late)
 
 
 def place_rows(blk, z, core, parts, k, dst):
@@ -469,19 +502,25 @@
         return lax.all_to_all(x, "node", split_axis=0, concat_axis=0, tiled=True)
 
     pack_args = (cap, exp_local, nodes, expert_ids, gates, tokens, out_grad)
-    first, pos = pack(((0, 0), (0, 1)), *pack_args, (place,))
-    second, packed = pack(((1, 0), (1, 1)), *pack_args, ())
+    first, second, pos = pack(*pack_args, (place,))
     got = (exchange(first), exchange(second))
     x_rows = tuple((g, 0) for g in got)
     dy_rows = tuple((g, 1) for g in got)
 
     all_ks = (0, 1, 2)
-    own0, *other0 = products(0, blk, all_ks, place, x_rows[0], dy_rows[0], weights, (packed,), 3)
-    mine0, step2 = sum_over_width(own0, other0, (), (), 3)
-    out0, hidden0 = grad_rows(0, blk, rows, place, gather_rows(mine0), weights)
-    own1, other1 = products(1, blk, all_ks, place, x_rows[1], dy_rows[1], weights, (), 1)
-    mine1, _ = sum_over_width(own1, other1, step2, (), 1)
-    out1, hidden1 = grad_rows(1, blk, rows, place, gather_rows(mine1), weights)
+    own0, *other0, rows0 = products(
+        0, blk, all_ks, place, x_rows[0], dy_rows[0], weights, (), 3, True
+    )
+    x_rows, dy_rows = ((rows0, 0), x_rows[1]), ((rows0, 1), dy_rows[1])
+    mine0, step2 = finish_sum(*sum_on_ring(own0, other0, (), 3), ())
+    parts0 = forward_rows(mine0)
+    own1, other1 = products(1, blk, all_ks, place, x_rows[1], dy_rows[1], weights, (), 1, False)
+    ring1 = sum_on_ring(own1, other1, step2, 1)
+    parts0 = swap_rows(parts0, ())
+    out0, hidden0 = grad_rows(0, blk, rows, place, parts0, weights)
+    mine1, _ = finish_sum(*ring1, ())
+    parts1 = swap_rows(forward_rows(mine1), ())
+    out1, hidden1 = grad_rows(1, blk, rows, place, parts1, weights)
     backs = [exchange(out0), exchange(out1)]
     grads = ()
     for e, hidden_vals in enumerate((hidden0, hidden1)):

time: 197 us -> 191 us (0.970)
  blocking collectives: 0 us -> 37.6 us
  waiting for transfers between devices: 92.2 us -> 61.1 us
  starting transfers between devices: 48.1 us -> 40.6 us
  local copies, waits for them, and re-layouts: 2.92 us -> 0.07 us
    all_to_all x0 -> x1, blocking collectives: none -> 37.6 us  [exchange(): return lax.all_to_all(x, 'node', split_axis=0, concat_axis=0, tiled=True)]
    all_to_all x4 -> x3, waiting for transfers between devices: 35.2 us -> 3.73 us  [exchange(): return lax.all_to_all(x, 'node', split_axis=0, concat_axis=0, tiled=True)]
    all_to_all x4 -> x3, starting transfers between devices: 23.5 us -> 16.9 us  [exchange(): return lax.all_to_all(x, 'node', split_axis=0, concat_axis=0, tiled=True)]
    unnamed x10 -> x0, local copies, waits for them, and re-layouts: 2.85 us -> none
    pallas_call x2 -> x1, Pallas kernels: 6.14 us -> 4.12 us  [pack(): pl.pallas_call(functools.partial(pack_kernel, cap, exp_local, nodes), out...]
  transfers between devices with their start and end apart: 34 -> 33, of which waited for: 18 -> 16; matrix products, arithmetic and copies ran while one was open for 0% -> 0% of each run, Pallas kernels for 24% -> 23%
where the time goes in v3:
time: 191 us
  waiting for transfers between devices  61.1 us (32%)
  Pallas kernels  50.1 us (26%)
  starting transfers between devices  40.6 us (21%)
  blocking collectives  37.6 us (20%)
    ppermute x30, waiting for transfers between devices, move(): lax.ppermute(x, 'local', [(i, (i // 2 + dz) % 4 * 2 + (i + dcore) % 2) fo...  57.4 us
    all_to_all x1, blocking collectives, exchange(): return lax.all_to_all(x, 'node', split_axis=0, concat_axis=0, tiled=True)  37.6 us
    ppermute x30, starting transfers between devices, move(): lax.ppermute(x, 'local', [(i, (i // 2 + dz) % 4 * 2 + (i + dcore) % 2) fo...  23.7 us
    all_to_all x3, starting transfers between devices, exchange(): return lax.all_to_all(x, 'node', split_axis=0, concat_axis=0, tiled=True)  16.9 us
    pallas_call x2, Pallas kernels, products(): pl.pallas_call(functools.partial(products_kernel, e, blk, ks, x_at, dy_at...  15.7 us
    pallas_call x2, Pallas kernels, weight_grads(): pl.pallas_call(functools.partial(weight_grads_kernel, e, x_at, dy_at), ou...  15.4 us
    pallas_call x2, Pallas kernels, grad_rows(): pl.pallas_call(functools.partial(grad_rows_kernel, e, blk), out_shape=(pl...  11.9 us
    pallas_call x1, Pallas kernels, pack(): pl.pallas_call(functools.partial(pack_kernel, cap, exp_local, nodes), out...  4.12 us
  transfers between devices with their start and end apart: 33, of which 16 were waited for; matrix products, arithmetic and copies ran while one was open for 0% of the time, Pallas kernels for 23%

profile of v3, /device:TPU:0, one launch (start us, length us, event | category | flops | bytes accessed | tf_op | source)
XLA Modules:
  0.0 190.5 jit_solution(15284137972144937623)
XLA Ops:
  0.7 4.1 %pack.1 = (bf16[640,1792]{1,0:T(8,128)(2,1)}, bf16[640,1792]{1,0:T(8,128)(2,1)}, f32[32,128]{1,0:T(8,128)S(1)}) custom-call(s32[8,128]{1,0:T(8,128)} %bitcast.28, f32[8,128]{1,0:T(8,128)} %bitcast.29, bf16[128,896]{1,0:T(8,128)(2,1)} %tok_ref.1, bf16[128,896]{1,0:T(8,128)(2,1)} %grad_ref.1, s32[2]{0:T(128)S(1)} %pad_add_fusion.refs_0_.place), custom_call_target="tpu_custom_call" | custom-call | flops 1 | bytes 1 | tf_op jit(solution)/shard_map/pack/pallas_call | solution.py:110
  4.8 37.6 %all_to_all.44 = bf16[16,40,1792]{2,1,0:T(8,128)(2,1)S(1)} all-to-all(bf16[16,40,1792]{2,1,0:T(8,128)(2,1)} %bitcast.25), channel_id=1, replica_groups=mesh['node'=16,'local'=8] {'node'}, dimensions={0} | all-to-all | bytes 4587520 | tf_op jit(solution)/shard_map/all_to_all | solution.py:502
  42.5 4.5 %all-to-all-start.2 = ((bf16[16,40,1792]{2,1,0:T(8,128)(2,1)}), bf16[16,40,1792]{2,1,0:T(8,128)(2,1)}, u32[]{:S(2)}, u32[]{:S(2)}) async-start(bf16[16,40,1792]{2,1,0:T(8,128)(2,1)} %bitcast.24), calls=%async_computation.2 | async-start | bytes 4587520 | tf_op jit(solution)/shard_map/all_to_all | solution.py:502
  46.9 8.0 %products.2 = (bf16[8,3,80,512]{3,2,1,0:T(8,128)(2,1)S(1)}, bf16[8,1,80,512]{3,2,1,0:T(8,128)(2,1)S(1)}, bf16[8,1,80,512]{3,2,1,0:T(8,128)(2,1)S(1)}, bf16[8,1,8...) custom-call(s32[2]{0:T(128)S(1)} %pad_add_fusion.refs_0_.place, bf16[640,1792]{1,0:T(8,128)(2,1)S(1)} %bitcast.20, ...), custom_call_target="tpu_custom_call" | custom-call | flops 1 | bytes 1 | tf_op jit(solution)/shard_map/products/pallas_call | solution.py:215
  55.6 1.5 collective-permute-done.refs_0_
  59.4 4.1 %collective-permute-start.3 = (bf16[2,3,80,512]{3,2,1,0:T(8,128)(2,1)S(1)}, bf16[2,3,80,512]{3,2,1,0:T(8,128)(2,1)S(1)}, u32[]{:S(2)}, u32[]{:S(2)}) collective-permute-start(bf16[2,3,80,512]{3,2,1,0:T(8,128)(2,1)S(1)} %get-tuple-element.41), channel_id=1, source_target_pairs={{0,6},{1,7},{2,0},{3,1},{4,2},{5,3},{6,4},{7,5},{8,14},{9,15},{10,... | collective-permute-start | bytes 1474568 | tf_op jit(solution)/shard_map/ppermute | solution.py:266
  63.5 10.8 %collective-permute-done.3.rm_ref = bf16[2,3,80,512]{3,2,1,0:T(8,128)(2,1)S(1)} collective-permute-done((bf16[2,3,80,512]{3,2,1,0:T(8,128)(2,1)S(1)}, bf16[2,3,80,512]{3,2,1,0:T(8,128)(2,1)S(1)}, u32[]{:S(2)}, u32[]{:S(2)}) %collective-permute-start.3) | collective-permute-done | bytes 491552 | tf_op jit(solution)/shard_map/ppermute | solution.py:266
  74.3 3.4 %collective-permute-done.4.rp_ref = bf16[2,3,80,512]{3,2,1,0:T(8,128)(2,1)S(1)} collective-permute-done((bf16[2,3,80,512]{3,2,1,0:T(8,128)(2,1)S(1)}, bf16[2,3,80,512]{3,2,1,0:T(8,128)(2,1)S(1)}, u32[]{:S(2)}, u32[]{:S(2)}) %collective-permute-start.4) | collective-permute-done | bytes 491552 | tf_op jit(solution)/shard_map/ppermute | solution.py:266
  77.9 3.2 %collective-permute-start.6 = (bf16[3,80,512]{2,1,0:T(8,128)(2,1)S(1)}, bf16[3,80,512]{2,1,0:T(8,128)(2,1)S(1)}, u32[]{:S(2)}, u32[]{:S(2)}) collective-permute-start(bf16[3,80,512]{2,1,0:T(8,128)(2,1)S(1)} %get-tuple-element.44), channel_id=1, source_target_pairs={{0,6},{1,7},{2,0},{3,1},{4,2},{5,3},{6,4},{7,5},{8,14},{9,15},{10,... | collective-permute-start | bytes 737288 | tf_op jit(solution)/shard_map/ppermute | solution.py:266
  81.1 7.7 %products.3 = (bf16[8,3,80,512]{3,2,1,0:T(8,128)(2,1)S(1)}, bf16[8,3,80,512]{3,2,1,0:T(8,128)(2,1)S(1)}) custom-call(s32[2]{0:T(128)S(1)} %pad_add_fusion.refs_0_.place, bf16[640,1792]{1,0:T(8,128)(2,1)} %bitcast.11.x_ref.dy_ref, bf16[640,1792]{1,0:T(8,128)(2,1)} %bitcast.11.x_ref.dy_ref, bf16[2,896,1024]{2,1,0:T(8,128)(2,1)} %refs_10_.3, ...), custom_call_target="tpu_custom_call" | custom-call | flops 1 | bytes 1 | tf_op jit(solution)/shard_map/products/pallas_call | solution.py:215
  89.3 2.4 %collective-permute-start.8 = (bf16[2,3,80,512]{3,2,1,0:T(8,128)(2,1)S(1)}, bf16[2,3,80,512]{3,2,1,0:T(8,128)(2,1)S(1)}, u32[]{:S(2)}, u32[]{:S(2)}) collective-permute-start(bf16[2,3,80,512]{3,2,1,0:T(8,128)(2,1)S(1)} %swiglu.2.refs_0_), channel_id=1, source_target_pairs={{0,6},{1,7},{2,0},{3,1},{4,2},{5,3},{6,4},{7,5},{8,14},{9,15},{10,... | collective-permute-start | bytes 1474568 | tf_op jit(solution)/shard_map/ppermute | solution.py:266
  93.4 2.2 %collective-permute-start.17 = (bf16[2,3,80,512]{3,2,1,0:T(8,128)(2,1)S(1)}, bf16[2,3,80,512]{3,2,1,0:T(8,128)(2,1)S(1)}, u32[]{:S(2)}, u32[]{:S(2)}) collective-permute-start(bf16[2,3,80,512]{3,2,1,0:T(8,128)(2,1)S(1)} %get-tuple-element.50), channel_id=1, source_target_pairs={{0,6},{1,7},{2,0},{3,1},{4,2},{5,3},{6,4},{7,5},{8,14},{9,15},{10,... | collective-permute-start | bytes 1474568 | tf_op jit(solution)/shard_map/ppermute | solution.py:266
  95.6 7.9 %collective-permute-done.8.refs_2_ = bf16[2,3,80,512]{3,2,1,0:T(8,128)(2,1)S(1)} collective-permute-done((bf16[2,3,80,512]{3,2,1,0:T(8,128)(2,1)S(1)}, bf16[2,3,80,512]{3,2,1,0:T(8,128)(2,1)S(1)}, u32[]{:S(2)}, u32[]{:S(2)}) %collective-permute-start.8) | collective-permute-done | bytes 491552 | tf_op jit(solution)/shard_map/ppermute | solution.py:266
  103.6 3.4 %collective-permute-start.10 = (bf16[3,80,512]{2,1,0:T(8,128)(2,1)S(1)}, bf16[3,80,512]{2,1,0:T(8,128)(2,1)S(1)}, u32[]{:S(2)}, u32[]{:S(2)}) collective-permute-start(bf16[3,80,512]{2,1,0:T(8,128)(2,1)S(1)} %slice_bitcast_fusion.2), channel_id=1, source_target_pairs={{0,6},{1,7},{2,0},{3,1},{4,2},{5,3},{6,4},{7,5},{8,14},{9,15},{10,... | collective-permute-start | bytes 737288 | tf_op jit(solution)/shard_map/ppermute | solution.py:266
  107.0 7.1 %collective-permute-done.17.rm_ref = bf16[2,3,80,512]{3,2,1,0:T(8,128)(2,1)S(1)} collective-permute-done((bf16[2,3,80,512]{3,2,1,0:T(8,128)(2,1)S(1)}, bf16[2,3,80,512]{3,2,1,0:T(8,128)(2,1)S(1)}, u32[]{:S(2)}, u32[]{:S(2)}) %collective-permute-start.17) | collective-permute-done | bytes 491552 | tf_op jit(solution)/shard_map/ppermute | solution.py:266
  114.4 3.3 %collective-permute-start.20 = (bf16[3,80,512]{2,1,0:T(8,128)(2,1)S(1)}, bf16[3,80,512]{2,1,0:T(8,128)(2,1)S(1)}, u32[]{:S(2)}, u32[]{:S(2)}) collective-permute-start(bf16[3,80,512]{2,1,0:T(8,128)(2,1)S(1)} %get-tuple-element.53), channel_id=1, source_target_pairs={{0,6},{1,7},{2,0},{3,1},{4,2},{5,3},{6,4},{7,5},{8,14},{9,15},{10,... | collective-permute-start | bytes 737288 | tf_op jit(solution)/shard_map/ppermute | solution.py:266
  117.7 3.7 %collective-permute-done.7.refs_1_ = bf16[2,3,80,512]{3,2,1,0:T(8,128)(2,1)S(1)} collective-permute-done((bf16[2,3,80,512]{3,2,1,0:T(8,128)(2,1)S(1)}, bf16[2,3,80,512]{3,2,1,0:T(8,128)(2,1)S(1)}, u32[]{:S(2)}, u32[]{:S(2)}) %collective-permute-start.7) | collective-permute-done | bytes 491552 | tf_op jit(solution)/shard_map/ppermute | solution.py:266
  121.7 5.1 %collective-permute-done.19.sp_ref = bf16[3,80,512]{2,1,0:T(8,128)(2,1)S(1)} collective-permute-done((bf16[3,80,512]{2,1,0:T(8,128)(2,1)S(1)}, bf16[3,80,512]{2,1,0:T(8,128)(2,1)S(1)}, u32[]{:S(2)}, u32[]{:S(2)}) %collective-permute-start.19) | collective-permute-done | bytes 245792 | tf_op jit(solution)/shard_map/ppermute | solution.py:266
  128.0 2.9 %collective-permute-done.9.refs_3_ = bf16[3,80,512]{2,1,0:T(8,128)(2,1)S(1)} collective-permute-done((bf16[3,80,512]{2,1,0:T(8,128)(2,1)S(1)}, bf16[3,80,512]{2,1,0:T(8,128)(2,1)S(1)}, u32[]{:S(2)}, u32[]{:S(2)}) %collective-permute-start.9) | collective-permute-done | bytes 245792 | tf_op jit(solution)/shard_map/ppermute | solution.py:266
  130.9 1.5 collective-permute-done.14.refs_8_
  132.4 5.9 %grad_rows.2 = (bf16[640,896]{1,0:T(8,128)(2,1)}, bf16[3,640,1024]{2,1,0:T(8,128)(2,1)}) custom-call(s32[2]{0:T(128)S(1)} %pad_add_fusion.refs_0_.place, bf16[2,3,80,512]{3,2,1,0:T(8,128)(2,1)S(1)} %swiglu.2.refs_0_, bf16[2,3,80,512]{3,2,1,0:T(8,128)(2,1)S(1)} %collective-permute-done.7.refs_1_, bf16[2,3,80,512]{3,2,1,0:T(8,128)(2,1)S(1)} %collective-permute-done.8.refs_2_, ...), custom_call_target="tpu_custom_call" | custom-call | flops 1 | bytes 1 | tf_op jit(solution)/shard_map/grad_rows/pallas_call | solution.py:393
  138.3 5.3 %all-to-all-start.1 = ((bf16[16,40,896]{2,1,0:T(8,128)(2,1)}), bf16[16,40,896]{2,1,0:T(8,128)(2,1)S(1)}, u32[]{:S(2)}, u32[]{:S(2)}) async-start(bf16[16,40,896]{2,1,0:T(8,128)(2,1)} %bitcast.26), calls=%async_computation.1 | async-start | bytes 2293760 | tf_op jit(solution)/shard_map/all_to_all | solution.py:502
  143.8 1.8 collective-permute-start.24
  146.5 5.7 %collective-permute-done.24.refs_4_ = bf16[3,80,512]{2,1,0:T(8,128)(2,1)S(1)} collective-permute-done((bf16[3,80,512]{2,1,0:T(8,128)(2,1)S(1)}, bf16[3,80,512]{2,1,0:T(8,128)(2,1)S(1)}, u32[]{:S(2)}, u32[]{:S(2)}) %collective-permute-start.24) | collective-permute-done | bytes 245792 | tf_op jit(solution)/shard_map/ppermute | solution.py:266
  152.2 3.3 %collective-permute-done.23.refs_3_ = bf16[3,80,512]{2,1,0:T(8,128)(2,1)S(1)} collective-permute-done((bf16[3,80,512]{2,1,0:T(8,128)(2,1)S(1)}, bf16[3,80,512]{2,1,0:T(8,128)(2,1)S(1)}, u32[]{:S(2)}, u32[]{:S(2)}) %collective-permute-start.23) | collective-permute-done | bytes 245792 | tf_op jit(solution)/shard_map/ppermute | solution.py:266
  155.5 1.5 collective-permute-done.28.refs_8_
  157.0 5.9 %grad_rows.3 = (bf16[640,896]{1,0:T(8,128)(2,1)}, bf16[3,640,1024]{2,1,0:T(8,128)(2,1)}) custom-call(s32[2]{0:T(128)S(1)} %pad_add_fusion.refs_0_.place, bf16[2,3,80,512]{3,2,1,0:T(8,128)(2,1)S(1)} %swiglu.3.refs_0_, bf16[2,3,80,512]{3,2,1,0:T(8,128)(2,1)S(1)} %collective-permute-done.21.refs_1_, ...), custom_call_target="tpu_custom_call" | custom-call | flops 1 | bytes 1 | tf_op jit(solution)/shard_map/grad_rows/pallas_call | solution.py:393
  162.9 7.2 %all-to-all-start.3 = ((bf16[16,40,896]{2,1,0:T(8,128)(2,1)}), bf16[16,40,896]{2,1,0:T(8,128)(2,1)S(1)}, u32[]{:S(2)}, u32[]{:S(2)}) async-start(bf16[16,40,896]{2,1,0:T(8,128)(2,1)} %bitcast.27), calls=%async_computation.3 | async-start | bytes 2293760 | tf_op jit(solution)/shard_map/all_to_all | solution.py:502
  170.1 7.7 %weight_grads.2 = (bf16[2,896,1024]{2,1,0:T(8,128)(2,1)}, bf16[2,896,1024]{2,1,0:T(8,128)(2,1)}, bf16[2,1024,896]{2,1,0:T(8,128)(2,1)}) custom-call(bf16[640,1792]{1,0:T(8,128)(2,1)} %get-tuple-element.56.x_ref.dy_ref, bf16[640,1792]{1,0:T(8,128)(2,1)} %get-tuple-element.56.x_ref.dy_ref, bf16[3,640,1024]{2,1,0:T(8,128)(2,1)} %get-tuple-element.57.h_ref), custom_call_target="tpu_custom_call" | custom-call | flops 1 | bytes 1 | tf_op jit(solution)/shard_map/weight_grads/pallas_call | solution.py:447
  177.8 7.7 %weight_grads.3 = (bf16[2,896,1024]{2,1,0:T(8,128)(2,1)}, bf16[2,896,1024]{2,1,0:T(8,128)(2,1)}, bf16[2,1024,896]{2,1,0:T(8,128)(2,1)}) custom-call(bf16[640,1792]{1,0:T(8,128)(2,1)} %bitcast.11.x_ref.dy_ref, bf16[640,1792]{1,0:T(8,128)(2,1)} %bitcast.11.x_ref.dy_ref, ...), custom_call_target="tpu_custom_call", output_to_operand_aliasing={{0}: (3, {}), {1}: (4, {}), {2}: (5, {})} | custom-call | flops 1 | bytes 1 | tf_op jit(solution)/shard_map/weight_grads/pallas_call | solution.py:447
  185.5 3.7 %all-to-all-done.3 = bf16[16,40,896]{2,1,0:T(8,128)(2,1)S(1)} async-done(((bf16[16,40,896]{2,1,0:T(8,128)(2,1)}), bf16[16,40,896]{2,1,0:T(8,128)(2,1)S(1)}, u32[]{:S(2)}, u32[]{:S(2)}) %all-to-all-start.3) | async-done | bytes 1146912 | tf_op jit(solution)/shard_map/all_to_all | solution.py:502
  189.2 1.3 combine.1
  (55 shorter events, 8.2 us)
Async XLA Ops:
  42.5 38.7 %all-to-all-start.2 = ((bf16[16,40,1792]{2,1,0:T(8,128)(2,1)}), bf16[16,40,1792]{2,1,0:T(8,128)(2,1)}, u32[]{:S(2)}, u32[]{:S(2)}) async-start(bf16[16,40,1792]{2,1,0:T(8,128)(2,1)} %bitcast.24), calls=%async_computation.2 | async-start | bytes 4587520 | tf_op jit(solution)/shard_map/all_to_all | solution.py:502
  54.9 2.2 %collective-permute-start = (bf16[8,1,80,512]{3,2,1,0:T(8,128)(2,1)S(1)}, bf16[8,1,80,512]{3,2,1,0:T(8,128)(2,1)S(1)}, u32[]{:S(2)}, u32[]{:S(2)}) collective-permute-start(bf16[8,1,80,512]{3,2,1,0:T(8,128)(2,1)S(1)} %get-tuple-element.37), channel_id=1, source_target_pairs={{0,1},{1,0},{2,3},{3,2},{4,5},{5,4},{6,7},{7,6},{8,9},{9,8},{10,11... | collective-permute-start | bytes 1966088 | tf_op jit(solution)/shard_map/ppermute | solution.py:266
  55.0 3.0 %collective-permute-start.1 = (bf16[8,1,80,512]{3,2,1,0:T(8,128)(2,1)S(1)}, bf16[8,1,80,512]{3,2,1,0:T(8,128)(2,1)S(1)}, u32[]{:S(2)}, u32[]{:S(2)}) collective-permute-start(bf16[8,1,80,512]{3,2,1,0:T(8,128)(2,1)S(1)} %get-tuple-element.38), channel_id=1, source_target_pairs={{0,1},{1,0},{2,3},{3,2},{4,5},{5,4},{6,7},{7,6},{8,9},{9,8},{10,11... | collective-permute-start | bytes 1966088 | tf_op jit(solution)/shard_map/ppermute | solution.py:266
  55.5 3.5 %collective-permute-start.2 = (bf16[8,1,80,512]{3,2,1,0:T(8,128)(2,1)S(1)}, bf16[8,1,80,512]{3,2,1,0:T(8,128)(2,1)S(1)}, u32[]{:S(2)}, u32[]{:S(2)}) collective-permute-start(bf16[8,1,80,512]{3,2,1,0:T(8,128)(2,1)S(1)} %get-tuple-element.39), channel_id=1, source_target_pairs={{0,1},{1,0},{2,3},{3,2},{4,5},{5,4},{6,7},{7,6},{8,9},{9,8},{10,11... | collective-permute-start | bytes 1966088 | tf_op jit(solution)/shard_map/ppermute | solution.py:266
  59.4 14.9 %collective-permute-start.3 = (bf16[2,3,80,512]{3,2,1,0:T(8,128)(2,1)S(1)}, bf16[2,3,80,512]{3,2,1,0:T(8,128)(2,1)S(1)}, u32[]{:S(2)}, u32[]{:S(2)}) collective-permute-start(bf16[2,3,80,512]{3,2,1,0:T(8,128)(2,1)S(1)} %get-tuple-element.41), channel_id=1, source_target_pairs={{0,6},{1,7},{2,0},{3,1},{4,2},{5,3},{6,4},{7,5},{8,14},{9,15},{10,... | collective-permute-start | bytes 1474568 | tf_op jit(solution)/shard_map/ppermute | solution.py:266
  63.5 14.2 %collective-permute-start.4 = (bf16[2,3,80,512]{3,2,1,0:T(8,128)(2,1)S(1)}, bf16[2,3,80,512]{3,2,1,0:T(8,128)(2,1)S(1)}, u32[]{:S(2)}, u32[]{:S(2)}) collective-permute-start(bf16[2,3,80,512]{3,2,1,0:T(8,128)(2,1)S(1)} %get-tuple-element.42), channel_id=1, source_target_pairs={{0,2},{1,3},{2,4},{3,5},{4,6},{5,7},{6,0},{7,1},{8,10},{9,11},{10,... | collective-permute-start | bytes 1474568 | tf_op jit(solution)/shard_map/ppermute | solution.py:266
  77.8 11.0 %collective-permute-start.5 = (bf16[3,80,512]{2,1,0:T(8,128)(2,1)S(1)}, bf16[3,80,512]{2,1,0:T(8,128)(2,1)S(1)}, u32[]{:S(2)}, u32[]{:S(2)}) collective-permute-start(bf16[3,80,512]{2,1,0:T(8,128)(2,1)S(1)} %get-tuple-element.43), channel_id=1, source_target_pairs={{0,2},{1,3},{2,4},{3,5},{4,6},{5,7},{6,0},{7,1},{8,10},{9,11},{10,... | collective-permute-start | bytes 737288 | tf_op jit(solution)/shard_map/ppermute | solution.py:266
  77.9 10.9 %collective-permute-start.6 = (bf16[3,80,512]{2,1,0:T(8,128)(2,1)S(1)}, bf16[3,80,512]{2,1,0:T(8,128)(2,1)S(1)}, u32[]{:S(2)}, u32[]{:S(2)}) collective-permute-start(bf16[3,80,512]{2,1,0:T(8,128)(2,1)S(1)} %get-tuple-element.44), channel_id=1, source_target_pairs={{0,6},{1,7},{2,0},{3,1},{4,2},{5,3},{6,4},{7,5},{8,14},{9,15},{10,... | collective-permute-start | bytes 737288 | tf_op jit(solution)/shard_map/ppermute | solution.py:266
  88.9 4.1 %collective-permute-start.16 = (bf16[8,3,80,512]{3,2,1,0:T(8,128)(2,1)S(1)}, bf16[8,3,80,512]{3,2,1,0:T(8,128)(2,1)S(1)}, u32[]{:S(2)}, u32[]{:S(2)}) collective-permute-start(bf16[8,3,80,512]{3,2,1,0:T(8,128)(2,1)S(1)} %tie.1), channel_id=1, source_target_pairs={{0,1},{1,0},{2,3},{3,2},{4,5},{5,4},{6,7},{7,6},{8,9},{9,8},{10,11... | collective-permute-start | bytes 5898248 | tf_op jit(solution)/shard_map/ppermute | solution.py:266
  89.3 14.3 %collective-permute-start.8 = (bf16[2,3,80,512]{3,2,1,0:T(8,128)(2,1)S(1)}, bf16[2,3,80,512]{3,2,1,0:T(8,128)(2,1)S(1)}, u32[]{:S(2)}, u32[]{:S(2)}) collective-permute-start(bf16[2,3,80,512]{3,2,1,0:T(8,128)(2,1)S(1)} %swiglu.2.refs_0_), channel_id=1, source_target_pairs={{0,6},{1,7},{2,0},{3,1},{4,2},{5,3},{6,4},{7,5},{8,14},{9,15},{10,... | collective-permute-start | bytes 1474568 | tf_op jit(solution)/shard_map/ppermute | solution.py:266
  93.4 20.7 %collective-permute-start.17 = (bf16[2,3,80,512]{3,2,1,0:T(8,128)(2,1)S(1)}, bf16[2,3,80,512]{3,2,1,0:T(8,128)(2,1)S(1)}, u32[]{:S(2)}, u32[]{:S(2)}) collective-permute-start(bf16[2,3,80,512]{3,2,1,0:T(8,128)(2,1)S(1)} %get-tuple-element.50), channel_id=1, source_target_pairs={{0,6},{1,7},{2,0},{3,1},{4,2},{5,3},{6,4},{7,5},{8,14},{9,15},{10,... | collective-permute-start | bytes 1474568 | tf_op jit(solution)/shard_map/ppermute | solution.py:266
  95.6 18.5 %collective-permute-start.18 = (bf16[2,3,80,512]{3,2,1,0:T(8,128)(2,1)S(1)}, bf16[2,3,80,512]{3,2,1,0:T(8,128)(2,1)S(1)}, u32[]{:S(2)}, u32[]{:S(2)}) collective-permute-start(bf16[2,3,80,512]{3,2,1,0:T(8,128)(2,1)S(1)} %get-tuple-element.51), channel_id=1, source_target_pairs={{0,2},{1,3},{2,4},{3,5},{4,6},{5,7},{6,0},{7,1},{8,10},{9,11},{10,... | collective-permute-start | bytes 1474568 | tf_op jit(solution)/shard_map/ppermute | solution.py:266
  95.6 25.8 %collective-permute-start.7 = (bf16[2,3,80,512]{3,2,1,0:T(8,128)(2,1)S(1)}, bf16[2,3,80,512]{3,2,1,0:T(8,128)(2,1)S(1)}, u32[]{:S(2)}, u32[]{:S(2)}) collective-permute-start(bf16[2,3,80,512]{3,2,1,0:T(8,128)(2,1)S(1)} %swiglu.2.refs_0_), channel_id=1, source_target_pairs={{0,2},{1,3},{2,4},{3,5},{4,6},{5,7},{6,0},{7,1},{8,10},{9,11},{10,... | collective-permute-start | bytes 1474568 | tf_op jit(solution)/shard_map/ppermute | solution.py:266
  95.6 32.0 %collective-permute-start.11 = (bf16[2,3,80,512]{3,2,1,0:T(8,128)(2,1)S(1)}, bf16[2,3,80,512]{3,2,1,0:T(8,128)(2,1)S(1)}, u32[]{:S(2)}, u32[]{:S(2)}) collective-permute-start(bf16[2,3,80,512]{3,2,1,0:T(8,128)(2,1)S(1)} %swiglu.2.refs_0_), channel_id=1, source_target_pairs={{0,1},{1,0},{2,3},{3,2},{4,5},{5,4},{6,7},{7,6},{8,9},{9,8},{10,11... | collective-permute-start | bytes 1474568 | tf_op jit(solution)/shard_map/ppermute | solution.py:266
  103.6 18.0 %collective-permute-start.10 = (bf16[3,80,512]{2,1,0:T(8,128)(2,1)S(1)}, bf16[3,80,512]{2,1,0:T(8,128)(2,1)S(1)}, u32[]{:S(2)}, u32[]{:S(2)}) collective-permute-start(bf16[3,80,512]{2,1,0:T(8,128)(2,1)S(1)} %slice_bitcast_fusion.2), channel_id=1, source_target_pairs={{0,6},{1,7},{2,0},{3,1},{4,2},{5,3},{6,4},{7,5},{8,14},{9,15},{10,... | collective-permute-start | bytes 737288 | tf_op jit(solution)/shard_map/ppermute | solution.py:266
  114.2 12.5 %collective-permute-start.19 = (bf16[3,80,512]{2,1,0:T(8,128)(2,1)S(1)}, bf16[3,80,512]{2,1,0:T(8,128)(2,1)S(1)}, u32[]{:S(2)}, u32[]{:S(2)}) collective-permute-start(bf16[3,80,512]{2,1,0:T(8,128)(2,1)S(1)} %get-tuple-element.52), channel_id=1, source_target_pairs={{0,2},{1,3},{2,4},{3,5},{4,6},{5,7},{6,0},{7,1},{8,10},{9,11},{10,... | collective-permute-start | bytes 737288 | tf_op jit(solution)/shard_map/ppermute | solution.py:266
  114.4 12.3 %collective-permute-start.20 = (bf16[3,80,512]{2,1,0:T(8,128)(2,1)S(1)}, bf16[3,80,512]{2,1,0:T(8,128)(2,1)S(1)}, u32[]{:S(2)}, u32[]{:S(2)}) collective-permute-start(bf16[3,80,512]{2,1,0:T(8,128)(2,1)S(1)} %get-tuple-element.53), channel_id=1, source_target_pairs={{0,6},{1,7},{2,0},{3,1},{4,2},{5,3},{6,4},{7,5},{8,14},{9,15},{10,... | collective-permute-start | bytes 737288 | tf_op jit(solution)/shard_map/ppermute | solution.py:266
  121.5 9.4 %collective-permute-start.9 = (bf16[3,80,512]{2,1,0:T(8,128)(2,1)S(1)}, bf16[3,80,512]{2,1,0:T(8,128)(2,1)S(1)}, u32[]{:S(2)}, u32[]{:S(2)}) collective-permute-start(bf16[3,80,512]{2,1,0:T(8,128)(2,1)S(1)} %slice_bitcast_fusion.3), channel_id=1, source_target_pairs={{0,2},{1,3},{2,4},{3,5},{4,6},{5,7},{6,0},{7,1},{8,10},{9,11},{10,... | collective-permute-start | bytes 737288 | tf_op jit(solution)/shard_map/ppermute | solution.py:266
  121.6 9.3 %collective-permute-start.13 = (bf16[2,3,80,512]{3,2,1,0:T(8,128)(2,1)S(1)}, bf16[2,3,80,512]{3,2,1,0:T(8,128)(2,1)S(1)}, u32[]{:S(2)}, u32[]{:S(2)}) collective-permute-start(bf16[2,3,80,512]{3,2,1,0:T(8,128)(2,1)S(1)} %collective-permute-done.8.refs_2_), channel_id=1, source_target_pairs={{0,1},{1,0},{2,3},{3,2},{4,5},{5,4},{6,7},{7,6},{8,9},{9,8},{10,11... | collective-permute-start | bytes 1474568 | tf_op jit(solution)/shard_map/ppermute | solution.py:266
  126.7 5.7 %collective-permute-start.12 = (bf16[2,3,80,512]{3,2,1,0:T(8,128)(2,1)S(1)}, bf16[2,3,80,512]{3,2,1,0:T(8,128)(2,1)S(1)}, u32[]{:S(2)}, u32[]{:S(2)}) collective-permute-start(bf16[2,3,80,512]{3,2,1,0:T(8,128)(2,1)S(1)} %collective-permute-done.7.refs_1_), channel_id=1, source_target_pairs={{0,1},{1,0},{2,3},{3,2},{4,5},{5,4},{6,7},{7,6},{8,9},{9,8},{10,11... | collective-permute-start | bytes 1474568 | tf_op jit(solution)/shard_map/ppermute | solution.py:266
  126.7 4.1 %collective-permute-start.15 = (bf16[3,80,512]{2,1,0:T(8,128)(2,1)S(1)}, bf16[3,80,512]{2,1,0:T(8,128)(2,1)S(1)}, u32[]{:S(2)}, u32[]{:S(2)}) collective-permute-start(bf16[3,80,512]{2,1,0:T(8,128)(2,1)S(1)} %collective-permute-done.10.refs_4_), channel_id=1, source_target_pairs={{0,1},{1,0},{2,3},{3,2},{4,5},{5,4},{6,7},{7,6},{8,9},{9,8},{10,11... | collective-permute-start | bytes 737288 | tf_op jit(solution)/shard_map/ppermute | solution.py:266
  127.6 16.2 %collective-permute-start.22 = (bf16[2,3,80,512]{3,2,1,0:T(8,128)(2,1)S(1)}, bf16[2,3,80,512]{3,2,1,0:T(8,128)(2,1)S(1)}, u32[]{:S(2)}, u32[]{:S(2)}) collective-permute-start(bf16[2,3,80,512]{3,2,1,0:T(8,128)(2,1)S(1)} %swiglu.3.refs_0_), channel_id=1, source_target_pairs={{0,6},{1,7},{2,0},{3,1},{4,2},{5,3},{6,4},{7,5},{8,14},{9,15},{10,... | collective-permute-start | bytes 1474568 | tf_op jit(solution)/shard_map/ppermute | solution.py:266
  130.9 14.9 %collective-permute-start.21 = (bf16[2,3,80,512]{3,2,1,0:T(8,128)(2,1)S(1)}, bf16[2,3,80,512]{3,2,1,0:T(8,128)(2,1)S(1)}, u32[]{:S(2)}, u32[]{:S(2)}) collective-permute-start(bf16[2,3,80,512]{3,2,1,0:T(8,128)(2,1)S(1)} %swiglu.3.refs_0_), channel_id=1, source_target_pairs={{0,2},{1,3},{2,4},{3,5},{4,6},{5,7},{6,0},{7,1},{8,10},{9,11},{10,... | collective-permute-start | bytes 1474568 | tf_op jit(solution)/shard_map/ppermute | solution.py:266
  138.3 24.6 %all-to-all-start.1 = ((bf16[16,40,896]{2,1,0:T(8,128)(2,1)}), bf16[16,40,896]{2,1,0:T(8,128)(2,1)S(1)}, u32[]{:S(2)}, u32[]{:S(2)}) async-start(bf16[16,40,896]{2,1,0:T(8,128)(2,1)} %bitcast.26), calls=%async_computation.1 | async-start | bytes 2293760 | tf_op jit(solution)/shard_map/all_to_all | solution.py:502
  143.6 11.8 %collective-permute-start.25 = (bf16[2,3,80,512]{3,2,1,0:T(8,128)(2,1)S(1)}, bf16[2,3,80,512]{3,2,1,0:T(8,128)(2,1)S(1)}, u32[]{:S(2)}, u32[]{:S(2)}) collective-permute-start(bf16[2,3,80,512]{3,2,1,0:T(8,128)(2,1)S(1)} %swiglu.3.refs_0_), channel_id=1, source_target_pairs={{0,1},{1,0},{2,3},{3,2},{4,5},{5,4},{6,7},{7,6},{8,9},{9,8},{10,11... | collective-permute-start | bytes 1474568 | tf_op jit(solution)/shard_map/ppermute | solution.py:266
  143.8 8.4 %collective-permute-start.24 = (bf16[3,80,512]{2,1,0:T(8,128)(2,1)S(1)}, bf16[3,80,512]{2,1,0:T(8,128)(2,1)S(1)}, u32[]{:S(2)}, u32[]{:S(2)}) collective-permute-start(bf16[3,80,512]{2,1,0:T(8,128)(2,1)S(1)} %slice_bitcast_fusion), channel_id=1, source_target_pairs={{0,6},{1,7},{2,0},{3,1},{4,2},{5,3},{6,4},{7,5},{8,14},{9,15},{10,... | collective-permute-start | bytes 737288 | tf_op jit(solution)/shard_map/ppermute | solution.py:266
  145.6 9.9 %collective-permute-start.27 = (bf16[2,3,80,512]{3,2,1,0:T(8,128)(2,1)S(1)}, bf16[2,3,80,512]{3,2,1,0:T(8,128)(2,1)S(1)}, u32[]{:S(2)}, u32[]{:S(2)}) collective-permute-start(bf16[2,3,80,512]{3,2,1,0:T(8,128)(2,1)S(1)} %collective-permute-done.22.refs_2_), channel_id=1, source_target_pairs={{0,1},{1,0},{2,3},{3,2},{4,5},{5,4},{6,7},{7,6},{8,9},{9,8},{10,11... | collective-permute-start | bytes 1474568 | tf_op jit(solution)/shard_map/ppermute | solution.py:266
  145.8 9.7 %collective-permute-start.26 = (bf16[2,3,80,512]{3,2,1,0:T(8,128)(2,1)S(1)}, bf16[2,3,80,512]{3,2,1,0:T(8,128)(2,1)S(1)}, u32[]{:S(2)}, u32[]{:S(2)}) collective-permute-start(bf16[2,3,80,512]{3,2,1,0:T(8,128)(2,1)S(1)} %collective-permute-done.21.refs_1_), channel_id=1, source_target_pairs={{0,1},{1,0},{2,3},{3,2},{4,5},{5,4},{6,7},{7,6},{8,9},{9,8},{10,11... | collective-permute-start | bytes 1474568 | tf_op jit(solution)/shard_map/ppermute | solution.py:266
  146.2 9.3 %collective-permute-start.23 = (bf16[3,80,512]{2,1,0:T(8,128)(2,1)S(1)}, bf16[3,80,512]{2,1,0:T(8,128)(2,1)S(1)}, u32[]{:S(2)}, u32[]{:S(2)}) collective-permute-start(bf16[3,80,512]{2,1,0:T(8,128)(2,1)S(1)} %slice_bitcast_fusion.1), channel_id=1, source_target_pairs={{0,2},{1,3},{2,4},{3,5},{4,6},{5,7},{6,0},{7,1},{8,10},{9,11},{10,... | collective-permute-start | bytes 737288 | tf_op jit(solution)/shard_map/ppermute | solution.py:266
  152.2 3.3 %collective-permute-start.29 = (bf16[3,80,512]{2,1,0:T(8,128)(2,1)S(1)}, bf16[3,80,512]{2,1,0:T(8,128)(2,1)S(1)}, u32[]{:S(2)}, u32[]{:S(2)}) collective-permute-start(bf16[3,80,512]{2,1,0:T(8,128)(2,1)S(1)} %collective-permute-done.24.refs_4_), channel_id=1, source_target_pairs={{0,1},{1,0},{2,3},{3,2},{4,5},{5,4},{6,7},{7,6},{8,9},{9,8},{10,11... | collective-permute-start | bytes 737288 | tf_op jit(solution)/shard_map/ppermute | solution.py:266
  155.5 1.5 collective-permute-start.28
  162.9 26.3 %all-to-all-start.3 = ((bf16[16,40,896]{2,1,0:T(8,128)(2,1)}), bf16[16,40,896]{2,1,0:T(8,128)(2,1)S(1)}, u32[]{:S(2)}, u32[]{:S(2)}) async-start(bf16[16,40,896]{2,1,0:T(8,128)(2,1)} %bitcast.27), calls=%async_computation.3 | async-start | bytes 2293760 | tf_op jit(solution)/shard_map/all_to_all | solution.py:502
  (1 other events, 1.5 us)

commit v4 on v3

--- a/solution.py
+++ b/solution.py
@@ -97,9 +97,11 @@
             axis=0,
         )
         sel = sel.astype(BF)
-        out_val[e, :, :width] = dot(sel, tok_ref[...], NN).astype(BF)
-        out_val[e, :, width:] = (scale * dot(sel, grad_ref[...], NN)).astype(BF)
-        outs.append(copy(out_val.at[e], out_refs[e], sems, e))
+        for kind in range(2):
+            at = slice(kind * width, (kind + 1) * width)
+            picked = dot(sel, (tok_ref, grad_ref)[kind][...], NN)
+            out_val[e, :, at] = (picked if kind == 0 else scale * picked).astype(BF)
+            outs.append(copy(out_val.at[e, :, at], out_refs[e].at[:, at], sems, 2 * e + kind))
     for c in outs:
         c.wait()
 
@@ -115,7 +117,7 @@
         out_specs=(pl.BlockSpec(memory_space=pltpu.HBM),) * exp_local + (VM,),
         scratch_shapes=[
             pltpu.VMEM((exp_local, rows, 2 * width), BF),
-            pltpu.SemaphoreType.DMA((exp_local,)),
+            pltpu.SemaphoreType.DMA((2 * exp_local,)),
         ],
         compiler_params=params(24),
         cost_estimate=cost(1, 1),
@@ -155,57 +157,66 @@
     return jnp.where(j == 0, 7, jnp.where(j == 1, 1, jnp.where(j == 2, 2, 5)))
 
 
-def products_kernel(e, blk, ks, x_at, dy_at, n_after, keep, place, x_ref, dy_ref, *refs):
+def products_kernel(e, blk, x_at, dy_at, n_after, keep, place, x_ref, dy_ref, *refs):
     w_refs = refs[:3]
-    own_ref, *other_refs, x, w, wd, stage, sems, out_sems = refs[3 + n_after :]
+    own_ref, *other_refs, x, wg, wu, wd, stage, sems, out_sems = refs[3 + n_after :]
     if keep:
         kept_ref = other_refs.pop()
     z, core = place[0], place[1]
     rows, width = x.shape[1:]
-    hh = wd.shape[1]
+    hh = wg.shape[2]
     cols = [slice(0, hh), slice(hh, 2 * hh)]
 
     def rows_copy(kind):
         ref, at = ((x_ref, x_at), (dy_ref, dy_at))[kind]
         return copy(ref.at[:, at * width : (at + 1) * width], x.at[kind], sems, kind)
 
-    def weight_copies(k):
-        if k == 2:
-            return [copy(w_refs[2].at[e, cols[h]], wd.at[h], sems, 6 + h) for h in range(2)]
-        return [copy(w_refs[k].at[e, :, cols[h]], w.at[k, h], sems, 2 + 2 * k + h) for h in range(2)]
-
-    x_in = {ks[0] // 2: rows_copy(ks[0] // 2)}
-    w_in = {ks[0]: weight_copies(ks[0])}
+    def store(k, h, val):
+        for q in range(rows // blk):
+            slot = ring_slot(h, lax.rem(q // 2 - z + 4, 4))
+            stage[lax.rem(q + core, 2), slot, k] = val[q * blk : (q + 1) * blk]
+
+    def send(k):
+        other = other_refs[0].at[:, k] if len(other_refs) == 1 else other_refs[k].at[:, 0]
+        outs.append(copy(stage.at[1, :, k], other, out_sems, 2 * k + 1))
+        outs.append(copy(stage.at[0, :, k], own_ref.at[:, k], out_sems, 2 * k))
+
+    def keep_rows(kind):
+        if keep:
+            at = slice(kind * width, (kind + 1) * width)
+            outs.append(copy(x.at[kind], kept_ref.at[:, at], out_sems, 6 + kind))
+
     outs = []
-    for k in ks:
-        for h in range(2):
-            if h == 0 and k in (ks[0], 2):
-                x_in[k // 2].wait()
-                if keep:
-                    kind = slice(k // 2 * width, (k // 2 + 1) * width)
-                    outs.append(copy(x.at[k // 2], kept_ref.at[:, kind], out_sems, 6 + k // 2))
-            w_in[k][h].wait()
-            if k == ks[0] and h == 0:
-                for later in ks[1:]:
-                    if later == 2:
-                        x_in[1] = rows_copy(1)
-                    w_in[later] = weight_copies(later)
-            val = dot(x[k // 2], wd[h] if k == 2 else w[k, h], NT if k == 2 else NN).astype(BF)
-            for q in range(rows // blk):
-                slot = ring_slot(h, lax.rem(q // 2 - z + 4, 4))
-                stage[lax.rem(q + core, 2), slot, k] = val[q * blk : (q + 1) * blk]
-        outs.append(copy(
-            stage.at[1, :, k],
-            other_refs[0].at[:, k] if len(other_refs) == 1 else other_refs[k].at[:, 0],
-            out_sems,
-            2 * k + 1,
-        ))
-        outs.append(copy(stage.at[0, :, k], own_ref.at[:, k], out_sems, 2 * k))
+    x_in = rows_copy(0)
+    first = copy(w_refs[0].at[e, :, cols[0]], wg.at[0], sems, 2)
+    x_in.wait()
+    first.wait()
+    second = copy(w_refs[0].at[e, :, cols[1]], wg.at[1], sems, 3)
+    up_in = copy(w_refs[1].at[e], wu, sems, 4)
+    dy_in = rows_copy(1)
+    down_in = copy(w_refs[2].at[e], wd, sems, 5)
+    store(0, 0, dot(x[0], wg[0], NN).astype(BF))
+    second.wait()
+    store(0, 1, dot(x[0], wg[1], NN).astype(BF))
+    send(0)
+    up_in.wait()
+    val = dot(x[0], wu[...], NN).astype(BF)
+    for h in range(2):
+        store(1, h, val[:, cols[h]])
+    send(1)
+    keep_rows(0)
+    dy_in.wait()
+    keep_rows(1)
+    down_in.wait()
+    val = dot(x[1], wd[...], NT).astype(BF)
+    for h in range(2):
+        store(2, h, val[:, cols[h]])
+    send(2)
     for c in outs:
         c.wait()
 
 
-def products(e, blk, ks, place, x_rows, dy_rows, weights, after, pieces, keep):
+def products(e, blk, place, x_rows, dy_rows, weights, after, pieces, keep):
     (x_arr, x_at), (dy_arr, dy_at) = x_rows, dy_rows
     at_home = in_vmem if keep else in_hbm
     rows = x_arr.shape[0]
@@ -213,7 +224,7 @@
     hh = hidden // 2
     out = jax.ShapeDtypeStruct((8, 3, blk, hh), BF)
     return pl.pallas_call(
-        functools.partial(products_kernel, e, blk, ks, x_at, dy_at, len(after), keep),
+        functools.partial(products_kernel, e, blk, x_at, dy_at, len(after), keep),
         out_shape=(out,)
         + tuple(jax.ShapeDtypeStruct((8, 3 // pieces, blk, hh), BF) for _ in range(pieces))
         + ((pltpu.HBM((rows, 2 * width), BF),) if keep else ()),
@@ -222,10 +233,11 @@
         + ([pl.BlockSpec(memory_space=pltpu.HBM)] if keep else []),
         scratch_shapes=[
             pltpu.VMEM((2, rows, width), BF),
-            pltpu.VMEM((2, 2, width, hh), BF),
-            pltpu.VMEM((2, hh, width), BF),
+            pltpu.VMEM((2, width, hh), BF),
+            pltpu.VMEM((width, hidden), BF),
+            pltpu.VMEM((hidden, width), BF),
             pltpu.VMEM((2, 8, 3, blk, hh), BF),
-            pltpu.SemaphoreType.DMA((8,)),
+            pltpu.SemaphoreType.DMA((6,)),
             pltpu.SemaphoreType.DMA((8,)),
         ],
         compiler_params=params(BIG),
@@ -507,14 +519,13 @@
     x_rows = tuple((g, 0) for g in got)
     dy_rows = tuple((g, 1) for g in got)
 
-    all_ks = (0, 1, 2)
     own0, *other0, rows0 = products(
-        0, blk, all_ks, place, x_rows[0], dy_rows[0], weights, (), 3, True
+        0, blk, place, x_rows[0], dy_rows[0], weights, (), 3, True
     )
     x_rows, dy_rows = ((rows0, 0), x_rows[1]), ((rows0, 1), dy_rows[1])
     mine0, step2 = finish_sum(*sum_on_ring(own0, other0, (), 3), ())
     parts0 = forward_rows(mine0)
-    own1, other1 = products(1, blk, all_ks, place, x_rows[1], dy_rows[1], weights, (), 1, False)
+    own1, other1 = products(1, blk, place, x_rows[1], dy_rows[1], weights, (), 1, False)
     ring1 = sum_on_ring(own1, other1, step2, 1)
     parts0 = swap_rows(parts0, ())
     out0, hidden0 = grad_rows(0, blk, rows, place, parts0, weights)

time: 191 us -> 190 us (level)
  transfers between devices with their start and end apart: 33 -> 33, of which waited for: 16 -> 17; matrix products, arithmetic and copies ran while one was open for 0% -> 0% of each run, Pallas kernels for 23% -> 23%
where the time goes in v4:
time: 190 us
  waiting for transfers between devices  60.9 us (32%)
  Pallas kernels  49.2 us (26%)
  starting transfers between devices  40.8 us (21%)
  blocking collectives  37.6 us (20%)
    ppermute x30, waiting for transfers between devices, move(): lax.ppermute(x, 'local', [(i, (i // 2 + dz) % 4 * 2 + (i + dcore) % 2) fo...  57.2 us
    all_to_all x1, blocking collectives, exchange(): return lax.all_to_all(x, 'node', split_axis=0, concat_axis=0, tiled=True)  37.6 us
    ppermute x30, starting transfers between devices, move(): lax.ppermute(x, 'local', [(i, (i // 2 + dz) % 4 * 2 + (i + dcore) % 2) fo...  24.9 us
    all_to_all x3, starting transfers between devices, exchange(): return lax.all_to_all(x, 'node', split_axis=0, concat_axis=0, tiled=True)  15.9 us
    pallas_call x2, Pallas kernels, weight_grads(): pl.pallas_call(functools.partial(weight_grads_kernel, e, x_at, dy_at), ou...  15.4 us
    pallas_call x2, Pallas kernels, products(): pl.pallas_call(functools.partial(products_kernel, e, blk, x_at, dy_at, le...  15.1 us
    pallas_call x2, Pallas kernels, grad_rows(): pl.pallas_call(functools.partial(grad_rows_kernel, e, blk), out_shape=(pl...  11.9 us
    pallas_call x1, Pallas kernels, pack(): pl.pallas_call(functools.partial(pack_kernel, cap, exp_local, nodes), out...  3.88 us
  transfers between devices with their start and end apart: 33, of which 17 were waited for; matrix products, arithmetic and copies ran while one was open for 0% of the time, Pallas kernels for 23%

profile of v4, /device:TPU:0, one launch (start us, length us, event | category | flops | bytes accessed | tf_op | source)
XLA Modules:
  0.0 189.7 jit_solution(11178488004234263200)
XLA Ops:
  0.7 3.9 %pack.1 = (bf16[640,1792]{1,0:T(8,128)(2,1)}, bf16[640,1792]{1,0:T(8,128)(2,1)}, f32[32,128]{1,0:T(8,128)S(1)}) custom-call(s32[8,128]{1,0:T(8,128)} %bitcast.28, f32[8,128]{1,0:T(8,128)} %bitcast.29, bf16[128,896]{1,0:T(8,128)(2,1)} %tok_ref.1, bf16[128,896]{1,0:T(8,128)(2,1)} %grad_ref.1, s32[2]{0:T(128)S(1)} %pad_add_fusion.refs_0_.place), custom_call_target="tpu_custom_call" | custom-call | flops 1 | bytes 1 | tf_op jit(solution)/shard_map/pack/pallas_call | solution.py:112
  4.6 37.6 %all_to_all.44 = bf16[16,40,1792]{2,1,0:T(8,128)(2,1)S(1)} all-to-all(bf16[16,40,1792]{2,1,0:T(8,128)(2,1)} %bitcast.25), channel_id=1, replica_groups=mesh['node'=16,'local'=8] {'node'}, dimensions={0} | all-to-all | bytes 4587520 | tf_op jit(solution)/shard_map/all_to_all | solution.py:514
  42.2 4.5 %all-to-all-start.2 = ((bf16[16,40,1792]{2,1,0:T(8,128)(2,1)}), bf16[16,40,1792]{2,1,0:T(8,128)(2,1)}, u32[]{:S(2)}, u32[]{:S(2)}) async-start(bf16[16,40,1792]{2,1,0:T(8,128)(2,1)} %bitcast.24), calls=%async_computation.2 | async-start | bytes 4587520 | tf_op jit(solution)/shard_map/all_to_all | solution.py:514
  46.7 7.4 %products.2 = (bf16[8,3,80,512]{3,2,1,0:T(8,128)(2,1)S(1)}, bf16[8,1,80,512]{3,2,1,0:T(8,128)(2,1)S(1)}, bf16[8,1,80,512]{3,2,1,0:T(8,128)(2,1)S(1)}, bf16[8,1,8...) custom-call(s32[2]{0:T(128)S(1)} %pad_add_fusion.refs_0_.place, bf16[640,1792]{1,0:T(8,128)(2,1)S(1)} %bitcast.20, ...), custom_call_target="tpu_custom_call" | custom-call | flops 1 | bytes 1 | tf_op jit(solution)/shard_map/products/pallas_call | solution.py:226
  54.8 1.5 collective-permute-done.refs_0_
  58.6 4.1 %collective-permute-start.3 = (bf16[2,3,80,512]{3,2,1,0:T(8,128)(2,1)S(1)}, bf16[2,3,80,512]{3,2,1,0:T(8,128)(2,1)S(1)}, u32[]{:S(2)}, u32[]{:S(2)}) collective-permute-start(bf16[2,3,80,512]{3,2,1,0:T(8,128)(2,1)S(1)} %get-tuple-element.41), channel_id=1, source_target_pairs={{0,6},{1,7},{2,0},{3,1},{4,2},{5,3},{6,4},{7,5},{8,14},{9,15},{10,... | collective-permute-start | bytes 1474568 | tf_op jit(solution)/shard_map/ppermute | solution.py:278
  62.7 10.8 %collective-permute-done.3.rm_ref = bf16[2,3,80,512]{3,2,1,0:T(8,128)(2,1)S(1)} collective-permute-done((bf16[2,3,80,512]{3,2,1,0:T(8,128)(2,1)S(1)}, bf16[2,3,80,512]{3,2,1,0:T(8,128)(2,1)S(1)}, u32[]{:S(2)}, u32[]{:S(2)}) %collective-permute-start.3) | collective-permute-done | bytes 491552 | tf_op jit(solution)/shard_map/ppermute | solution.py:278
  73.5 3.4 %collective-permute-done.4.rp_ref = bf16[2,3,80,512]{3,2,1,0:T(8,128)(2,1)S(1)} collective-permute-done((bf16[2,3,80,512]{3,2,1,0:T(8,128)(2,1)S(1)}, bf16[2,3,80,512]{3,2,1,0:T(8,128)(2,1)S(1)}, u32[]{:S(2)}, u32[]{:S(2)}) %collective-permute-start.4) | collective-permute-done | bytes 491552 | tf_op jit(solution)/shard_map/ppermute | solution.py:278
  77.1 3.2 %collective-permute-start.6 = (bf16[3,80,512]{2,1,0:T(8,128)(2,1)S(1)}, bf16[3,80,512]{2,1,0:T(8,128)(2,1)S(1)}, u32[]{:S(2)}, u32[]{:S(2)}) collective-permute-start(bf16[3,80,512]{2,1,0:T(8,128)(2,1)S(1)} %get-tuple-element.44), channel_id=1, source_target_pairs={{0,6},{1,7},{2,0},{3,1},{4,2},{5,3},{6,4},{7,5},{8,14},{9,15},{10,... | collective-permute-start | bytes 737288 | tf_op jit(solution)/shard_map/ppermute | solution.py:278
  80.4 7.6 %products.3 = (bf16[8,3,80,512]{3,2,1,0:T(8,128)(2,1)S(1)}, bf16[8,3,80,512]{3,2,1,0:T(8,128)(2,1)S(1)}) custom-call(s32[2]{0:T(128)S(1)} %pad_add_fusion.refs_0_.place, bf16[640,1792]{1,0:T(8,128)(2,1)} %bitcast.11.x_ref.dy_ref, bf16[640,1792]{1,0:T(8,128)(2,1)} %bitcast.11.x_ref.dy_ref, bf16[2,896,1024]{2,1,0:T(8,128)(2,1)} %refs_10_.3, ...), custom_call_target="tpu_custom_call" | custom-call | flops 1 | bytes 1 | tf_op jit(solution)/shard_map/products/pallas_call | solution.py:226
  88.5 3.0 %collective-permute-start.8 = (bf16[2,3,80,512]{3,2,1,0:T(8,128)(2,1)S(1)}, bf16[2,3,80,512]{3,2,1,0:T(8,128)(2,1)S(1)}, u32[]{:S(2)}, u32[]{:S(2)}) collective-permute-start(bf16[2,3,80,512]{3,2,1,0:T(8,128)(2,1)S(1)} %swiglu.2.refs_0_), channel_id=1, source_target_pairs={{0,6},{1,7},{2,0},{3,1},{4,2},{5,3},{6,4},{7,5},{8,14},{9,15},{10,... | collective-permute-start | bytes 1474568 | tf_op jit(solution)/shard_map/ppermute | solution.py:278
  92.5 2.8 %collective-permute-start.17 = (bf16[2,3,80,512]{3,2,1,0:T(8,128)(2,1)S(1)}, bf16[2,3,80,512]{3,2,1,0:T(8,128)(2,1)S(1)}, u32[]{:S(2)}, u32[]{:S(2)}) collective-permute-start(bf16[2,3,80,512]{3,2,1,0:T(8,128)(2,1)S(1)} %get-tuple-element.50), channel_id=1, source_target_pairs={{0,6},{1,7},{2,0},{3,1},{4,2},{5,3},{6,4},{7,5},{8,14},{9,15},{10,... | collective-permute-start | bytes 1474568 | tf_op jit(solution)/shard_map/ppermute | solution.py:278
  95.3 7.6 %collective-permute-done.8.refs_2_ = bf16[2,3,80,512]{3,2,1,0:T(8,128)(2,1)S(1)} collective-permute-done((bf16[2,3,80,512]{3,2,1,0:T(8,128)(2,1)S(1)}, bf16[2,3,80,512]{3,2,1,0:T(8,128)(2,1)S(1)}, u32[]{:S(2)}, u32[]{:S(2)}) %collective-permute-start.8) | collective-permute-done | bytes 491552 | tf_op jit(solution)/shard_map/ppermute | solution.py:278
  103.0 3.8 %collective-permute-start.10 = (bf16[3,80,512]{2,1,0:T(8,128)(2,1)S(1)}, bf16[3,80,512]{2,1,0:T(8,128)(2,1)S(1)}, u32[]{:S(2)}, u32[]{:S(2)}) collective-permute-start(bf16[3,80,512]{2,1,0:T(8,128)(2,1)S(1)} %slice_bitcast_fusion.2), channel_id=1, source_target_pairs={{0,6},{1,7},{2,0},{3,1},{4,2},{5,3},{6,4},{7,5},{8,14},{9,15},{10,... | collective-permute-start | bytes 737288 | tf_op jit(solution)/shard_map/ppermute | solution.py:278
  106.7 6.8 %collective-permute-done.17.rm_ref = bf16[2,3,80,512]{3,2,1,0:T(8,128)(2,1)S(1)} collective-permute-done((bf16[2,3,80,512]{3,2,1,0:T(8,128)(2,1)S(1)}, bf16[2,3,80,512]{3,2,1,0:T(8,128)(2,1)S(1)}, u32[]{:S(2)}, u32[]{:S(2)}) %collective-permute-start.17) | collective-permute-done | bytes 491552 | tf_op jit(solution)/shard_map/ppermute | solution.py:278
  114.1 3.3 %collective-permute-start.20 = (bf16[3,80,512]{2,1,0:T(8,128)(2,1)S(1)}, bf16[3,80,512]{2,1,0:T(8,128)(2,1)S(1)}, u32[]{:S(2)}, u32[]{:S(2)}) collective-permute-start(bf16[3,80,512]{2,1,0:T(8,128)(2,1)S(1)} %get-tuple-element.53), channel_id=1, source_target_pairs={{0,6},{1,7},{2,0},{3,1},{4,2},{5,3},{6,4},{7,5},{8,14},{9,15},{10,... | collective-permute-start | bytes 737288 | tf_op jit(solution)/shard_map/ppermute | solution.py:278
  117.4 3.7 %collective-permute-done.7.refs_1_ = bf16[2,3,80,512]{3,2,1,0:T(8,128)(2,1)S(1)} collective-permute-done((bf16[2,3,80,512]{3,2,1,0:T(8,128)(2,1)S(1)}, bf16[2,3,80,512]{3,2,1,0:T(8,128)(2,1)S(1)}, u32[]{:S(2)}, u32[]{:S(2)}) %collective-permute-start.7) | collective-permute-done | bytes 491552 | tf_op jit(solution)/shard_map/ppermute | solution.py:278
  121.4 5.1 %collective-permute-done.19.sp_ref = bf16[3,80,512]{2,1,0:T(8,128)(2,1)S(1)} collective-permute-done((bf16[3,80,512]{2,1,0:T(8,128)(2,1)S(1)}, bf16[3,80,512]{2,1,0:T(8,128)(2,1)S(1)}, u32[]{:S(2)}, u32[]{:S(2)}) %collective-permute-start.19) | collective-permute-done | bytes 245792 | tf_op jit(solution)/shard_map/ppermute | solution.py:278
  127.7 2.9 %collective-permute-done.9.refs_3_ = bf16[3,80,512]{2,1,0:T(8,128)(2,1)S(1)} collective-permute-done((bf16[3,80,512]{2,1,0:T(8,128)(2,1)S(1)}, bf16[3,80,512]{2,1,0:T(8,128)(2,1)S(1)}, u32[]{:S(2)}, u32[]{:S(2)}) %collective-permute-start.9) | collective-permute-done | bytes 245792 | tf_op jit(solution)/shard_map/ppermute | solution.py:278
  130.6 1.5 collective-permute-done.14.refs_8_
  132.1 5.9 %grad_rows.2 = (bf16[640,896]{1,0:T(8,128)(2,1)}, bf16[3,640,1024]{2,1,0:T(8,128)(2,1)}) custom-call(s32[2]{0:T(128)S(1)} %pad_add_fusion.refs_0_.place, bf16[2,3,80,512]{3,2,1,0:T(8,128)(2,1)S(1)} %swiglu.2.refs_0_, bf16[2,3,80,512]{3,2,1,0:T(8,128)(2,1)S(1)} %collective-permute-done.7.refs_1_, bf16[2,3,80,512]{3,2,1,0:T(8,128)(2,1)S(1)} %collective-permute-done.8.refs_2_, ...), custom_call_target="tpu_custom_call" | custom-call | flops 1 | bytes 1 | tf_op jit(solution)/shard_map/grad_rows/pallas_call | solution.py:405
  138.0 4.8 %all-to-all-start.1 = ((bf16[16,40,896]{2,1,0:T(8,128)(2,1)}), bf16[16,40,896]{2,1,0:T(8,128)(2,1)S(1)}, u32[]{:S(2)}, u32[]{:S(2)}) async-start(bf16[16,40,896]{2,1,0:T(8,128)(2,1)} %bitcast.26), calls=%async_computation.1 | async-start | bytes 2293760 | tf_op jit(solution)/shard_map/all_to_all | solution.py:514
  142.9 1.8 collective-permute-start.24
  145.6 5.7 %collective-permute-done.24.refs_4_ = bf16[3,80,512]{2,1,0:T(8,128)(2,1)S(1)} collective-permute-done((bf16[3,80,512]{2,1,0:T(8,128)(2,1)S(1)}, bf16[3,80,512]{2,1,0:T(8,128)(2,1)S(1)}, u32[]{:S(2)}, u32[]{:S(2)}) %collective-permute-start.24) | collective-permute-done | bytes 245792 | tf_op jit(solution)/shard_map/ppermute | solution.py:278
  151.3 3.8 %collective-permute-done.23.refs_3_ = bf16[3,80,512]{2,1,0:T(8,128)(2,1)S(1)} collective-permute-done((bf16[3,80,512]{2,1,0:T(8,128)(2,1)S(1)}, bf16[3,80,512]{2,1,0:T(8,128)(2,1)S(1)}, u32[]{:S(2)}, u32[]{:S(2)}) %collective-permute-start.23) | collective-permute-done | bytes 245792 | tf_op jit(solution)/shard_map/ppermute | solution.py:278
  155.2 1.5 collective-permute-done.28.refs_8_
  156.6 5.9 %grad_rows.3 = (bf16[640,896]{1,0:T(8,128)(2,1)}, bf16[3,640,1024]{2,1,0:T(8,128)(2,1)}) custom-call(s32[2]{0:T(128)S(1)} %pad_add_fusion.refs_0_.place, bf16[2,3,80,512]{3,2,1,0:T(8,128)(2,1)S(1)} %swiglu.3.refs_0_, bf16[2,3,80,512]{3,2,1,0:T(8,128)(2,1)S(1)} %collective-permute-done.21.refs_1_, ...), custom_call_target="tpu_custom_call" | custom-call | flops 1 | bytes 1 | tf_op jit(solution)/shard_map/grad_rows/pallas_call | solution.py:405
  162.6 6.7 %all-to-all-start.3 = ((bf16[16,40,896]{2,1,0:T(8,128)(2,1)}), bf16[16,40,896]{2,1,0:T(8,128)(2,1)S(1)}, u32[]{:S(2)}, u32[]{:S(2)}) async-start(bf16[16,40,896]{2,1,0:T(8,128)(2,1)} %bitcast.27), calls=%async_computation.3 | async-start | bytes 2293760 | tf_op jit(solution)/shard_map/all_to_all | solution.py:514
  169.2 7.7 %weight_grads.2 = (bf16[2,896,1024]{2,1,0:T(8,128)(2,1)}, bf16[2,896,1024]{2,1,0:T(8,128)(2,1)}, bf16[2,1024,896]{2,1,0:T(8,128)(2,1)}) custom-call(bf16[640,1792]{1,0:T(8,128)(2,1)} %get-tuple-element.56.x_ref.dy_ref, bf16[640,1792]{1,0:T(8,128)(2,1)} %get-tuple-element.56.x_ref.dy_ref, bf16[3,640,1024]{2,1,0:T(8,128)(2,1)} %get-tuple-element.57.h_ref), custom_call_target="tpu_custom_call" | custom-call | flops 1 | bytes 1 | tf_op jit(solution)/shard_map/weight_grads/pallas_call | solution.py:459
  176.9 7.7 %weight_grads.3 = (bf16[2,896,1024]{2,1,0:T(8,128)(2,1)}, bf16[2,896,1024]{2,1,0:T(8,128)(2,1)}, bf16[2,1024,896]{2,1,0:T(8,128)(2,1)}) custom-call(bf16[640,1792]{1,0:T(8,128)(2,1)} %bitcast.11.x_ref.dy_ref, bf16[640,1792]{1,0:T(8,128)(2,1)} %bitcast.11.x_ref.dy_ref, ...), custom_call_target="tpu_custom_call", output_to_operand_aliasing={{0}: (3, {}), {1}: (4, {}), {2}: (5, {})} | custom-call | flops 1 | bytes 1 | tf_op jit(solution)/shard_map/weight_grads/pallas_call | solution.py:459
  184.7 3.7 %all-to-all-done.3 = bf16[16,40,896]{2,1,0:T(8,128)(2,1)S(1)} async-done(((bf16[16,40,896]{2,1,0:T(8,128)(2,1)}), bf16[16,40,896]{2,1,0:T(8,128)(2,1)S(1)}, u32[]{:S(2)}, u32[]{:S(2)}) %all-to-all-start.3) | async-done | bytes 1146912 | tf_op jit(solution)/shard_map/all_to_all | solution.py:514
  188.4 1.3 combine.1
  (55 shorter events, 7.9 us)
Async XLA Ops:
  42.2 38.1 %all-to-all-start.2 = ((bf16[16,40,1792]{2,1,0:T(8,128)(2,1)}), bf16[16,40,1792]{2,1,0:T(8,128)(2,1)}, u32[]{:S(2)}, u32[]{:S(2)}) async-start(bf16[16,40,1792]{2,1,0:T(8,128)(2,1)} %bitcast.24), calls=%async_computation.2 | async-start | bytes 4587520 | tf_op jit(solution)/shard_map/all_to_all | solution.py:514
  54.1 2.2 %collective-permute-start = (bf16[8,1,80,512]{3,2,1,0:T(8,128)(2,1)S(1)}, bf16[8,1,80,512]{3,2,1,0:T(8,128)(2,1)S(1)}, u32[]{:S(2)}, u32[]{:S(2)}) collective-permute-start(bf16[8,1,80,512]{3,2,1,0:T(8,128)(2,1)S(1)} %get-tuple-element.37), channel_id=1, source_target_pairs={{0,1},{1,0},{2,3},{3,2},{4,5},{5,4},{6,7},{7,6},{8,9},{9,8},{10,11... | collective-permute-start | bytes 1966088 | tf_op jit(solution)/shard_map/ppermute | solution.py:278
  54.2 3.0 %collective-permute-start.1 = (bf16[8,1,80,512]{3,2,1,0:T(8,128)(2,1)S(1)}, bf16[8,1,80,512]{3,2,1,0:T(8,128)(2,1)S(1)}, u32[]{:S(2)}, u32[]{:S(2)}) collective-permute-start(bf16[8,1,80,512]{3,2,1,0:T(8,128)(2,1)S(1)} %get-tuple-element.38), channel_id=1, source_target_pairs={{0,1},{1,0},{2,3},{3,2},{4,5},{5,4},{6,7},{7,6},{8,9},{9,8},{10,11... | collective-permute-start | bytes 1966088 | tf_op jit(solution)/shard_map/ppermute | solution.py:278
  54.7 3.5 %collective-permute-start.2 = (bf16[8,1,80,512]{3,2,1,0:T(8,128)(2,1)S(1)}, bf16[8,1,80,512]{3,2,1,0:T(8,128)(2,1)S(1)}, u32[]{:S(2)}, u32[]{:S(2)}) collective-permute-start(bf16[8,1,80,512]{3,2,1,0:T(8,128)(2,1)S(1)} %get-tuple-element.39), channel_id=1, source_target_pairs={{0,1},{1,0},{2,3},{3,2},{4,5},{5,4},{6,7},{7,6},{8,9},{9,8},{10,11... | collective-permute-start | bytes 1966088 | tf_op jit(solution)/shard_map/ppermute | solution.py:278
  58.6 14.9 %collective-permute-start.3 = (bf16[2,3,80,512]{3,2,1,0:T(8,128)(2,1)S(1)}, bf16[2,3,80,512]{3,2,1,0:T(8,128)(2,1)S(1)}, u32[]{:S(2)}, u32[]{:S(2)}) collective-permute-start(bf16[2,3,80,512]{3,2,1,0:T(8,128)(2,1)S(1)} %get-tuple-element.41), channel_id=1, source_target_pairs={{0,6},{1,7},{2,0},{3,1},{4,2},{5,3},{6,4},{7,5},{8,14},{9,15},{10,... | collective-permute-start | bytes 1474568 | tf_op jit(solution)/shard_map/ppermute | solution.py:278
  62.7 14.2 %collective-permute-start.4 = (bf16[2,3,80,512]{3,2,1,0:T(8,128)(2,1)S(1)}, bf16[2,3,80,512]{3,2,1,0:T(8,128)(2,1)S(1)}, u32[]{:S(2)}, u32[]{:S(2)}) collective-permute-start(bf16[2,3,80,512]{3,2,1,0:T(8,128)(2,1)S(1)} %get-tuple-element.42), channel_id=1, source_target_pairs={{0,2},{1,3},{2,4},{3,5},{4,6},{5,7},{6,0},{7,1},{8,10},{9,11},{10,... | collective-permute-start | bytes 1474568 | tf_op jit(solution)/shard_map/ppermute | solution.py:278
  77.0 11.0 %collective-permute-start.5 = (bf16[3,80,512]{2,1,0:T(8,128)(2,1)S(1)}, bf16[3,80,512]{2,1,0:T(8,128)(2,1)S(1)}, u32[]{:S(2)}, u32[]{:S(2)}) collective-permute-start(bf16[3,80,512]{2,1,0:T(8,128)(2,1)S(1)} %get-tuple-element.43), channel_id=1, source_target_pairs={{0,2},{1,3},{2,4},{3,5},{4,6},{5,7},{6,0},{7,1},{8,10},{9,11},{10,... | collective-permute-start | bytes 737288 | tf_op jit(solution)/shard_map/ppermute | solution.py:278
  77.1 10.9 %collective-permute-start.6 = (bf16[3,80,512]{2,1,0:T(8,128)(2,1)S(1)}, bf16[3,80,512]{2,1,0:T(8,128)(2,1)S(1)}, u32[]{:S(2)}, u32[]{:S(2)}) collective-permute-start(bf16[3,80,512]{2,1,0:T(8,128)(2,1)S(1)} %get-tuple-element.44), channel_id=1, source_target_pairs={{0,6},{1,7},{2,0},{3,1},{4,2},{5,3},{6,4},{7,5},{8,14},{9,15},{10,... | collective-permute-start | bytes 737288 | tf_op jit(solution)/shard_map/ppermute | solution.py:278
  88.0 4.1 %collective-permute-start.16 = (bf16[8,3,80,512]{3,2,1,0:T(8,128)(2,1)S(1)}, bf16[8,3,80,512]{3,2,1,0:T(8,128)(2,1)S(1)}, u32[]{:S(2)}, u32[]{:S(2)}) collective-permute-start(bf16[8,3,80,512]{3,2,1,0:T(8,128)(2,1)S(1)} %tie.1), channel_id=1, source_target_pairs={{0,1},{1,0},{2,3},{3,2},{4,5},{5,4},{6,7},{7,6},{8,9},{9,8},{10,11... | collective-permute-start | bytes 5898248 | tf_op jit(solution)/shard_map/ppermute | solution.py:278
  88.5 14.5 %collective-permute-start.8 = (bf16[2,3,80,512]{3,2,1,0:T(8,128)(2,1)S(1)}, bf16[2,3,80,512]{3,2,1,0:T(8,128)(2,1)S(1)}, u32[]{:S(2)}, u32[]{:S(2)}) collective-permute-start(bf16[2,3,80,512]{3,2,1,0:T(8,128)(2,1)S(1)} %swiglu.2.refs_0_), channel_id=1, source_target_pairs={{0,6},{1,7},{2,0},{3,1},{4,2},{5,3},{6,4},{7,5},{8,14},{9,15},{10,... | collective-permute-start | bytes 1474568 | tf_op jit(solution)/shard_map/ppermute | solution.py:278
  92.5 20.9 %collective-permute-start.17 = (bf16[2,3,80,512]{3,2,1,0:T(8,128)(2,1)S(1)}, bf16[2,3,80,512]{3,2,1,0:T(8,128)(2,1)S(1)}, u32[]{:S(2)}, u32[]{:S(2)}) collective-permute-start(bf16[2,3,80,512]{3,2,1,0:T(8,128)(2,1)S(1)} %get-tuple-element.50), channel_id=1, source_target_pairs={{0,6},{1,7},{2,0},{3,1},{4,2},{5,3},{6,4},{7,5},{8,14},{9,15},{10,... | collective-permute-start | bytes 1474568 | tf_op jit(solution)/shard_map/ppermute | solution.py:278
  95.3 18.2 %collective-permute-start.18 = (bf16[2,3,80,512]{3,2,1,0:T(8,128)(2,1)S(1)}, bf16[2,3,80,512]{3,2,1,0:T(8,128)(2,1)S(1)}, u32[]{:S(2)}, u32[]{:S(2)}) collective-permute-start(bf16[2,3,80,512]{3,2,1,0:T(8,128)(2,1)S(1)} %get-tuple-element.51), channel_id=1, source_target_pairs={{0,2},{1,3},{2,4},{3,5},{4,6},{5,7},{6,0},{7,1},{8,10},{9,11},{10,... | collective-permute-start | bytes 1474568 | tf_op jit(solution)/shard_map/ppermute | solution.py:278
  95.3 25.8 %collective-permute-start.7 = (bf16[2,3,80,512]{3,2,1,0:T(8,128)(2,1)S(1)}, bf16[2,3,80,512]{3,2,1,0:T(8,128)(2,1)S(1)}, u32[]{:S(2)}, u32[]{:S(2)}) collective-permute-start(bf16[2,3,80,512]{3,2,1,0:T(8,128)(2,1)S(1)} %swiglu.2.refs_0_), channel_id=1, source_target_pairs={{0,2},{1,3},{2,4},{3,5},{4,6},{5,7},{6,0},{7,1},{8,10},{9,11},{10,... | collective-permute-start | bytes 1474568 | tf_op jit(solution)/shard_map/ppermute | solution.py:278
  95.3 32.0 %collective-permute-start.11 = (bf16[2,3,80,512]{3,2,1,0:T(8,128)(2,1)S(1)}, bf16[2,3,80,512]{3,2,1,0:T(8,128)(2,1)S(1)}, u32[]{:S(2)}, u32[]{:S(2)}) collective-permute-start(bf16[2,3,80,512]{3,2,1,0:T(8,128)(2,1)S(1)} %swiglu.2.refs_0_), channel_id=1, source_target_pairs={{0,1},{1,0},{2,3},{3,2},{4,5},{5,4},{6,7},{7,6},{8,9},{9,8},{10,11... | collective-permute-start | bytes 1474568 | tf_op jit(solution)/shard_map/ppermute | solution.py:278
  103.0 18.3 %collective-permute-start.10 = (bf16[3,80,512]{2,1,0:T(8,128)(2,1)S(1)}, bf16[3,80,512]{2,1,0:T(8,128)(2,1)S(1)}, u32[]{:S(2)}, u32[]{:S(2)}) collective-permute-start(bf16[3,80,512]{2,1,0:T(8,128)(2,1)S(1)} %slice_bitcast_fusion.2), channel_id=1, source_target_pairs={{0,6},{1,7},{2,0},{3,1},{4,2},{5,3},{6,4},{7,5},{8,14},{9,15},{10,... | collective-permute-start | bytes 737288 | tf_op jit(solution)/shard_map/ppermute | solution.py:278
  113.6 12.8 %collective-permute-start.19 = (bf16[3,80,512]{2,1,0:T(8,128)(2,1)S(1)}, bf16[3,80,512]{2,1,0:T(8,128)(2,1)S(1)}, u32[]{:S(2)}, u32[]{:S(2)}) collective-permute-start(bf16[3,80,512]{2,1,0:T(8,128)(2,1)S(1)} %get-tuple-element.52), channel_id=1, source_target_pairs={{0,2},{1,3},{2,4},{3,5},{4,6},{5,7},{6,0},{7,1},{8,10},{9,11},{10,... | collective-permute-start | bytes 737288 | tf_op jit(solution)/shard_map/ppermute | solution.py:278
  114.1 12.3 %collective-permute-start.20 = (bf16[3,80,512]{2,1,0:T(8,128)(2,1)S(1)}, bf16[3,80,512]{2,1,0:T(8,128)(2,1)S(1)}, u32[]{:S(2)}, u32[]{:S(2)}) collective-permute-start(bf16[3,80,512]{2,1,0:T(8,128)(2,1)S(1)} %get-tuple-element.53), channel_id=1, source_target_pairs={{0,6},{1,7},{2,0},{3,1},{4,2},{5,3},{6,4},{7,5},{8,14},{9,15},{10,... | collective-permute-start | bytes 737288 | tf_op jit(solution)/shard_map/ppermute | solution.py:278
  121.2 9.4 %collective-permute-start.9 = (bf16[3,80,512]{2,1,0:T(8,128)(2,1)S(1)}, bf16[3,80,512]{2,1,0:T(8,128)(2,1)S(1)}, u32[]{:S(2)}, u32[]{:S(2)}) collective-permute-start(bf16[3,80,512]{2,1,0:T(8,128)(2,1)S(1)} %slice_bitcast_fusion.3), channel_id=1, source_target_pairs={{0,2},{1,3},{2,4},{3,5},{4,6},{5,7},{6,0},{7,1},{8,10},{9,11},{10,... | collective-permute-start | bytes 737288 | tf_op jit(solution)/shard_map/ppermute | solution.py:278
  121.3 9.3 %collective-permute-start.13 = (bf16[2,3,80,512]{3,2,1,0:T(8,128)(2,1)S(1)}, bf16[2,3,80,512]{3,2,1,0:T(8,128)(2,1)S(1)}, u32[]{:S(2)}, u32[]{:S(2)}) collective-permute-start(bf16[2,3,80,512]{3,2,1,0:T(8,128)(2,1)S(1)} %collective-permute-done.8.refs_2_), channel_id=1, source_target_pairs={{0,1},{1,0},{2,3},{3,2},{4,5},{5,4},{6,7},{7,6},{8,9},{9,8},{10,11... | collective-permute-start | bytes 1474568 | tf_op jit(solution)/shard_map/ppermute | solution.py:278
  126.4 5.7 %collective-permute-start.12 = (bf16[2,3,80,512]{3,2,1,0:T(8,128)(2,1)S(1)}, bf16[2,3,80,512]{3,2,1,0:T(8,128)(2,1)S(1)}, u32[]{:S(2)}, u32[]{:S(2)}) collective-permute-start(bf16[2,3,80,512]{3,2,1,0:T(8,128)(2,1)S(1)} %collective-permute-done.7.refs_1_), channel_id=1, source_target_pairs={{0,1},{1,0},{2,3},{3,2},{4,5},{5,4},{6,7},{7,6},{8,9},{9,8},{10,11... | collective-permute-start | bytes 1474568 | tf_op jit(solution)/shard_map/ppermute | solution.py:278
  126.4 4.1 %collective-permute-start.15 = (bf16[3,80,512]{2,1,0:T(8,128)(2,1)S(1)}, bf16[3,80,512]{2,1,0:T(8,128)(2,1)S(1)}, u32[]{:S(2)}, u32[]{:S(2)}) collective-permute-start(bf16[3,80,512]{2,1,0:T(8,128)(2,1)S(1)} %collective-permute-done.10.refs_4_), channel_id=1, source_target_pairs={{0,1},{1,0},{2,3},{3,2},{4,5},{5,4},{6,7},{7,6},{8,9},{9,8},{10,11... | collective-permute-start | bytes 737288 | tf_op jit(solution)/shard_map/ppermute | solution.py:278
  127.3 15.6 %collective-permute-start.22 = (bf16[2,3,80,512]{3,2,1,0:T(8,128)(2,1)S(1)}, bf16[2,3,80,512]{3,2,1,0:T(8,128)(2,1)S(1)}, u32[]{:S(2)}, u32[]{:S(2)}) collective-permute-start(bf16[2,3,80,512]{3,2,1,0:T(8,128)(2,1)S(1)} %swiglu.3.refs_0_), channel_id=1, source_target_pairs={{0,6},{1,7},{2,0},{3,1},{4,2},{5,3},{6,4},{7,5},{8,14},{9,15},{10,... | collective-permute-start | bytes 1474568 | tf_op jit(solution)/shard_map/ppermute | solution.py:278
  130.6 14.8 %collective-permute-start.21 = (bf16[2,3,80,512]{3,2,1,0:T(8,128)(2,1)S(1)}, bf16[2,3,80,512]{3,2,1,0:T(8,128)(2,1)S(1)}, u32[]{:S(2)}, u32[]{:S(2)}) collective-permute-start(bf16[2,3,80,512]{3,2,1,0:T(8,128)(2,1)S(1)} %swiglu.3.refs_0_), channel_id=1, source_target_pairs={{0,2},{1,3},{2,4},{3,5},{4,6},{5,7},{6,0},{7,1},{8,10},{9,11},{10,... | collective-permute-start | bytes 1474568 | tf_op jit(solution)/shard_map/ppermute | solution.py:278
  138.0 24.6 %all-to-all-start.1 = ((bf16[16,40,896]{2,1,0:T(8,128)(2,1)}), bf16[16,40,896]{2,1,0:T(8,128)(2,1)S(1)}, u32[]{:S(2)}, u32[]{:S(2)}) async-start(bf16[16,40,896]{2,1,0:T(8,128)(2,1)} %bitcast.26), calls=%async_computation.1 | async-start | bytes 2293760 | tf_op jit(solution)/shard_map/all_to_all | solution.py:514
  142.8 12.3 %collective-permute-start.25 = (bf16[2,3,80,512]{3,2,1,0:T(8,128)(2,1)S(1)}, bf16[2,3,80,512]{3,2,1,0:T(8,128)(2,1)S(1)}, u32[]{:S(2)}, u32[]{:S(2)}) collective-permute-start(bf16[2,3,80,512]{3,2,1,0:T(8,128)(2,1)S(1)} %swiglu.3.refs_0_), channel_id=1, source_target_pairs={{0,1},{1,0},{2,3},{3,2},{4,5},{5,4},{6,7},{7,6},{8,9},{9,8},{10,11... | collective-permute-start | bytes 1474568 | tf_op jit(solution)/shard_map/ppermute | solution.py:278
  142.9 8.4 %collective-permute-start.24 = (bf16[3,80,512]{2,1,0:T(8,128)(2,1)S(1)}, bf16[3,80,512]{2,1,0:T(8,128)(2,1)S(1)}, u32[]{:S(2)}, u32[]{:S(2)}) collective-permute-start(bf16[3,80,512]{2,1,0:T(8,128)(2,1)S(1)} %slice_bitcast_fusion), channel_id=1, source_target_pairs={{0,6},{1,7},{2,0},{3,1},{4,2},{5,3},{6,4},{7,5},{8,14},{9,15},{10,... | collective-permute-start | bytes 737288 | tf_op jit(solution)/shard_map/ppermute | solution.py:278
  144.7 10.4 %collective-permute-start.27 = (bf16[2,3,80,512]{3,2,1,0:T(8,128)(2,1)S(1)}, bf16[2,3,80,512]{3,2,1,0:T(8,128)(2,1)S(1)}, u32[]{:S(2)}, u32[]{:S(2)}) collective-permute-start(bf16[2,3,80,512]{3,2,1,0:T(8,128)(2,1)S(1)} %collective-permute-done.22.refs_2_), channel_id=1, source_target_pairs={{0,1},{1,0},{2,3},{3,2},{4,5},{5,4},{6,7},{7,6},{8,9},{9,8},{10,11... | collective-permute-start | bytes 1474568 | tf_op jit(solution)/shard_map/ppermute | solution.py:278
  145.4 9.7 %collective-permute-start.26 = (bf16[2,3,80,512]{3,2,1,0:T(8,128)(2,1)S(1)}, bf16[2,3,80,512]{3,2,1,0:T(8,128)(2,1)S(1)}, u32[]{:S(2)}, u32[]{:S(2)}) collective-permute-start(bf16[2,3,80,512]{3,2,1,0:T(8,128)(2,1)S(1)} %collective-permute-done.21.refs_1_), channel_id=1, source_target_pairs={{0,1},{1,0},{2,3},{3,2},{4,5},{5,4},{6,7},{7,6},{8,9},{9,8},{10,11... | collective-permute-start | bytes 1474568 | tf_op jit(solution)/shard_map/ppermute | solution.py:278
  145.5 9.6 %collective-permute-start.23 = (bf16[3,80,512]{2,1,0:T(8,128)(2,1)S(1)}, bf16[3,80,512]{2,1,0:T(8,128)(2,1)S(1)}, u32[]{:S(2)}, u32[]{:S(2)}) collective-permute-start(bf16[3,80,512]{2,1,0:T(8,128)(2,1)S(1)} %slice_bitcast_fusion.1), channel_id=1, source_target_pairs={{0,2},{1,3},{2,4},{3,5},{4,6},{5,7},{6,0},{7,1},{8,10},{9,11},{10,... | collective-permute-start | bytes 737288 | tf_op jit(solution)/shard_map/ppermute | solution.py:278
  151.3 3.8 %collective-permute-start.29 = (bf16[3,80,512]{2,1,0:T(8,128)(2,1)S(1)}, bf16[3,80,512]{2,1,0:T(8,128)(2,1)S(1)}, u32[]{:S(2)}, u32[]{:S(2)}) collective-permute-start(bf16[3,80,512]{2,1,0:T(8,128)(2,1)S(1)} %collective-permute-done.24.refs_4_), channel_id=1, source_target_pairs={{0,1},{1,0},{2,3},{3,2},{4,5},{5,4},{6,7},{7,6},{8,9},{9,8},{10,11... | collective-permute-start | bytes 737288 | tf_op jit(solution)/shard_map/ppermute | solution.py:278
  155.1 1.5 collective-permute-start.28
  162.6 25.8 %all-to-all-start.3 = ((bf16[16,40,896]{2,1,0:T(8,128)(2,1)}), bf16[16,40,896]{2,1,0:T(8,128)(2,1)S(1)}, u32[]{:S(2)}, u32[]{:S(2)}) async-start(bf16[16,40,896]{2,1,0:T(8,128)(2,1)} %bitcast.27), calls=%async_computation.3 | async-start | bytes 2293760 | tf_op jit(solution)/shard_map/all_to_all | solution.py:514
  (1 other events, 1.5 us)

commit v5 on v4

--- a/solution.py
+++ b/solution.py
@@ -246,20 +246,48 @@
     )(place, at_home(x_arr), at_home(dy_arr), *[in_hbm(w) for w in weights], *after)
 
 
+def write_hidden(out_ref, half, totals):
+    gate, up, gh = totals
+    sig = jax.nn.sigmoid(gate)
+    act = gate * sig
+    out_ref[half, 0] = (act * up).astype(BF)
+    out_ref[half, 1] = (gh * up * sig * (1.0 + gate * (1.0 - sig))).astype(BF)
+    out_ref[half, 2] = (gh * act).astype(BF)
+
+
 def swiglu_kernel(kept_ref, rm_ref, rp_ref, sp_ref, sm_ref, *refs):
-    out_ref = refs[-1]
     for half, (direct, ringed) in enumerate(((rm_ref, sp_ref), (rp_ref, sm_ref))):
-        gate, up, gh = [
+        totals = [
             kept_ref[2 + half, k].astype(F32)
             + direct[1, k].astype(F32)
             + ringed[k].astype(F32)
             for k in range(3)
         ]
-        sig = jax.nn.sigmoid(gate)
-        act = gate * sig
-        out_ref[half, 0] = (act * up).astype(BF)
-        out_ref[half, 1] = (gh * up * sig * (1.0 + gate * (1.0 - sig))).astype(BF)
-        out_ref[half, 2] = (gh * act).astype(BF)
+        write_hidden(refs[-1], half, totals)
+
+
+def swiglu_direct_kernel(own_ref, *refs):
+    for half in range(2):
+        totals = [own_ref[half, k].astype(F32) for k in range(3)]
+        for ref in refs[:-1]:
+            totals = [t + ref[half, k].astype(F32) for k, t in enumerate(totals)]
+        write_hidden(refs[-1], half, totals)
+
+
+def sum_directly(own, other):
+    got = [move(piece, 0, 1) for piece in other]
+    *sent, mine = add(DIRECT, own, got)
+    came = tuple(move(x, dz) for x, dz in zip(sent, (1, -1, 2)))
+    out = pl.pallas_call(
+        swiglu_direct_kernel,
+        out_shape=jax.ShapeDtypeStruct(mine.shape, BF),
+        in_specs=[VM] * 4,
+        out_specs=VM,
+        compiler_params=params(24),
+        cost_estimate=cost(1, 1),
+        name="swiglu",
+    )(mine, *came)
+    return out, came
 
 
 def swiglu(kept, rm, rp, sp, sm, after):
@@ -299,25 +327,24 @@
     )(kept, rp, rm, *after)
 
 
-def add_kernel(pieces, own_ref, *refs):
+RING = ((0, 1), (2, 3), (4, 5, 6, 7))
+DIRECT = ((4, 1), (3, 5), (0, 2), (6, 7))
+
+
+def add_kernel(groups, pieces, own_ref, *refs):
     got_refs = refs[:pieces]
-    outs = refs[pieces:]
-    for out_ref, at in zip(outs, (0, 2, 4)):
-        n = out_ref.shape[0]
-        if pieces == 1:
-            got = got_refs[0][at : at + n].astype(F32)
-            out_ref[...] = (own_ref[at : at + n].astype(F32) + got).astype(BF)
-        else:
+    for out_ref, slots in zip(refs[pieces:], groups):
+        for i, slot in enumerate(slots):
             for k in range(3):
-                got = got_refs[k][at : at + n, 0].astype(F32)
-                out_ref[:, k] = (own_ref[at : at + n, k].astype(F32) + got).astype(BF)
-
-
-def add(own, got):
+                got = got_refs[0][slot, k] if pieces == 1 else got_refs[k][slot, 0]
+                out_ref[i, k] = (own_ref[slot, k].astype(F32) + got.astype(F32)).astype(BF)
+
+
+def add(groups, own, got):
     tail = own.shape[1:]
     return pl.pallas_call(
-        functools.partial(add_kernel, len(got)),
-        out_shape=tuple(jax.ShapeDtypeStruct((n,) + tail, BF) for n in (2, 2, 4)),
+        functools.partial(add_kernel, groups, len(got)),
+        out_shape=tuple(jax.ShapeDtypeStruct((len(g),) + tail, BF) for g in groups),
         compiler_params=params(24),
         cost_estimate=cost(1, 1),
         name="add",
@@ -328,7 +355,7 @@
     if pieces == 1:
         other = (tie(other, *swap_after),) if swap_after else (other,)
     got = [move(piece, 0, 1) for piece in other]
-    to_next, to_prev, kept = add(own, got)
+    to_next, to_prev, kept = add(RING, own, got)
     return kept, move(to_next, 1), move(to_prev, -1)
 
 
@@ -523,7 +550,7 @@
         0, blk, place, x_rows[0], dy_rows[0], weights, (), 3, True
     )
     x_rows, dy_rows = ((rows0, 0), x_rows[1]), ((rows0, 1), dy_rows[1])
-    mine0, step2 = finish_sum(*sum_on_ring(own0, other0, (), 3), ())
+    mine0, step2 = sum_directly(own0, other0)
     parts0 = forward_rows(mine0)
     own1, other1 = products(1, blk, place, x_rows[1], dy_rows[1], weights, (), 1, False)
     ring1 = sum_on_ring(own1, other1, step2, 1)

time: 190 us -> 190 us (level)
    ppermute x30 -> x29, waiting for transfers between devices: 57.2 us -> 42.6 us  [move(): lax.ppermute(x, 'local', [(i, (i // 2 + dz) % 4 * 2 + (i + dcore) % 2) fo...]
    all_to_all x3, waiting for transfers between devices: 3.74 us -> 17.5 us  [exchange(): return lax.all_to_all(x, 'node', split_axis=0, concat_axis=0, tiled=True)]
    ppermute x30 -> x29, starting transfers between devices: 24.9 us -> 25.2 us  [move(): lax.ppermute(x, 'local', [(i, (i // 2 + dz) % 4 * 2 + (i + dcore) % 2) fo...]
  transfers between devices with their start and end apart: 33 -> 32, of which waited for: 17 -> 16; matrix products, arithmetic and copies ran while one was open for 0% -> 0% of each run, Pallas kernels for 23% -> 24%
where the time goes in v5:
time: 190 us
  waiting for transfers between devices  60.1 us (32%)
  Pallas kernels  49.9 us (26%)
  starting transfers between devices  40.9 us (22%)
  blocking collectives  37.6 us (20%)
    ppermute x29, waiting for transfers between devices, move(): lax.ppermute(x, 'local', [(i, (i // 2 + dz) % 4 * 2 + (i + dcore) % 2) fo...  42.6 us
    all_to_all x1, blocking collectives, exchange(): return lax.all_to_all(x, 'node', split_axis=0, concat_axis=0, tiled=True)  37.6 us
    ppermute x29, starting transfers between devices, move(): lax.ppermute(x, 'local', [(i, (i // 2 + dz) % 4 * 2 + (i + dcore) % 2) fo...  25.2 us
    all_to_all x3, waiting for transfers between devices, exchange(): return lax.all_to_all(x, 'node', split_axis=0, concat_axis=0, tiled=True)  17.5 us
    all_to_all x3, starting transfers between devices, exchange(): return lax.all_to_all(x, 'node', split_axis=0, concat_axis=0, tiled=True)  15.6 us
    pallas_call x2, Pallas kernels, weight_grads(): pl.pallas_call(functools.partial(weight_grads_kernel, e, x_at, dy_at), ou...  15.4 us
    pallas_call x2, Pallas kernels, products(): pl.pallas_call(functools.partial(products_kernel, e, blk, x_at, dy_at, le...  15.1 us
    pallas_call x2, Pallas kernels, grad_rows(): pl.pallas_call(functools.partial(grad_rows_kernel, e, blk), out_shape=(pl...  11.9 us
  transfers between devices with their start and end apart: 32, of which 16 were waited for; matrix products, arithmetic and copies ran while one was open for 0% of the time, Pallas kernels for 24%

profile of v5, /device:TPU:0, one launch (start us, length us, event | category | flops | bytes accessed | tf_op | source)
XLA Modules:
  0.0 189.6 jit_solution(12395979971269634302)
XLA Ops:
  0.7 3.9 %pack.1 = (bf16[640,1792]{1,0:T(8,128)(2,1)}, bf16[640,1792]{1,0:T(8,128)(2,1)}, f32[32,128]{1,0:T(8,128)S(1)}) custom-call(s32[8,128]{1,0:T(8,128)} %bitcast.28, f32[8,128]{1,0:T(8,128)} %bitcast.29, bf16[128,896]{1,0:T(8,128)(2,1)} %tok_ref.1, bf16[128,896]{1,0:T(8,128)(2,1)} %grad_ref.1, s32[2]{0:T(128)S(1)} %pad_add_fusion.refs_0_.place), custom_call_target="tpu_custom_call" | custom-call | flops 1 | bytes 1 | tf_op jit(solution)/shard_map/pack/pallas_call | solution.py:112
  4.6 37.6 %all_to_all.44 = bf16[16,40,1792]{2,1,0:T(8,128)(2,1)S(1)} all-to-all(bf16[16,40,1792]{2,1,0:T(8,128)(2,1)} %bitcast.25), channel_id=1, replica_groups=mesh['node'=16,'local'=8] {'node'}, dimensions={0} | all-to-all | bytes 4587520 | tf_op jit(solution)/shard_map/all_to_all | solution.py:541
  42.2 4.4 %all-to-all-start.2 = ((bf16[16,40,1792]{2,1,0:T(8,128)(2,1)}), bf16[16,40,1792]{2,1,0:T(8,128)(2,1)}, u32[]{:S(2)}, u32[]{:S(2)}) async-start(bf16[16,40,1792]{2,1,0:T(8,128)(2,1)} %bitcast.24), calls=%async_computation.2 | async-start | bytes 4587520 | tf_op jit(solution)/shard_map/all_to_all | solution.py:541
  46.7 7.4 %products.2 = (bf16[8,3,80,512]{3,2,1,0:T(8,128)(2,1)S(1)}, bf16[8,1,80,512]{3,2,1,0:T(8,128)(2,1)S(1)}, bf16[8,1,80,512]{3,2,1,0:T(8,128)(2,1)S(1)}, bf16[8,1,8...) custom-call(s32[2]{0:T(128)S(1)} %pad_add_fusion.refs_0_.place, bf16[640,1792]{1,0:T(8,128)(2,1)S(1)} %bitcast.20, ...), custom_call_target="tpu_custom_call" | custom-call | flops 1 | bytes 1 | tf_op jit(solution)/shard_map/products/pallas_call | solution.py:226
  54.8 1.5 collective-permute-done.refs_0_
  59.3 1.9 %collective-permute-start.3 = (bf16[2,3,80,512]{3,2,1,0:T(8,128)(2,1)}, bf16[2,3,80,512]{3,2,1,0:T(8,128)(2,1)S(1)}, u32[]{:S(2)}, u32[]{:S(2)}) collective-permute-start(bf16[2,3,80,512]{3,2,1,0:T(8,128)(2,1)} %get-tuple-element.40), channel_id=1, source_target_pairs={{0,2},{1,3},{2,4},{3,5},{4,6},{5,7},{6,0},{7,1},{8,10},{9,11},{10,... | collective-permute-start | bytes 1474568 | tf_op jit(solution)/shard_map/ppermute | solution.py:306
  61.2 2.1 %collective-permute-start.4 = (bf16[2,3,80,512]{3,2,1,0:T(8,128)(2,1)S(1)}, bf16[2,3,80,512]{3,2,1,0:T(8,128)(2,1)S(1)}, u32[]{:S(2)}, u32[]{:S(2)}) collective-permute-start(bf16[2,3,80,512]{3,2,1,0:T(8,128)(2,1)S(1)} %get-tuple-element.41), channel_id=1, source_target_pairs={{0,6},{1,7},{2,0},{3,1},{4,2},{5,3},{6,4},{7,5},{8,14},{9,15},{10,... | collective-permute-start | bytes 1474568 | tf_op jit(solution)/shard_map/ppermute | solution.py:306
  63.4 1.9 collective-permute-start.5
  65.2 13.8 %all-to-all-done.2 = bf16[16,40,1792]{2,1,0:T(8,128)(2,1)} async-done(((bf16[16,40,1792]{2,1,0:T(8,128)(2,1)}), bf16[16,40,1792]{2,1,0:T(8,128)(2,1)}, u32[]{:S(2)}, u32[]{:S(2)}) %all-to-all-start.2) | async-done | bytes 2293792 | tf_op jit(solution)/shard_map/all_to_all | solution.py:541
  79.0 7.6 %products.3 = (bf16[8,3,80,512]{3,2,1,0:T(8,128)(2,1)S(1)}, bf16[8,3,80,512]{3,2,1,0:T(8,128)(2,1)S(1)}) custom-call(s32[2]{0:T(128)S(1)} %pad_add_fusion.refs_0_.place, bf16[640,1792]{1,0:T(8,128)(2,1)} %bitcast.11.x_ref.dy_ref, bf16[640,1792]{1,0:T(8,128)(2,1)} %bitcast.11.x_ref.dy_ref, bf16[2,896,1024]{2,1,0:T(8,128)(2,1)} %refs_10_.3, ...), custom_call_target="tpu_custom_call" | custom-call | flops 1 | bytes 1 | tf_op jit(solution)/shard_map/products/pallas_call | solution.py:226
  87.2 4.1 %collective-permute-start.7 = (bf16[2,3,80,512]{3,2,1,0:T(8,128)(2,1)S(1)}, bf16[2,3,80,512]{3,2,1,0:T(8,128)(2,1)S(1)}, u32[]{:S(2)}, u32[]{:S(2)}) collective-permute-start(bf16[2,3,80,512]{3,2,1,0:T(8,128)(2,1)S(1)} %swiglu.2.refs_0_), channel_id=1, source_target_pairs={{0,6},{1,7},{2,0},{3,1},{4,2},{5,3},{6,4},{7,5},{8,14},{9,15},{10,... | collective-permute-start | bytes 1474568 | tf_op jit(solution)/shard_map/ppermute | solution.py:306
  91.8 3.6 %collective-permute-start.16 = (bf16[2,3,80,512]{3,2,1,0:T(8,128)(2,1)S(1)}, bf16[2,3,80,512]{3,2,1,0:T(8,128)(2,1)S(1)}, u32[]{:S(2)}, u32[]{:S(2)}) collective-permute-start(bf16[2,3,80,512]{3,2,1,0:T(8,128)(2,1)S(1)} %get-tuple-element.48), channel_id=1, source_target_pairs={{0,6},{1,7},{2,0},{3,1},{4,2},{5,3},{6,4},{7,5},{8,14},{9,15},{10,... | collective-permute-start | bytes 1474568 | tf_op jit(solution)/shard_map/ppermute | solution.py:306
  95.4 7.4 %collective-permute-done.7.refs_2_ = bf16[2,3,80,512]{3,2,1,0:T(8,128)(2,1)S(1)} collective-permute-done((bf16[2,3,80,512]{3,2,1,0:T(8,128)(2,1)S(1)}, bf16[2,3,80,512]{3,2,1,0:T(8,128)(2,1)S(1)}, u32[]{:S(2)}, u32[]{:S(2)}) %collective-permute-start.7) | collective-permute-done | bytes 491552 | tf_op jit(solution)/shard_map/ppermute | solution.py:306
  102.9 3.8 %collective-permute-start.9 = (bf16[3,80,512]{2,1,0:T(8,128)(2,1)S(1)}, bf16[3,80,512]{2,1,0:T(8,128)(2,1)S(1)}, u32[]{:S(2)}, u32[]{:S(2)}) collective-permute-start(bf16[3,80,512]{2,1,0:T(8,128)(2,1)S(1)} %slice_bitcast_fusion.2), channel_id=1, source_target_pairs={{0,6},{1,7},{2,0},{3,1},{4,2},{5,3},{6,4},{7,5},{8,14},{9,15},{10,... | collective-permute-start | bytes 737288 | tf_op jit(solution)/shard_map/ppermute | solution.py:306
  106.6 6.8 %collective-permute-done.16.rm_ref = bf16[2,3,80,512]{3,2,1,0:T(8,128)(2,1)S(1)} collective-permute-done((bf16[2,3,80,512]{3,2,1,0:T(8,128)(2,1)S(1)}, bf16[2,3,80,512]{3,2,1,0:T(8,128)(2,1)S(1)}, u32[]{:S(2)}, u32[]{:S(2)}) %collective-permute-start.16) | collective-permute-done | bytes 491552 | tf_op jit(solution)/shard_map/ppermute | solution.py:306
  114.0 3.3 %collective-permute-start.19 = (bf16[3,80,512]{2,1,0:T(8,128)(2,1)S(1)}, bf16[3,80,512]{2,1,0:T(8,128)(2,1)S(1)}, u32[]{:S(2)}, u32[]{:S(2)}) collective-permute-start(bf16[3,80,512]{2,1,0:T(8,128)(2,1)S(1)} %get-tuple-element.51), channel_id=1, source_target_pairs={{0,6},{1,7},{2,0},{3,1},{4,2},{5,3},{6,4},{7,5},{8,14},{9,15},{10,... | collective-permute-start | bytes 737288 | tf_op jit(solution)/shard_map/ppermute | solution.py:306
  117.3 3.8 %collective-permute-done.6.refs_1_ = bf16[2,3,80,512]{3,2,1,0:T(8,128)(2,1)S(1)} collective-permute-done((bf16[2,3,80,512]{3,2,1,0:T(8,128)(2,1)S(1)}, bf16[2,3,80,512]{3,2,1,0:T(8,128)(2,1)S(1)}, u32[]{:S(2)}, u32[]{:S(2)}) %collective-permute-start.6) | collective-permute-done | bytes 491552 | tf_op jit(solution)/shard_map/ppermute | solution.py:306
  121.4 5.1 %collective-permute-done.18.sp_ref = bf16[3,80,512]{2,1,0:T(8,128)(2,1)S(1)} collective-permute-done((bf16[3,80,512]{2,1,0:T(8,128)(2,1)S(1)}, bf16[3,80,512]{2,1,0:T(8,128)(2,1)S(1)}, u32[]{:S(2)}, u32[]{:S(2)}) %collective-permute-start.18) | collective-permute-done | bytes 245792 | tf_op jit(solution)/shard_map/ppermute | solution.py:306
  127.6 3.0 %collective-permute-done.8.refs_3_ = bf16[3,80,512]{2,1,0:T(8,128)(2,1)S(1)} collective-permute-done((bf16[3,80,512]{2,1,0:T(8,128)(2,1)S(1)}, bf16[3,80,512]{2,1,0:T(8,128)(2,1)S(1)}, u32[]{:S(2)}, u32[]{:S(2)}) %collective-permute-start.8) | collective-permute-done | bytes 245792 | tf_op jit(solution)/shard_map/ppermute | solution.py:306
  130.6 1.5 collective-permute-done.13.refs_8_
  132.1 5.9 %grad_rows.2 = (bf16[640,896]{1,0:T(8,128)(2,1)}, bf16[3,640,1024]{2,1,0:T(8,128)(2,1)}) custom-call(s32[2]{0:T(128)S(1)} %pad_add_fusion.refs_0_.place, bf16[2,3,80,512]{3,2,1,0:T(8,128)(2,1)S(1)} %swiglu.2.refs_0_, bf16[2,3,80,512]{3,2,1,0:T(8,128)(2,1)S(1)} %collective-permute-done.6.refs_1_, bf16[2,3,80,512]{3,2,1,0:T(8,128)(2,1)S(1)} %collective-permute-done.7.refs_2_, ...), custom_call_target="tpu_custom_call" | custom-call | flops 1 | bytes 1 | tf_op jit(solution)/shard_map/grad_rows/pallas_call | solution.py:432
  138.0 4.6 %all-to-all-start.1 = ((bf16[16,40,896]{2,1,0:T(8,128)(2,1)}), bf16[16,40,896]{2,1,0:T(8,128)(2,1)S(1)}, u32[]{:S(2)}, u32[]{:S(2)}) async-start(bf16[16,40,896]{2,1,0:T(8,128)(2,1)} %bitcast.26), calls=%async_computation.1 | async-start | bytes 2293760 | tf_op jit(solution)/shard_map/all_to_all | solution.py:541
  142.8 1.8 collective-permute-start.23
  145.6 5.6 %collective-permute-done.23.refs_4_ = bf16[3,80,512]{2,1,0:T(8,128)(2,1)S(1)} collective-permute-done((bf16[3,80,512]{2,1,0:T(8,128)(2,1)S(1)}, bf16[3,80,512]{2,1,0:T(8,128)(2,1)S(1)}, u32[]{:S(2)}, u32[]{:S(2)}) %collective-permute-start.23) | collective-permute-done | bytes 245792 | tf_op jit(solution)/shard_map/ppermute | solution.py:306
  151.2 3.9 %collective-permute-done.22.refs_3_ = bf16[3,80,512]{2,1,0:T(8,128)(2,1)S(1)} collective-permute-done((bf16[3,80,512]{2,1,0:T(8,128)(2,1)S(1)}, bf16[3,80,512]{2,1,0:T(8,128)(2,1)S(1)}, u32[]{:S(2)}, u32[]{:S(2)}) %collective-permute-start.22) | collective-permute-done | bytes 245792 | tf_op jit(solution)/shard_map/ppermute | solution.py:306
  155.2 1.5 collective-permute-done.27.refs_8_
  156.6 5.9 %grad_rows.3 = (bf16[640,896]{1,0:T(8,128)(2,1)}, bf16[3,640,1024]{2,1,0:T(8,128)(2,1)}) custom-call(s32[2]{0:T(128)S(1)} %pad_add_fusion.refs_0_.place, bf16[2,3,80,512]{3,2,1,0:T(8,128)(2,1)S(1)} %swiglu.3.refs_0_, bf16[2,3,80,512]{3,2,1,0:T(8,128)(2,1)S(1)} %collective-permute-done.20.refs_1_, ...), custom_call_target="tpu_custom_call" | custom-call | flops 1 | bytes 1 | tf_op jit(solution)/shard_map/grad_rows/pallas_call | solution.py:432
  162.6 6.5 %all-to-all-start.3 = ((bf16[16,40,896]{2,1,0:T(8,128)(2,1)}), bf16[16,40,896]{2,1,0:T(8,128)(2,1)S(1)}, u32[]{:S(2)}, u32[]{:S(2)}) async-start(bf16[16,40,896]{2,1,0:T(8,128)(2,1)} %bitcast.27), calls=%async_computation.3 | async-start | bytes 2293760 | tf_op jit(solution)/shard_map/all_to_all | solution.py:541
  169.2 7.7 %weight_grads.2 = (bf16[2,896,1024]{2,1,0:T(8,128)(2,1)}, bf16[2,896,1024]{2,1,0:T(8,128)(2,1)}, bf16[2,1024,896]{2,1,0:T(8,128)(2,1)}) custom-call(bf16[640,1792]{1,0:T(8,128)(2,1)} %get-tuple-element.54.x_ref.dy_ref, bf16[640,1792]{1,0:T(8,128)(2,1)} %get-tuple-element.54.x_ref.dy_ref, bf16[3,640,1024]{2,1,0:T(8,128)(2,1)} %get-tuple-element.55.h_ref), custom_call_target="tpu_custom_call" | custom-call | flops 1 | bytes 1 | tf_op jit(solution)/shard_map/weight_grads/pallas_call | solution.py:486
  176.9 7.7 %weight_grads.3 = (bf16[2,896,1024]{2,1,0:T(8,128)(2,1)}, bf16[2,896,1024]{2,1,0:T(8,128)(2,1)}, bf16[2,1024,896]{2,1,0:T(8,128)(2,1)}) custom-call(bf16[640,1792]{1,0:T(8,128)(2,1)} %bitcast.11.x_ref.dy_ref, bf16[640,1792]{1,0:T(8,128)(2,1)} %bitcast.11.x_ref.dy_ref, ...), custom_call_target="tpu_custom_call", output_to_operand_aliasing={{0}: (3, {}), {1}: (4, {}), {2}: (5, {})} | custom-call | flops 1 | bytes 1 | tf_op jit(solution)/shard_map/weight_grads/pallas_call | solution.py:486
  184.6 3.7 %all-to-all-done.3 = bf16[16,40,896]{2,1,0:T(8,128)(2,1)S(1)} async-done(((bf16[16,40,896]{2,1,0:T(8,128)(2,1)}), bf16[16,40,896]{2,1,0:T(8,128)(2,1)S(1)}, u32[]{:S(2)}, u32[]{:S(2)}) %all-to-all-start.3) | async-done | bytes 1146912 | tf_op jit(solution)/shard_map/all_to_all | solution.py:541
  188.3 1.3 combine.1
  (52 shorter events, 7.9 us)
Async XLA Ops:
  42.2 36.8 %all-to-all-start.2 = ((bf16[16,40,1792]{2,1,0:T(8,128)(2,1)}), bf16[16,40,1792]{2,1,0:T(8,128)(2,1)}, u32[]{:S(2)}, u32[]{:S(2)}) async-start(bf16[16,40,1792]{2,1,0:T(8,128)(2,1)} %bitcast.24), calls=%async_computation.2 | async-start | bytes 4587520 | tf_op jit(solution)/shard_map/all_to_all | solution.py:541
  54.1 2.2 %collective-permute-start = (bf16[8,1,80,512]{3,2,1,0:T(8,128)(2,1)S(1)}, bf16[8,1,80,512]{3,2,1,0:T(8,128)(2,1)S(1)}, u32[]{:S(2)}, u32[]{:S(2)}) collective-permute-start(bf16[8,1,80,512]{3,2,1,0:T(8,128)(2,1)S(1)} %get-tuple-element.36), channel_id=1, source_target_pairs={{0,1},{1,0},{2,3},{3,2},{4,5},{5,4},{6,7},{7,6},{8,9},{9,8},{10,11... | collective-permute-start | bytes 1966088 | tf_op jit(solution)/shard_map/ppermute | solution.py:306
  54.2 3.0 %collective-permute-start.1 = (bf16[8,1,80,512]{3,2,1,0:T(8,128)(2,1)S(1)}, bf16[8,1,80,512]{3,2,1,0:T(8,128)(2,1)S(1)}, u32[]{:S(2)}, u32[]{:S(2)}) collective-permute-start(bf16[8,1,80,512]{3,2,1,0:T(8,128)(2,1)S(1)} %get-tuple-element.37), channel_id=1, source_target_pairs={{0,1},{1,0},{2,3},{3,2},{4,5},{5,4},{6,7},{7,6},{8,9},{9,8},{10,11... | collective-permute-start | bytes 1966088 | tf_op jit(solution)/shard_map/ppermute | solution.py:306
  54.7 3.5 %collective-permute-start.2 = (bf16[8,1,80,512]{3,2,1,0:T(8,128)(2,1)S(1)}, bf16[8,1,80,512]{3,2,1,0:T(8,128)(2,1)S(1)}, u32[]{:S(2)}, u32[]{:S(2)}) collective-permute-start(bf16[8,1,80,512]{3,2,1,0:T(8,128)(2,1)S(1)} %get-tuple-element.38), channel_id=1, source_target_pairs={{0,1},{1,0},{2,3},{3,2},{4,5},{5,4},{6,7},{7,6},{8,9},{9,8},{10,11... | collective-permute-start | bytes 1966088 | tf_op jit(solution)/shard_map/ppermute | solution.py:306
  59.3 27.4 %collective-permute-start.3 = (bf16[2,3,80,512]{3,2,1,0:T(8,128)(2,1)}, bf16[2,3,80,512]{3,2,1,0:T(8,128)(2,1)S(1)}, u32[]{:S(2)}, u32[]{:S(2)}) collective-permute-start(bf16[2,3,80,512]{3,2,1,0:T(8,128)(2,1)} %get-tuple-element.40), channel_id=1, source_target_pairs={{0,2},{1,3},{2,4},{3,5},{4,6},{5,7},{6,0},{7,1},{8,10},{9,11},{10,... | collective-permute-start | bytes 1474568 | tf_op jit(solution)/shard_map/ppermute | solution.py:306
  61.2 25.4 %collective-permute-start.4 = (bf16[2,3,80,512]{3,2,1,0:T(8,128)(2,1)S(1)}, bf16[2,3,80,512]{3,2,1,0:T(8,128)(2,1)S(1)}, u32[]{:S(2)}, u32[]{:S(2)}) collective-permute-start(bf16[2,3,80,512]{3,2,1,0:T(8,128)(2,1)S(1)} %get-tuple-element.41), channel_id=1, source_target_pairs={{0,6},{1,7},{2,0},{3,1},{4,2},{5,3},{6,4},{7,5},{8,14},{9,15},{10,... | collective-permute-start | bytes 1474568 | tf_op jit(solution)/shard_map/ppermute | solution.py:306
  63.4 23.4 %collective-permute-start.5 = (bf16[2,3,80,512]{3,2,1,0:T(8,128)(2,1)S(1)}, bf16[2,3,80,512]{3,2,1,0:T(8,128)(2,1)S(1)}, u32[]{:S(2)}, u32[]{:S(2)}) collective-permute-start(bf16[2,3,80,512]{3,2,1,0:T(8,128)(2,1)S(1)} %get-tuple-element.42), channel_id=1, source_target_pairs={{0,4},{1,5},{2,6},{3,7},{4,0},{5,1},{6,2},{7,3},{8,12},{9,13},{10,... | collective-permute-start | bytes 1474568 | tf_op jit(solution)/shard_map/ppermute | solution.py:306
  86.8 4.5 %collective-permute-start.15 = (bf16[8,3,80,512]{3,2,1,0:T(8,128)(2,1)S(1)}, bf16[8,3,80,512]{3,2,1,0:T(8,128)(2,1)S(1)}, u32[]{:S(2)}, u32[]{:S(2)}) collective-permute-start(bf16[8,3,80,512]{3,2,1,0:T(8,128)(2,1)S(1)} %tie.1), channel_id=1, source_target_pairs={{0,1},{1,0},{2,3},{3,2},{4,5},{5,4},{6,7},{7,6},{8,9},{9,8},{10,11... | collective-permute-start | bytes 5898248 | tf_op jit(solution)/shard_map/ppermute | solution.py:306
  87.2 15.6 %collective-permute-start.7 = (bf16[2,3,80,512]{3,2,1,0:T(8,128)(2,1)S(1)}, bf16[2,3,80,512]{3,2,1,0:T(8,128)(2,1)S(1)}, u32[]{:S(2)}, u32[]{:S(2)}) collective-permute-start(bf16[2,3,80,512]{3,2,1,0:T(8,128)(2,1)S(1)} %swiglu.2.refs_0_), channel_id=1, source_target_pairs={{0,6},{1,7},{2,0},{3,1},{4,2},{5,3},{6,4},{7,5},{8,14},{9,15},{10,... | collective-permute-start | bytes 1474568 | tf_op jit(solution)/shard_map/ppermute | solution.py:306
  91.8 21.6 %collective-permute-start.16 = (bf16[2,3,80,512]{3,2,1,0:T(8,128)(2,1)S(1)}, bf16[2,3,80,512]{3,2,1,0:T(8,128)(2,1)S(1)}, u32[]{:S(2)}, u32[]{:S(2)}) collective-permute-start(bf16[2,3,80,512]{3,2,1,0:T(8,128)(2,1)S(1)} %get-tuple-element.48), channel_id=1, source_target_pairs={{0,6},{1,7},{2,0},{3,1},{4,2},{5,3},{6,4},{7,5},{8,14},{9,15},{10,... | collective-permute-start | bytes 1474568 | tf_op jit(solution)/shard_map/ppermute | solution.py:306
  95.3 18.1 %collective-permute-start.17 = (bf16[2,3,80,512]{3,2,1,0:T(8,128)(2,1)S(1)}, bf16[2,3,80,512]{3,2,1,0:T(8,128)(2,1)S(1)}, u32[]{:S(2)}, u32[]{:S(2)}) collective-permute-start(bf16[2,3,80,512]{3,2,1,0:T(8,128)(2,1)S(1)} %get-tuple-element.49), channel_id=1, source_target_pairs={{0,2},{1,3},{2,4},{3,5},{4,6},{5,7},{6,0},{7,1},{8,10},{9,11},{10,... | collective-permute-start | bytes 1474568 | tf_op jit(solution)/shard_map/ppermute | solution.py:306
  95.3 25.8 %collective-permute-start.6 = (bf16[2,3,80,512]{3,2,1,0:T(8,128)(2,1)S(1)}, bf16[2,3,80,512]{3,2,1,0:T(8,128)(2,1)S(1)}, u32[]{:S(2)}, u32[]{:S(2)}) collective-permute-start(bf16[2,3,80,512]{3,2,1,0:T(8,128)(2,1)S(1)} %swiglu.2.refs_0_), channel_id=1, source_target_pairs={{0,2},{1,3},{2,4},{3,5},{4,6},{5,7},{6,0},{7,1},{8,10},{9,11},{10,... | collective-permute-start | bytes 1474568 | tf_op jit(solution)/shard_map/ppermute | solution.py:306
  95.4 31.9 %collective-permute-start.10 = (bf16[2,3,80,512]{3,2,1,0:T(8,128)(2,1)S(1)}, bf16[2,3,80,512]{3,2,1,0:T(8,128)(2,1)S(1)}, u32[]{:S(2)}, u32[]{:S(2)}) collective-permute-start(bf16[2,3,80,512]{3,2,1,0:T(8,128)(2,1)S(1)} %swiglu.2.refs_0_), channel_id=1, source_target_pairs={{0,1},{1,0},{2,3},{3,2},{4,5},{5,4},{6,7},{7,6},{8,9},{9,8},{10,11... | collective-permute-start | bytes 1474568 | tf_op jit(solution)/shard_map/ppermute | solution.py:306
  102.9 18.4 %collective-permute-start.9 = (bf16[3,80,512]{2,1,0:T(8,128)(2,1)S(1)}, bf16[3,80,512]{2,1,0:T(8,128)(2,1)S(1)}, u32[]{:S(2)}, u32[]{:S(2)}) collective-permute-start(bf16[3,80,512]{2,1,0:T(8,128)(2,1)S(1)} %slice_bitcast_fusion.2), channel_id=1, source_target_pairs={{0,6},{1,7},{2,0},{3,1},{4,2},{5,3},{6,4},{7,5},{8,14},{9,15},{10,... | collective-permute-start | bytes 737288 | tf_op jit(solution)/shard_map/ppermute | solution.py:306
  113.5 12.9 %collective-permute-start.18 = (bf16[3,80,512]{2,1,0:T(8,128)(2,1)S(1)}, bf16[3,80,512]{2,1,0:T(8,128)(2,1)S(1)}, u32[]{:S(2)}, u32[]{:S(2)}) collective-permute-start(bf16[3,80,512]{2,1,0:T(8,128)(2,1)S(1)} %get-tuple-element.50), channel_id=1, source_target_pairs={{0,2},{1,3},{2,4},{3,5},{4,6},{5,7},{6,0},{7,1},{8,10},{9,11},{10,... | collective-permute-start | bytes 737288 | tf_op jit(solution)/shard_map/ppermute | solution.py:306
  114.0 12.4 %collective-permute-start.19 = (bf16[3,80,512]{2,1,0:T(8,128)(2,1)S(1)}, bf16[3,80,512]{2,1,0:T(8,128)(2,1)S(1)}, u32[]{:S(2)}, u32[]{:S(2)}) collective-permute-start(bf16[3,80,512]{2,1,0:T(8,128)(2,1)S(1)} %get-tuple-element.51), channel_id=1, source_target_pairs={{0,6},{1,7},{2,0},{3,1},{4,2},{5,3},{6,4},{7,5},{8,14},{9,15},{10,... | collective-permute-start | bytes 737288 | tf_op jit(solution)/shard_map/ppermute | solution.py:306
  121.2 9.4 %collective-permute-start.8 = (bf16[3,80,512]{2,1,0:T(8,128)(2,1)S(1)}, bf16[3,80,512]{2,1,0:T(8,128)(2,1)S(1)}, u32[]{:S(2)}, u32[]{:S(2)}) collective-permute-start(bf16[3,80,512]{2,1,0:T(8,128)(2,1)S(1)} %slice_bitcast_fusion.3), channel_id=1, source_target_pairs={{0,2},{1,3},{2,4},{3,5},{4,6},{5,7},{6,0},{7,1},{8,10},{9,11},{10,... | collective-permute-start | bytes 737288 | tf_op jit(solution)/shard_map/ppermute | solution.py:306
  121.3 9.3 %collective-permute-start.12 = (bf16[2,3,80,512]{3,2,1,0:T(8,128)(2,1)S(1)}, bf16[2,3,80,512]{3,2,1,0:T(8,128)(2,1)S(1)}, u32[]{:S(2)}, u32[]{:S(2)}) collective-permute-start(bf16[2,3,80,512]{3,2,1,0:T(8,128)(2,1)S(1)} %collective-permute-done.7.refs_2_), channel_id=1, source_target_pairs={{0,1},{1,0},{2,3},{3,2},{4,5},{5,4},{6,7},{7,6},{8,9},{9,8},{10,11... | collective-permute-start | bytes 1474568 | tf_op jit(solution)/shard_map/ppermute | solution.py:306
  126.4 5.7 %collective-permute-start.11 = (bf16[2,3,80,512]{3,2,1,0:T(8,128)(2,1)S(1)}, bf16[2,3,80,512]{3,2,1,0:T(8,128)(2,1)S(1)}, u32[]{:S(2)}, u32[]{:S(2)}) collective-permute-start(bf16[2,3,80,512]{3,2,1,0:T(8,128)(2,1)S(1)} %collective-permute-done.6.refs_1_), channel_id=1, source_target_pairs={{0,1},{1,0},{2,3},{3,2},{4,5},{5,4},{6,7},{7,6},{8,9},{9,8},{10,11... | collective-permute-start | bytes 1474568 | tf_op jit(solution)/shard_map/ppermute | solution.py:306
  126.4 4.1 %collective-permute-start.14 = (bf16[3,80,512]{2,1,0:T(8,128)(2,1)S(1)}, bf16[3,80,512]{2,1,0:T(8,128)(2,1)S(1)}, u32[]{:S(2)}, u32[]{:S(2)}) collective-permute-start(bf16[3,80,512]{2,1,0:T(8,128)(2,1)S(1)} %collective-permute-done.9.refs_4_), channel_id=1, source_target_pairs={{0,1},{1,0},{2,3},{3,2},{4,5},{5,4},{6,7},{7,6},{8,9},{9,8},{10,11... | collective-permute-start | bytes 737288 | tf_op jit(solution)/shard_map/ppermute | solution.py:306
  127.3 15.5 %collective-permute-start.21 = (bf16[2,3,80,512]{3,2,1,0:T(8,128)(2,1)S(1)}, bf16[2,3,80,512]{3,2,1,0:T(8,128)(2,1)S(1)}, u32[]{:S(2)}, u32[]{:S(2)}) collective-permute-start(bf16[2,3,80,512]{3,2,1,0:T(8,128)(2,1)S(1)} %swiglu.3.refs_0_), channel_id=1, source_target_pairs={{0,6},{1,7},{2,0},{3,1},{4,2},{5,3},{6,4},{7,5},{8,14},{9,15},{10,... | collective-permute-start | bytes 1474568 | tf_op jit(solution)/shard_map/ppermute | solution.py:306
  130.6 1.5 collective-permute-start.13
  130.6 14.8 %collective-permute-start.20 = (bf16[2,3,80,512]{3,2,1,0:T(8,128)(2,1)S(1)}, bf16[2,3,80,512]{3,2,1,0:T(8,128)(2,1)S(1)}, u32[]{:S(2)}, u32[]{:S(2)}) collective-permute-start(bf16[2,3,80,512]{3,2,1,0:T(8,128)(2,1)S(1)} %swiglu.3.refs_0_), channel_id=1, source_target_pairs={{0,2},{1,3},{2,4},{3,5},{4,6},{5,7},{6,0},{7,1},{8,10},{9,11},{10,... | collective-permute-start | bytes 1474568 | tf_op jit(solution)/shard_map/ppermute | solution.py:306
  138.0 24.6 %all-to-all-start.1 = ((bf16[16,40,896]{2,1,0:T(8,128)(2,1)}), bf16[16,40,896]{2,1,0:T(8,128)(2,1)S(1)}, u32[]{:S(2)}, u32[]{:S(2)}) async-start(bf16[16,40,896]{2,1,0:T(8,128)(2,1)} %bitcast.26), calls=%async_computation.1 | async-start | bytes 2293760 | tf_op jit(solution)/shard_map/all_to_all | solution.py:541
  142.7 12.4 %collective-permute-start.24 = (bf16[2,3,80,512]{3,2,1,0:T(8,128)(2,1)S(1)}, bf16[2,3,80,512]{3,2,1,0:T(8,128)(2,1)S(1)}, u32[]{:S(2)}, u32[]{:S(2)}) collective-permute-start(bf16[2,3,80,512]{3,2,1,0:T(8,128)(2,1)S(1)} %swiglu.3.refs_0_), channel_id=1, source_target_pairs={{0,1},{1,0},{2,3},{3,2},{4,5},{5,4},{6,7},{7,6},{8,9},{9,8},{10,11... | collective-permute-start | bytes 1474568 | tf_op jit(solution)/shard_map/ppermute | solution.py:306
  142.8 8.4 %collective-permute-start.23 = (bf16[3,80,512]{2,1,0:T(8,128)(2,1)S(1)}, bf16[3,80,512]{2,1,0:T(8,128)(2,1)S(1)}, u32[]{:S(2)}, u32[]{:S(2)}) collective-permute-start(bf16[3,80,512]{2,1,0:T(8,128)(2,1)S(1)} %slice_bitcast_fusion), channel_id=1, source_target_pairs={{0,6},{1,7},{2,0},{3,1},{4,2},{5,3},{6,4},{7,5},{8,14},{9,15},{10,... | collective-permute-start | bytes 737288 | tf_op jit(solution)/shard_map/ppermute | solution.py:306
  144.6 10.5 %collective-permute-start.26 = (bf16[2,3,80,512]{3,2,1,0:T(8,128)(2,1)S(1)}, bf16[2,3,80,512]{3,2,1,0:T(8,128)(2,1)S(1)}, u32[]{:S(2)}, u32[]{:S(2)}) collective-permute-start(bf16[2,3,80,512]{3,2,1,0:T(8,128)(2,1)S(1)} %collective-permute-done.21.refs_2_), channel_id=1, source_target_pairs={{0,1},{1,0},{2,3},{3,2},{4,5},{5,4},{6,7},{7,6},{8,9},{9,8},{10,11... | collective-permute-start | bytes 1474568 | tf_op jit(solution)/shard_map/ppermute | solution.py:306
  145.5 9.7 %collective-permute-start.25 = (bf16[2,3,80,512]{3,2,1,0:T(8,128)(2,1)S(1)}, bf16[2,3,80,512]{3,2,1,0:T(8,128)(2,1)S(1)}, u32[]{:S(2)}, u32[]{:S(2)}) collective-permute-start(bf16[2,3,80,512]{3,2,1,0:T(8,128)(2,1)S(1)} %collective-permute-done.20.refs_1_), channel_id=1, source_target_pairs={{0,1},{1,0},{2,3},{3,2},{4,5},{5,4},{6,7},{7,6},{8,9},{9,8},{10,11... | collective-permute-start | bytes 1474568 | tf_op jit(solution)/shard_map/ppermute | solution.py:306
  145.5 9.6 %collective-permute-start.22 = (bf16[3,80,512]{2,1,0:T(8,128)(2,1)S(1)}, bf16[3,80,512]{2,1,0:T(8,128)(2,1)S(1)}, u32[]{:S(2)}, u32[]{:S(2)}) collective-permute-start(bf16[3,80,512]{2,1,0:T(8,128)(2,1)S(1)} %slice_bitcast_fusion.1), channel_id=1, source_target_pairs={{0,2},{1,3},{2,4},{3,5},{4,6},{5,7},{6,0},{7,1},{8,10},{9,11},{10,... | collective-permute-start | bytes 737288 | tf_op jit(solution)/shard_map/ppermute | solution.py:306
  151.2 3.9 %collective-permute-start.28 = (bf16[3,80,512]{2,1,0:T(8,128)(2,1)S(1)}, bf16[3,80,512]{2,1,0:T(8,128)(2,1)S(1)}, u32[]{:S(2)}, u32[]{:S(2)}) collective-permute-start(bf16[3,80,512]{2,1,0:T(8,128)(2,1)S(1)} %collective-permute-done.23.refs_4_), channel_id=1, source_target_pairs={{0,1},{1,0},{2,3},{3,2},{4,5},{5,4},{6,7},{7,6},{8,9},{9,8},{10,11... | collective-permute-start | bytes 737288 | tf_op jit(solution)/shard_map/ppermute | solution.py:306
  155.1 1.5 collective-permute-start.27
  162.6 25.7 %all-to-all-start.3 = ((bf16[16,40,896]{2,1,0:T(8,128)(2,1)}), bf16[16,40,896]{2,1,0:T(8,128)(2,1)S(1)}, u32[]{:S(2)}, u32[]{:S(2)}) async-start(bf16[16,40,896]{2,1,0:T(8,128)(2,1)} %bitcast.27), calls=%async_computation.3 | async-start | bytes 2293760 | tf_op jit(solution)/shard_map/all_to_all | solution.py:541
